TPU v7x, 32 devices: a whole 2x2x4 slice. The times are simulated.
32 devices in a mesh: expert: 8 (over y, x, core), dp: 4 (over z).
Axes of the slice: x: 2, y: 2, z: 4, core: 2. Of those that a mesh axis runs over, the one named last changes fastest.
Arguments:
- dy_values: bfloat16 [2048, 4096], P('expert', 'dp'), may hold values from -6 to 6
- dy_scales: bfloat16 [2048, 32], P('expert', 'dp'), may hold values from 0.25 to 4
- expert_ids: int32 [2048, 1], P('expert'), may hold values from 0 to 7; in each aligned block of 256 rows (0 to 255, 256 to 511, ...) at most 64 rows name the same one
- saved_pre: bfloat16 [4096, 2048], P('expert'), may hold values from -6 to 6
- w_gate: bfloat16 [8, 4096, 1024], P('expert', 'dp'), may hold values from -0.1875 to 0.1875
- w_up: bfloat16 [8, 4096, 1024], P('expert', 'dp'), may hold values from -0.1875 to 0.1875
- w_down: bfloat16 [8, 4096, 1024], P('expert', 'dp'), may hold values from -0.09375 to 0.09375
Outputs:
- grad_input: bfloat16 [2048, 4096], P('expert', 'dp')
- grad_down: float32 [8, 4096, 1024], P('expert', 'dp')
Inputs may be any that keep to these rules, and one draw needn't show every extreme that they name: `expert_ids`: among the rows of one index of expert (aligned blocks of 256 rows) no expert occurs more than 64 times.
All inputs are finite; a program needn't handle non-finite values.
Results may differ from a plain program's by a relative error of at most 0.0057.
Values may be sent and summed in bfloat16 or wider, within the bound.
No kernel may reach another device: no remote copies, remote signals or barrier semaphores. Data moves between devices by JAX's collectives and lax.ppermute only.
A program may use at most 64 MiB of HBM per device.

v0:
```python
import jax
import jax.numpy as jnp
from jax import lax
from jax.sharding import PartitionSpec as P


def dequantize(values, scales):
    row_count, feature_count = values.shape
    block_count = scales.shape[1]
    blocked = values.astype(jnp.float32).reshape(
        row_count, block_count, feature_count // block_count
    )
    blocked = blocked * scales.astype(jnp.float32)[:, :, None]
    return blocked.reshape(row_count, feature_count).astype(jnp.bfloat16)


def swiglu_parts(hidden_grad, gate_pre, up_pre):
    sigmoid_gate = jax.nn.sigmoid(gate_pre)
    d_gate = hidden_grad * up_pre * sigmoid_gate * (1.0 + gate_pre * (1.0 - sigmoid_gate))
    d_up = hidden_grad * jax.nn.silu(gate_pre)
    return (d_gate.astype(jnp.bfloat16), d_up.astype(jnp.bfloat16))


def per_device(dy_values, dy_scales, expert_ids, saved_pre, w_gate, w_up, w_down):
    groups = lax.axis_size("expert")
    slot_count = saved_pre.shape[0]
    per_expert = slot_count // groups
    hidden_width = w_down.shape[2]
    feature_count = dy_values.shape[1]
    route_ids = expert_ids[:, 0]
    onehot = (route_ids[:, None] == jnp.arange(groups, dtype=jnp.int32)[None, :]).astype(jnp.int32)
    earlier = jnp.cumsum(onehot, axis=0) - onehot
    position = route_ids * per_expert + jnp.sum(earlier * onehot, axis=1)
    out_values = jnp.zeros((slot_count, feature_count), jnp.bfloat16).at[position].set(dy_values)
    out_scales = (
        jnp.zeros((slot_count, dy_scales.shape[1]), jnp.bfloat16).at[position].set(dy_scales)
    )
    got_values, got_scales = (
        lax.all_to_all(out_values, "expert", split_axis=0, concat_axis=0, tiled=True),
        lax.all_to_all(out_scales, "expert", split_axis=0, concat_axis=0, tiled=True),
    )
    received = dequantize(got_values, got_scales)
    gate_full = saved_pre[:, :hidden_width].astype(jnp.float32)
    up_full = saved_pre[:, hidden_width:].astype(jnp.float32)
    hidden = (jax.nn.silu(gate_full) * up_full).astype(jnp.bfloat16)
    partial_grad = jnp.dot(received, w_down[0], preferred_element_type=jnp.float32)
    hidden_grad = lax.psum(partial_grad, "dp")
    d_gate, d_up = swiglu_parts(hidden_grad, gate_full, up_full)
    pre_grad = jnp.concatenate([d_gate, d_up], axis=1)
    paired = jnp.concatenate([w_gate[0], w_up[0]], axis=1)
    slot_grad = lax.dot_general(
        pre_grad, paired, (((1,), (1,)), ((), ())), preferred_element_type=jnp.float32
    ).astype(jnp.bfloat16)
    returned = lax.all_to_all(slot_grad, "expert", split_axis=0, concat_axis=0, tiled=True)
    grad_input = returned[position]
    grad_down = lax.dot_general(
        received, hidden, (((0,), (0,)), ((), ())), preferred_element_type=jnp.float32
    )
    return (grad_input, grad_down[None])


def solution(mesh):
    return jax.shard_map(
        per_device,
        mesh=mesh,
        in_specs=(
            P("expert", "dp"),
            P("expert", "dp"),
            P("expert", None),
            P("expert", None),
            P("expert", "dp", None),
            P("expert", "dp", None),
            P("expert", "dp", None),
        ),
        out_specs=(P("expert", "dp"), P("expert", "dp", None)),
        check_vma=False,
    )
```

profile of v0, /device:TPU:0, one launch (start us, length us, event | category | flops | bytes accessed | tf_op | source)
XLA Modules:
  0.0 166.4 jit_solution(2454329161560276853)
XLA Ops:
  7.2 0.0 copy-start
  7.2 0.8 fusion.34
  8.0 0.6 reduce-window.6
  8.6 0.2 slice_reduce_fusion
  8.8 0.8 fusion.33
  9.6 0.7 compare_select_fusion
  10.3 0.8 copy.12
  11.1 1.2 scatter_custom_fusion.1
  12.3 0.1 copy.13
  12.4 0.7 reshape.90
  13.1 5.2 %all-to-all-start.1 = ((bf16[8,2,256]{2,1,0:T(2,128)(2,1)}), bf16[8,2,256]{2,1,0:T(2,128)(2,1)S(1)}, u32[]{:S(2)}, u32[]{:S(2)}) async-start(bf16[8,2,256]{2,1,0:T(2,128)(2,1)} %reshape.90), calls=%async_computation.1 | async-start | bytes 16384 | tf_op jit(solution)/shard_map/all_to_all | solution.py:40
  18.3 3.1 %scatter_custom_fusion = bf16[512,1024]{1,0:T(8,128)(2,1)} fusion(s32[256]{0:T(256)S(1)} %bitcast.61, bf16[256,1024]{1,0:T(8,128)(2,1)} %param.7, bf16[]{:T(256)} %constant.5.clone.1), kind=kCustom, calls=%fused_computation.35 | custom fusion | bytes 1049088 | tf_op jit(solution)/shard_map/scatter | solution.py:34
  21.4 1.6 all-to-all-done.1
  23.0 3.6 %all-to-all-start = ((bf16[8,64,1024]{2,1,0:T(8,128)(2,1)}), bf16[8,64,1024]{2,1,0:T(8,128)(2,1)S(1)}, u32[]{:S(2)}, u32[]{:S(2)}) async-start(bf16[8,64,1024]{2,1,0:T(8,128)(2,1)} %bitcast.50), calls=%async_computation | async-start | bytes 2097152 | tf_op jit(solution)/shard_map/all_to_all | solution.py:39
  26.6 0.0 all-reduce.2.cloned.1.call-start
  26.6 0.1 reshape.91
  26.7 0.1 copy.16
  26.8 15.1 %all-to-all-done = bf16[8,64,1024]{2,1,0:T(8,128)(2,1)S(1)} async-done(((bf16[8,64,1024]{2,1,0:T(8,128)(2,1)}), bf16[8,64,1024]{2,1,0:T(8,128)(2,1)S(1)}, u32[]{:S(2)}, u32[]{:S(2)}) %all-to-all-start) | async-done | bytes 1048608 | tf_op jit(solution)/shard_map/all_to_all | solution.py:39
  41.9 0.0 copy-start.1
  41.9 0.3 copy.18
  42.2 0.9 fusion.13
  43.0 0.0 copy-done.1
  43.0 0.0 copy-done
  43.1 2.6 %fusion.17 = f32[512,1024]{1,0:T(8,128)} fusion(bf16[1,1024,1024]{2,1,0:T(8,128)(2,1)S(1)} %copy-done, bf16[64,8,8,128]{3,2,1,0:T(8,128)(2,1)S(1)} %bitcast.54), kind=kOutput, calls=%fused_computation.28 | convolution fusion | flops 1073741824 | bytes 5242880 | tf_op jit(solution)/shard_map/dot_general | solution.py:46
  45.6 0.0 all-reduce.2.cloned.1.call-update
  45.7 86.1 %all-reduce.2.cloned.1.call-done = f32[512,1024]{1,0:T(8,128)} async-done(((f32[512,1024]{1,0:T(8,128)}), f32[512,1024]{1,0:T(8,128)}) %all-reduce.2.cloned.1.call-update) | async-done | bytes 2097168 | tf_op jit(solution)/shard_map/psum | solution.py:47
  131.7 0.0 copy-start.4
  131.7 0.0 copy-start.5
  131.7 3.4 %fusion.6 = (bf16[512,1024]{1,0:T(8,128)(2,1)S(1)}, bf16[512,1024]{1,0:T(8,128)(2,1)S(1)}) fusion(f32[512,1024]{1,0:T(8,128)} %all-reduce.2.cloned.1.call-done, bf16[512,2048]{1,0:T(8,128)(2,1)} %param.10), kind=kLoop, calls=%fused_computation.15 | loop fusion | flops 7864320 | bytes 6291456 | tf_op jit(solution)/shard_map/convert_element_type | solution.py:21
  135.1 0.0 copy-done.4
  135.1 0.1 copy-done.5
  135.2 3.4 %fusion.19 = bf16[512,1024]{1,0:T(8,128)(2,1)} fusion(bf16[1024,1024]{1,0:T(8,128)(2,1)S(1)} %bitcast.64, bf16[1024,1024]{1,0:T(8,128)(2,1)S(1)} %bitcast.65, bf16[512,1024]{1,0:T(8,128)(2,1)S(1)} %get-tuple-element.3, bf16[512,1024]{1,0:T(8,128)(2,1)S(1)} %get-tuple-element.2), kind=kOutput, calls=%fused_computation.31 | convolution fusion | flops 2160590848 | bytes 7340032 | tf_op jit(solution)/shard_map/dot_general | solution.py:51
  138.6 3.7 %all-to-all-start.2 = ((bf16[8,64,1024]{2,1,0:T(8,128)(2,1)}), bf16[8,64,1024]{2,1,0:T(8,128)(2,1)S(1)}, u32[]{:S(2)}, u32[]{:S(2)}) async-start(bf16[8,64,1024]{2,1,0:T(8,128)(2,1)} %bitcast.53), calls=%async_computation.2 | async-start | bytes 2097152 | tf_op jit(solution)/shard_map/all_to_all | solution.py:54
  142.2 0.0 copy-start.2
  142.3 0.6 mul.56
  142.9 0.6 copy-done.2
  143.5 0.0 copy-start.3
  143.5 0.7 fusion.12
  144.2 0.9 copy-done.3
  145.0 3.4 %convolution_bitcast_fusion = f32[1,1024,1024]{2,1,0:T(8,128)} fusion(bf16[512,1024]{1,0:T(8,128)(2,1)S(1)} %fusion.12, bf16[512,2048]{1,0:T(8,128)(2,1)S(1)} %copy-done.3), kind=kOutput, calls=%fused_computation.12 | convolution fusion | flops 1077936128 | bytes 7340032 | tf_op jit(solution)/shard_map/dot_general | solution.py:56
  148.5 9.2 %all-to-all-done.2 = bf16[8,64,1024]{2,1,0:T(8,128)(2,1)S(1)} async-done(((bf16[8,64,1024]{2,1,0:T(8,128)(2,1)}), bf16[8,64,1024]{2,1,0:T(8,128)(2,1)S(1)}, u32[]{:S(2)}, u32[]{:S(2)}) %all-to-all-start.2) | async-done | bytes 1048608 | tf_op jit(solution)/shard_map/all_to_all | solution.py:54
  157.6 2.0 %gather_fusion = bf16[256,1024]{1,0:T(8,128)(2,1)} fusion(bf16[512,1024]{1,0:T(8,128)(2,1)S(1)} %bitcast.47, s32[1024]{0:T(1024)S(1)} %pad_clamp_fusion), kind=kCustom, calls=%fused_computation | custom fusion | bytes 1049600 | tf_op jit(solution)/shard_map/gather | solution.py:55
  (3 shorter events, 0.0 us)
Async XLA Ops:
  7.2 35.9 %copy-start = (bf16[1,1024,1024]{2,1,0:T(8,128)(2,1)S(1)}, bf16[1,1024,1024]{2,1,0:T(8,128)(2,1)}, u32[]{:S(2)}) copy-start(bf16[1,1024,1024]{2,1,0:T(8,128)(2,1)} %param.13) | copy-start | bytes 6291460
  13.1 9.9 %all-to-all-start.1 = ((bf16[8,2,256]{2,1,0:T(2,128)(2,1)}), bf16[8,2,256]{2,1,0:T(2,128)(2,1)S(1)}, u32[]{:S(2)}, u32[]{:S(2)}) async-start(bf16[8,2,256]{2,1,0:T(2,128)(2,1)} %reshape.90), calls=%async_computation.1 | async-start | bytes 16384 | tf_op jit(solution)/shard_map/all_to_all | solution.py:40
  23.0 18.9 %all-to-all-start = ((bf16[8,64,1024]{2,1,0:T(8,128)(2,1)}), bf16[8,64,1024]{2,1,0:T(8,128)(2,1)S(1)}, u32[]{:S(2)}, u32[]{:S(2)}) async-start(bf16[8,64,1024]{2,1,0:T(8,128)(2,1)} %bitcast.50), calls=%async_computation | async-start | bytes 2097152 | tf_op jit(solution)/shard_map/all_to_all | solution.py:39
  26.6 105.2 %all-reduce.2.cloned.1.call-start = ((), (), s32[]{:S(2)}) async-start(), calls=%async_computation.3 | async-start | bytes 4194304 | tf_op jit(solution)/shard_map/psum | solution.py:47
  41.9 1.1 copy-start.1
  131.7 3.4 %copy-start.4 = (bf16[1,1024,1024]{2,1,0:T(8,128)(2,1)S(1)}, bf16[1,1024,1024]{2,1,0:T(8,128)(2,1)}, u32[]{:S(2)}) copy-start(bf16[1,1024,1024]{2,1,0:T(8,128)(2,1)} %param.12) | copy-start | bytes 6291460
  131.7 3.5 %copy-start.5 = (bf16[1,1024,1024]{2,1,0:T(8,128)(2,1)S(1)}, bf16[1,1024,1024]{2,1,0:T(8,128)(2,1)}, u32[]{:S(2)}) copy-start(bf16[1,1024,1024]{2,1,0:T(8,128)(2,1)} %param.11) | copy-start | bytes 6291460
  138.6 19.1 %all-to-all-start.2 = ((bf16[8,64,1024]{2,1,0:T(8,128)(2,1)}), bf16[8,64,1024]{2,1,0:T(8,128)(2,1)S(1)}, u32[]{:S(2)}, u32[]{:S(2)}) async-start(bf16[8,64,1024]{2,1,0:T(8,128)(2,1)} %bitcast.53), calls=%async_computation.2 | async-start | bytes 2097152 | tf_op jit(solution)/shard_map/all_to_all | solution.py:54
  142.2 1.2 copy-start.2
  143.5 1.6 copy-start.3
Sparse Core Ops, SparseCore 0:
  45.8 85.8 all-reduce.1
where the time goes:
time: 167 us; the launch traced here: 166 us
  waiting for transfers between devices  112 us (67%)
  between operations  14.1 us (8%)
  starting transfers between devices  12.4 us (7%)
  local copies, waits for them, and re-layouts  10.8 us (6%)
  matrix products  9.37 us (6%)
  other arithmetic  7.85 us (5%)
    psum x1, waiting for transfers between devices, per_device(): hidden_grad = lax.psum(partial_grad, 'dp')  86.1 us
    all_to_all x1, waiting for transfers between devices, per_device(): lax.all_to_all(out_values, 'expert', split_axis=0, concat_axis=0, tiled=T...  15.1 us
    all_to_all x1, waiting for transfers between devices, per_device(): lax.all_to_all(slot_grad, 'expert', split_axis=0, concat_axis=0, tiled=True)  9.17 us
    all_to_all x1, starting transfers between devices, per_device(): lax.all_to_all(out_scales, 'expert', split_axis=0, concat_axis=0, tiled=T...  5.17 us
    all_to_all x1, starting transfers between devices, per_device(): lax.all_to_all(slot_grad, 'expert', split_axis=0, concat_axis=0, tiled=True)  3.66 us
    all_to_all x1, starting transfers between devices, per_device(): lax.all_to_all(out_values, 'expert', split_axis=0, concat_axis=0, tiled=T...  3.56 us
    unnamed x16, local copies, waits for them, and re-layouts  3.44 us
    dot_general x1, matrix products, per_device(): lax.dot_general(received, hidden, (((0,), (0,)), ((), ())), preferred_ele...  3.43 us
  transfers between devices with their start and end apart: 4, of which 4 were waited for; matrix products, arithmetic and copies ran while one was open for 5% of the time, Pallas kernels for 0%

commit v1 on v0

v1 whole, which is shorter than its diff:
```python
import functools

import jax
import jax.numpy as jnp
from jax import lax
from jax.experimental import pallas as pl
from jax.experimental.pallas import tpu as pltpu
from jax.sharding import PartitionSpec as P

CHUNKS = ((0, 1), (6, 7), (3, 5), (2, 4))
EARLY, LATE = sum(CHUNKS[:-1], ()), CHUNKS[-1]
ORDER = (
    ("first", 0), ("prep", 0), ("add", 0), ("first", 1), ("turn", 0), ("add", 0), ("add", 1),
    ("first", 2), ("first", 3), ("second", 0), ("add", 2), ("add", 1), ("add", 3), ("down", 0),
    ("second", 1), ("add", 2), ("add", 3), ("second", 2), ("second", 3),
)
WEIGHT = 20
LATE_WEIGHT = 20
MIB = 1 << 20
BF16, F32 = jnp.bfloat16, jnp.float32
TRANSPOSED = (((1,), (1,)), ((), ()))
BY_ROWS = (((0,), (0,)), ((), ()))


VMEM, SMEM, HBM, ANY = (
    pl.BlockSpec(memory_space=space) for space in (pltpu.VMEM, pltpu.SMEM, pltpu.HBM, pl.ANY)
)


def call(
    body, name, operands, specs, outs, out_specs, work, vmem,
    scratch=(), after=(), passed=(), weight=WEIGHT,
):
    count, results = len(operands), len(outs)
    inputs = count + len(after) + len(passed)

    def run(*refs):
        kept = refs[:count] + refs[inputs : inputs + results]
        body(*kept, *refs[inputs + results + len(passed) :])

    return pl.pallas_call(
        run,
        name=name,
        out_shape=list(outs) + [jax.ShapeDtypeStruct(x.shape, x.dtype) for x in passed],
        in_specs=list(specs) + [ANY] * (len(after) + len(passed)),
        out_specs=list(out_specs) + [ANY] * len(passed),
        scratch_shapes=scratch,
        input_output_aliases={
            count + len(after) + i: results + i for i in range(len(passed))
        },
        compiler_params=pltpu.CompilerParams(vmem_limit_bytes=vmem * MIB),
        cost_estimate=pl.CostEstimate(
            flops=weight * work, bytes_accessed=weight * work // 300, transcendentals=0
        ),
    )(*operands, *after, *passed)


def in_hbm(array):
    return pltpu.with_memory_space_constraint(array, pltpu.HBM)


def swish_parts(pre, width):
    gate, up = pre[:, :width].astype(F32), pre[:, width:].astype(F32)
    sigmoid = jax.nn.sigmoid(gate)
    return gate, up, sigmoid


def tiles(size):
    step = 256 if size % 256 == 0 else size
    return [slice(i, i + step) for i in range(0, size, step)]


def arrays_of(blocks):
    found = []
    for array, _ in blocks:
        if not any(array is other for other in found):
            found.append(array)
    return found


def spots_of(blocks, arrays):
    return [(next(i for i, x in enumerate(arrays) if x is array), row) for array, row in blocks]


def rows_at(refs, spots, cap):
    return jnp.concatenate([refs[i][row : row + cap] for i, row in spots], axis=0)


def pack_body(
    groups, cap, info, scales, ids, values, place, even, odd, ids_in, rows_in, sems
):
    bring_rows = pltpu.make_async_copy(values, rows_in, sems.at[0])
    bring_ids = pltpu.make_async_copy(ids, ids_in, sems.at[1])
    bring_ids.start()
    bring_rows.start()
    rows, features = values.shape
    slots, lines = groups * cap, max(8, groups)
    count = scales.shape[0]
    owner = lax.broadcasted_iota(jnp.int32, (count, features), 1) // (features // count)
    spread = jnp.where(owner == lax.broadcasted_iota(jnp.int32, (count, features), 0), 1.0, 0.0)
    factor = lax.dot_general(
        scales[...].astype(BF16), spread.astype(BF16), BY_ROWS, preferred_element_type=F32
    )
    bring_ids.wait()
    route = ids_in[...]
    line = lax.broadcasted_iota(jnp.int32, (lines, rows), 0)
    onehot = jnp.where(line == route, 1.0, 0.0)
    sooner = lax.broadcasted_iota(jnp.int32, (rows, rows), 0)
    later = lax.broadcasted_iota(jnp.int32, (rows, rows), 1)
    before = jnp.where(sooner < later, 1.0, 0.0).astype(BF16)
    earlier = jnp.dot(onehot.astype(BF16), before, preferred_element_type=F32)
    rank = jnp.sum(earlier * onehot, axis=0, keepdims=True).astype(jnp.int32)
    position = (route ^ info[1]) * cap + rank
    slot = lax.broadcasted_iota(jnp.int32, (slots, rows), 0)
    chosen = jnp.where(slot == position, 1.0, 0.0).astype(BF16)
    place[...] = chosen
    bring_rows.wait()
    scaled = (rows_in[...].astype(F32) * factor).astype(BF16)
    for part in tiles(features):
        packed = jnp.dot(chosen, scaled[:, part], preferred_element_type=F32).astype(BF16)
        for k in range(groups):
            out = odd if k % 2 else even
            out[k // 2 * cap : (k // 2 + 1) * cap, part] = packed[k * cap : (k + 1) * cap]


def pack(info, ids, values, scales, groups, cap):
    rows, features = values.shape
    half = jax.ShapeDtypeStruct((groups // 2 * cap, features), BF16)
    return call(
        functools.partial(pack_body, groups, cap),
        "pack",
        (info, scales.T.astype(F32), in_hbm(ids.T), in_hbm(values)),
        (SMEM, VMEM, HBM, HBM),
        [jax.ShapeDtypeStruct((groups * cap, rows), BF16), half, half],
        [VMEM] * 3,
        2 * rows * groups * cap * features,
        24,
        [
            pltpu.VMEM((1, rows), jnp.int32),
            pltpu.VMEM((rows, features), BF16),
            pltpu.SemaphoreType.DMA((2,)),
        ],
    )


def first_body(count, spots, bundles, cap, info, weight, *refs):
    arrays, send, keep = refs[:count], refs[count], refs[count + 1]
    for bundle, out in zip(bundles, refs[count + 2 :]):
        out[...] = rows_at(arrays, bundle, cap)
    half = len(spots) // 2
    upper, lower = rows_at(arrays, spots[:half], cap), rows_at(arrays, spots[half:], cap)
    odd = info[0] == 1
    rows = jnp.concatenate([jnp.where(odd, upper, lower), jnp.where(odd, lower, upper)], axis=0)
    for part in tiles(weight.shape[1]):
        partial = jnp.dot(rows, weight[:, part], preferred_element_type=F32)
        send[:, part] = partial[: half * cap].astype(BF16)
        keep[:, part] = partial[half * cap :]


def first(info, blocks, weight, cap, after, bundles=()):
    arrays = arrays_of([block for group in (blocks, *bundles) for block in group])
    features, width = weight.shape
    size = len(blocks) // 2 * cap
    return call(
        functools.partial(
            first_body,
            len(arrays),
            spots_of(blocks, arrays),
            [spots_of(bundle, arrays) for bundle in bundles],
            cap,
        ),
        "first",
        (info, weight, *arrays),
        [SMEM] + [VMEM] * (1 + len(arrays)),
        [jax.ShapeDtypeStruct((size, width), BF16), jax.ShapeDtypeStruct((size, width), F32)]
        + [jax.ShapeDtypeStruct((len(bundle) * cap, features), BF16) for bundle in bundles],
        [VMEM] * (2 + len(bundles)),
        4 * size * features * width,
        16,
        after=after,
    )


def add_body(count, keep, *refs):
    total = keep[...]
    for got in refs[:count]:
        total = total + got[...].astype(F32)
    refs[count][...] = total.astype(BF16)


def add(keep, gots, after):
    return call(
        functools.partial(add_body, len(gots)),
        "add",
        (keep, *gots),
        [VMEM] * (1 + len(gots)),
        [jax.ShapeDtypeStruct(keep.shape, BF16)],
        [VMEM],
        keep.size,
        8,
        after=after,
    )[0]


def prep_body(saved, gate_factor, up_factor, hidden):
    slots, width = hidden.shape
    step = 32 if slots % 32 == 0 else slots

    def some(i, carry):
        at = pl.ds(pl.multiple_of(i * step, step), step)
        gate, up, sigmoid = swish_parts(saved[at, :], width)
        silu = gate * sigmoid
        gate_factor[at, :] = up * sigmoid * (1.0 + gate * (1.0 - sigmoid))
        up_factor[at, :] = silu
        hidden[at, :] = (silu * up).astype(BF16)
        return carry

    lax.fori_loop(0, slots // step, some, 0)


def prep(saved_pre, after):
    slots, width = saved_pre.shape[0], saved_pre.shape[1] // 2
    return call(
        prep_body,
        "prep",
        (saved_pre,),
        [VMEM],
        [jax.ShapeDtypeStruct((slots, width), dtype) for dtype in (F32, F32, BF16)],
        [VMEM] * 3,
        1,
        16,
        after=after,
    )


def turn_body(*refs):
    half = len(refs) // 2
    for weight, turned in zip(refs[:half], refs[half:]):
        for part in tiles(weight.shape[0]):
            turned[:, part] = weight[part, :].T


def turn(weights, after):
    shapes = [jax.ShapeDtypeStruct(x.shape[::-1], x.dtype) for x in weights]
    count = len(weights)
    return call(
        turn_body, "turn", weights, [VMEM] * count, shapes, [VMEM] * count, 1, 16, after=after
    )


def slots_of(ref, info, k, cap):
    return ref[pl.ds(pl.multiple_of((info[1] ^ k) * cap, cap), cap), :]


def second_body(chunk, info, own, other, gate_factor, up_factor, w_gate, w_up, *outs):
    cap = outs[0].shape[0]
    odd = info[0] == 1
    mine, yours = own[...], other[...]
    grad = jnp.concatenate([jnp.where(odd, yours, mine), jnp.where(odd, mine, yours)], axis=0)
    grad = grad.astype(F32)
    d_gate, d_up = (
        jnp.concatenate(
            [
                grad[i * cap : (i + 1) * cap] * slots_of(factor, info, k, cap)
                for i, k in enumerate(chunk)
            ],
            axis=0,
        ).astype(BF16)
        for factor in (gate_factor, up_factor)
    )
    for part in tiles(w_gate.shape[1]):
        result = jnp.dot(d_gate, w_gate[:, part], preferred_element_type=F32)
        result += jnp.dot(d_up, w_up[:, part], preferred_element_type=F32)
        result = result.astype(BF16)
        for i, out in enumerate(outs):
            out[:, part] = result[i * cap : (i + 1) * cap]


def second(info, own, other, factors, weights, chunk, cap, after):
    width, features = weights[0].shape
    return call(
        functools.partial(second_body, chunk),
        "second",
        (info, own, other, *factors, *weights),
        [SMEM] + [VMEM] * 6,
        [jax.ShapeDtypeStruct((cap, features), BF16)] * len(chunk),
        [VMEM] * len(chunk),
        4 * len(chunk) * cap * features * width,
        24,
        after=after,
        weight=LATE_WEIGHT,
    )


def down_body(count, spots, groups, info, place, hidden, *refs):
    arrays, out, early, late, sums, sems = refs[:count], *refs[count:]
    cap = hidden.shape[0] // len(spots)
    features, width = out.shape
    for group, turned in zip(groups, (early, late)):
        turned[...] = rows_at([place], [(0, k * cap) for k in group], cap).T
    mine = jnp.concatenate([slots_of(hidden, info, k, cap) for k in range(len(spots))], axis=0)
    tile = sums.shape[1]
    copies = []
    for i in range(features // tile):
        part = [arrays[a][row : row + cap, i * tile : (i + 1) * tile] for a, row in spots]
        part = jnp.concatenate(part, axis=0)
        sums[i] = lax.dot_general(part, mine, BY_ROWS, preferred_element_type=F32)
        copies.append(
            pltpu.make_async_copy(sums.at[i], out.at[pl.ds(i * tile, tile)], sems.at[i])
        )
        copies[-1].start()
    for copy in copies:
        copy.wait()


def down(info, blocks, hidden, place, features, groups, after):
    arrays = arrays_of(blocks)
    slots, width = hidden.shape
    tile = min(features, 256)
    steps = features // tile
    return call(
        functools.partial(down_body, len(arrays), spots_of(blocks, arrays), groups),
        "down",
        (info, place, hidden, *arrays),
        [SMEM] + [VMEM] * (2 + len(arrays)),
        [jax.ShapeDtypeStruct((features, width), F32)]
        + [
            jax.ShapeDtypeStruct((place.shape[1], slots // len(blocks) * len(group)), BF16)
            for group in groups
        ],
        [HBM, VMEM, VMEM],
        2 * slots * features * width,
        24,
        [pltpu.VMEM((steps, tile, width), F32), pltpu.SemaphoreType.DMA((steps,))],
        after=after,
        weight=LATE_WEIGHT,
    )


def gather_body(count, place, *refs):
    blocks, sooner, out = refs[:count], refs[count:-1], refs[-1]
    for part in tiles(out.shape[1]):
        returned = jnp.concatenate([block[:, part] for block in blocks], axis=0)
        rows = jnp.dot(place[...], returned, preferred_element_type=F32).astype(BF16)
        out[:, part] = rows + sooner[0][:, part] if sooner else rows


def gather(place, blocks, after, sooner=()):
    count, (cap, features) = len(blocks), blocks[0].shape
    rows = place.shape[0]
    return call(
        functools.partial(gather_body, count),
        "gather",
        (place, *blocks, *sooner),
        [VMEM] * (1 + count + len(sooner)),
        [jax.ShapeDtypeStruct((rows, features), BF16)],
        [VMEM],
        2 * rows * count * cap * features,
        16,
        after=after,
    )[0]


def swap(block, axis, k):
    size = lax.axis_size(axis)
    return lax.ppermute(block, axis, [(i, i ^ k) for i in range(size)])


def near_device(dy_values, dy_scales, expert_ids, saved_pre, w_gate, w_up, w_down):
    groups = lax.axis_size("expert")
    cap = saved_pre.shape[0] // groups
    features = dy_values.shape[1]
    info = jnp.stack([lax.axis_index("dp") % 2, lax.axis_index("expert")]).astype(jnp.int32)
    place, even, odd = pack(info, expert_ids, dy_values, dy_scales, groups, cap)
    last, result = [place], {}
    keeps, gots, owns, others, returned = {}, {}, {}, {}, {}

    side = swap(odd, "expert", 1)
    blocks = {0: (even, 0), 1: (side, 0)}
    chips = range(2, groups, 2)
    bundles = [((even, k // 2 * cap), (side, k // 2 * cap)) for k in chips]

    def do_first(c):
        chosen = [blocks[k] for k in CHUNKS[c]]
        send, keeps[c], *sent = first(info, chosen, w_down[0], cap, last, () if c else bundles)
        last[:] = [send]
        gots[c] = [swap(send, "dp", 1)]
        for k, bundle in sorted(zip(chips, sent), reverse=True):
            got = swap(bundle, "expert", k)
            blocks.update({k: (got, 0), k + 1: (got, cap)})

    def do_add(c):
        part = add(keeps[c], gots[c], last)
        last[:] = [part]
        if len(gots[c]) == 1:
            gots[c].append(swap(part, "dp", 2))
        else:
            owns[c], others[c] = part, swap(part, "dp", 1)

    def do_prep(_):
        *result["factors"], result["hidden"] = prep(saved_pre, last)
        last[:] = [result["hidden"]]

    def do_turn(_):
        result["weights"] = turn((w_gate[0], w_up[0]), last)
        last[:] = result["weights"][:1]

    def do_second(c):
        grads = second(
            info, owns[c], others[c], result["factors"], result["weights"], CHUNKS[c], cap, last
        )
        last[:] = [grads[0]]
        for k, grad in zip(CHUNKS[c], grads):
            returned[k] = swap(grad, "expert", k) if k else grad

    def do_down(_):
        every = [blocks[k] for k in range(groups)]
        result["down"], *result["turned"] = down(
            info, every, result["hidden"], place, features, (EARLY, LATE), last
        )
        last[:] = result["turned"][:1]

    steps = {
        "first": do_first,
        "add": do_add,
        "prep": do_prep,
        "turn": do_turn,
        "second": do_second,
        "down": do_down,
    }
    for step, c in ORDER:
        steps[step](c)
    early, late = result["turned"]
    sooner = gather(early, [returned[k] for k in EARLY], last)
    grad_input = gather(late, [returned[k] for k in LATE], [], [sooner])
    return (grad_input, result["down"][None])


def far_device(dy_values, dy_scales, expert_ids, saved_pre, w_gate, w_up, w_down):
    groups, width = lax.axis_size("expert"), w_down.shape[2]
    slots = saved_pre.shape[0]
    cap = slots // groups
    route = expert_ids[:, 0]
    rows, count = route.shape[0], dy_scales.shape[1]
    onehot = (route[:, None] == jnp.arange(groups, dtype=jnp.int32)[None, :]).astype(BF16)
    earlier = jnp.dot(jnp.tri(rows, k=-1, dtype=BF16), onehot, preferred_element_type=F32)
    rank = jnp.sum(earlier * onehot.astype(F32), axis=1).astype(jnp.int32)
    place = route * cap + rank
    chosen = (place[:, None] == jnp.arange(slots, dtype=jnp.int32)[None, :]).astype(BF16)
    scaled = dy_values.astype(F32).reshape(rows, count, -1) * dy_scales.astype(F32)[:, :, None]
    scaled = scaled.reshape(dy_values.shape).astype(BF16)
    packed = lax.dot_general(chosen, scaled, BY_ROWS, preferred_element_type=F32).astype(BF16)
    received = lax.all_to_all(packed, "expert", split_axis=0, concat_axis=0, tiled=True)
    gate, up, sigmoid = swish_parts(saved_pre, width)
    hidden = (gate * sigmoid * up).astype(BF16)
    partial = jnp.dot(received, w_down[0], preferred_element_type=F32)
    grad = lax.psum(partial, "dp")
    d_gate = (grad * up * sigmoid * (1.0 + gate * (1.0 - sigmoid))).astype(BF16)
    d_up = (grad * (gate * sigmoid)).astype(BF16)
    result = lax.dot_general(d_gate, w_gate[0], TRANSPOSED, preferred_element_type=F32)
    result += lax.dot_general(d_up, w_up[0], TRANSPOSED, preferred_element_type=F32)
    returned = lax.all_to_all(
        result.astype(BF16), "expert", split_axis=0, concat_axis=0, tiled=True
    )
    grad_input = jnp.dot(chosen, returned, preferred_element_type=F32).astype(BF16)
    grad_down = lax.dot_general(received, hidden, BY_ROWS, preferred_element_type=F32)
    return (grad_input, grad_down[None])


def solution(mesh):
    near = mesh.shape["expert"] == 8 and mesh.shape["dp"] == 4
    return jax.shard_map(
        near_device if near else far_device,
        mesh=mesh,
        in_specs=(
            P("expert", "dp"),
            P("expert", "dp"),
            P("expert", None),
            P("expert", None),
            P("expert", "dp", None),
            P("expert", "dp", None),
            P("expert", "dp", None),
        ),
        out_specs=(P("expert", "dp"), P("expert", "dp", None)),
        check_vma=False,
    )
```

time: 167 us -> 65.6 us (0.39)
  waiting for transfers between devices: 112 us -> 15.1 us
  Pallas kernels: 0 us -> 18.4 us
  starting transfers between devices: 12.4 us -> 30.3 us
  between operations: 14.1 us -> 0.82 us
  local copies, waits for them, and re-layouts: 10.8 us -> 0.02 us
  matrix products: 9.37 us -> 0 us
  other arithmetic: 7.85 us -> 0.76 us
    psum x1 -> x0, waiting for transfers between devices: 86.1 us -> none  [per_device(): hidden_grad = lax.psum(partial_grad, 'dp')]
    ppermute x0 -> x23, starting transfers between devices: none -> 30.3 us  [swap(): return lax.ppermute(block, axis, [(i, i ^ k) for i in range(size)])]
    all_to_all x3 -> x0, waiting for transfers between devices: 25.8 us -> none  [the longest x1 15.1 us: per_device(): lax.all_to_all(out_values, 'expert', split_axis=0, concat_axis=0, tiled=T...]
    pallas_call x0 -> x22, Pallas kernels: none -> 18.4 us  [call(): pl.pallas_call(run, name=name, out_shape=list(outs) + [jax.ShapeDtypeStru...]
    ppermute x0 -> x23, waiting for transfers between devices: none -> 15.1 us  [swap(): return lax.ppermute(block, axis, [(i, i ^ k) for i in range(size)])]
    all_to_all x3 -> x0, starting transfers between devices: 12.4 us -> none  [the longest x1 5.17 us: per_device(): lax.all_to_all(out_scales, 'expert', split_axis=0, concat_axis=0, tiled=T...]
    dot_general x3 -> x0, matrix products: 9.37 us -> none  [the longest x1 3.43 us: per_device(): lax.dot_general(received, hidden, (((0,), (0,)), ((), ())), preferred_ele...]
    convert_element_type x4 -> x1, other arithmetic: 5.78 us -> 0.69 us  [pack(): scales.T.astype(F32)]
  transfers between devices with their start and end apart: 4 -> 23, of which waited for: 4 -> 11; matrix products, arithmetic and copies ran while one was open for 5% -> 0% of each run, Pallas kernels for 0% -> 22%
where the time goes in v1:
time: 65.6 us; the launch traced here: 65.4 us
  starting transfers between devices  30.3 us (46%)
  Pallas kernels  18.4 us (28%)
  waiting for transfers between devices  15.1 us (23%)
  between operations  0.82 us (1%)
  other arithmetic  0.76 us (1%)
    ppermute x23, starting transfers between devices, swap(): return lax.ppermute(block, axis, [(i, i ^ k) for i in range(size)])  30.3 us
    pallas_call x22, Pallas kernels, call(): pl.pallas_call(run, name=name, out_shape=list(outs) + [jax.ShapeDtypeStru...  18.4 us
    ppermute x23, waiting for transfers between devices, swap(): return lax.ppermute(block, axis, [(i, i ^ k) for i in range(size)])  15.1 us
  transfers between devices with their start and end apart: 23, of which 11 were waited for; matrix products, arithmetic and copies ran while one was open for 0% of the time, Pallas kernels for 22%

profile of v1, /device:TPU:0, one launch (start us, length us, event | category | flops | bytes accessed | tf_op | source)
XLA Modules:
  0.0 65.4 jit_solution(7967574675771773096)
XLA Ops:
  0.6 0.7 %convert_bitcast_fusion.refs_1_ = f32[8,256]{1,0:T(8,128)S(1)} fusion(bf16[256,8]{0,1:T(8,128)(2,1)} %param.8), kind=kLoop, calls=%fused_computation | loop fusion | flops 2048 | bytes 12288 | tf_op jit(solution)/shard_map/convert_element_type | solution.py:132
  1.3 0.1 pad_add_fusion.refs_0_
  1.4 2.2 %pack.1 = (bf16[512,256]{1,0:T(8,128)(2,1)S(1)}, bf16[256,1024]{1,0:T(8,128)(2,1)S(1)}, bf16[256,1024]{1,0:T(8,128)(2,1)S(1)}) custom-call(s32[2]{0:T(128)S(1)} %pad_add_fusion.refs_0_, f32[8,256]{1,0:T(8,128)S(1)} %convert_bitcast_fusion.refs_1_, s32[1,256]{1,0:T(1,128)} %bitcast.15, bf16[256,1024]{1,0:T(8,128)(2,1)} %refs_3_.1), custom_call_target="tpu_custom_call" | custom-call | flops 5368709120 | bytes 17895696 | tf_op jit(solution)/shard_map/pack/pallas_call | solution.py:41
  3.6 0.5 collective-permute-start
  4.1 1.5 %collective-permute-done.refs_3_.refs_4_ = bf16[256,1024]{1,0:T(8,128)(2,1)S(1)} collective-permute-done((bf16[256,1024]{1,0:T(8,128)(2,1)S(1)}, bf16[256,1024]{1,0:T(8,128)(2,1)S(1)}, u32[]{:S(2)}, u32[]{:S(2)}) %collective-permute-start) | collective-permute-done | bytes 524320 | tf_op jit(solution)/shard_map/ppermute | solution.py:366
  5.6 1.0 %first.4 = (bf16[64,1024]{1,0:T(8,128)(2,1)S(1)}, f32[64,1024]{1,0:T(8,128)S(1)}, bf16[128,1024]{1,0:T(8,128)(2,1)S(1)}, bf16[128,1024]{1,0:T(8,128)(2,1)S(1)}, bf16[128,1024]{1,0:T(8,128)(2,1)S(1)}) custom-call(s32[2]{0:T(128)S(1)} %pad_add_fusion.refs_0_, bf16[1024,1024]{1,0:T(8,128)(2,1)S(1)} %bitcast.11, ...), custom_call_target="tpu_custom_call" | custom-call | flops 5368709120 | bytes 17895696 | tf_op jit(solution)/shard_map/first/pallas_call | solution.py:41
  6.7 3.9 %collective-permute-start.3 = (bf16[128,1024]{1,0:T(8,128)(2,1)S(1)}, bf16[128,1024]{1,0:T(8,128)(2,1)S(1)}, u32[]{:S(2)}, u32[]{:S(2)}) collective-permute-start(bf16[128,1024]{1,0:T(8,128)(2,1)S(1)} %get-tuple-element.39), channel_id=1, source_target_pairs={{0,24},{4,28},{8,16},{12,20},{16,8},{20,12},{24,0},{28,4},{1,25},{... | collective-permute-start | bytes 786440 | tf_op jit(solution)/shard_map/ppermute | solution.py:366
  10.6 1.6 %collective-permute-start.4 = (bf16[64,1024]{1,0:T(8,128)(2,1)S(1)}, bf16[64,1024]{1,0:T(8,128)(2,1)S(1)}, u32[]{:S(2)}, u32[]{:S(2)}) collective-permute-start(bf16[64,1024]{1,0:T(8,128)(2,1)S(1)} %get-tuple-element.35.refs_1_), channel_id=1, source_target_pairs={{0,1},{1,0},{2,3},{3,2},{4,5},{5,4},{6,7},{7,6},{8,9},{9,8},{10,11... | collective-permute-start | bytes 393224 | tf_op jit(solution)/shard_map/ppermute | solution.py:366
  12.1 1.0 %prep.1 = (f32[512,1024]{1,0:T(8,128)S(1)}, f32[512,1024]{1,0:T(8,128)S(1)}, bf16[512,1024]{1,0:T(8,128)(2,1)S(1)}) custom-call(bf16[512,2048]{1,0:T(8,128)(2,1)S(1)} %copy-done, bf16[64,1024]{1,0:T(8,128)(2,1)S(1)} %get-tuple-element.35.refs_1_), custom_call_target="tpu_custom_call" | custom-call | flops 20 | tf_op jit(solution)/shard_map/prep/pallas_call | solution.py:41
  13.2 0.6 collective-permute-start.1
  13.8 0.5 collective-permute-start.2
  14.3 1.5 %collective-permute-done.4.refs_1_ = bf16[64,1024]{1,0:T(8,128)(2,1)S(1)} collective-permute-done((bf16[64,1024]{1,0:T(8,128)(2,1)S(1)}, bf16[64,1024]{1,0:T(8,128)(2,1)S(1)}, u32[]{:S(2)}, u32[]{:S(2)}) %collective-permute-start.4) | collective-permute-done | bytes 131104 | tf_op jit(solution)/shard_map/ppermute | solution.py:366
  15.9 2.7 %collective-permute-start.6 = (bf16[64,1024]{1,0:T(8,128)(2,1)S(1)}, bf16[64,1024]{1,0:T(8,128)(2,1)S(1)}, u32[]{:S(2)}, u32[]{:S(2)}) collective-permute-start(bf16[64,1024]{1,0:T(8,128)(2,1)S(1)} %add.15.refs_3_), channel_id=1, source_target_pairs={{0,2},{1,3},{2,0},{3,1},{4,6},{5,7},{6,4},{7,5},{8,10},{9,11},{10,... | collective-permute-start | bytes 393224 | tf_op jit(solution)/shard_map/ppermute | solution.py:366
  18.5 1.0 %first.5 = (bf16[64,1024]{1,0:T(8,128)(2,1)S(1)}, f32[64,1024]{1,0:T(8,128)S(1)}) custom-call(s32[2]{0:T(128)S(1)} %pad_add_fusion.refs_0_, bf16[1024,1024]{1,0:T(8,128)(2,1)S(1)} %bitcast.12, bf16[128,1024]{1,0:T(8,128)(2,1)S(1)} %collective-permute-done.3.refs_2_.refs_7_, bf16[64,1024]{1,0:T(8,128)(2,1)S(1)} %add.15.refs_3_), custom_call_target="tpu_custom_call" | custom-call | flops 5368709120 | bytes 17895696 | tf_op jit(solution)/shard_map/first/pallas_call | solution.py:41
  19.5 1.6 %collective-permute-start.5 = (bf16[64,1024]{1,0:T(8,128)(2,1)S(1)}, bf16[64,1024]{1,0:T(8,128)(2,1)S(1)}, u32[]{:S(2)}, u32[]{:S(2)}) collective-permute-start(bf16[64,1024]{1,0:T(8,128)(2,1)S(1)} %get-tuple-element.42.refs_2_), channel_id=1, source_target_pairs={{0,1},{1,0},{2,3},{3,2},{4,5},{5,4},{6,7},{7,6},{8,9},{9,8},{10,11... | collective-permute-start | bytes 393224 | tf_op jit(solution)/shard_map/ppermute | solution.py:366
  21.2 1.2 %turn.1 = (bf16[1024,1024]{1,0:T(8,128)(2,1)S(1)}, bf16[1024,1024]{1,0:T(8,128)(2,1)S(1)}) custom-call(bf16[1024,1024]{1,0:T(8,128)(2,1)S(1)} %bitcast.9, bf16[1024,1024]{1,0:T(8,128)(2,1)S(1)} %bitcast.10, bf16[64,1024]{1,0:T(8,128)(2,1)S(1)} %get-tuple-element.42.refs_2_), custom_call_target="tpu_custom_call" | custom-call | flops 20 | tf_op jit(solution)/shard_map/turn/pallas_call | solution.py:41
  22.4 1.7 %collective-permute-done.6.refs_2_ = bf16[64,1024]{1,0:T(8,128)(2,1)S(1)} collective-permute-done((bf16[64,1024]{1,0:T(8,128)(2,1)S(1)}, bf16[64,1024]{1,0:T(8,128)(2,1)S(1)}, u32[]{:S(2)}, u32[]{:S(2)}) %collective-permute-start.6) | collective-permute-done | bytes 131104 | tf_op jit(solution)/shard_map/ppermute | solution.py:366
  24.2 0.6 collective-permute-start.10
  24.8 1.0 %collective-permute-done.5.refs_1_ = bf16[64,1024]{1,0:T(8,128)(2,1)S(1)} collective-permute-done((bf16[64,1024]{1,0:T(8,128)(2,1)S(1)}, bf16[64,1024]{1,0:T(8,128)(2,1)S(1)}, u32[]{:S(2)}, u32[]{:S(2)}) %collective-permute-start.5) | collective-permute-done | bytes 131104 | tf_op jit(solution)/shard_map/ppermute | solution.py:366
  25.9 2.5 %collective-permute-start.8 = (bf16[64,1024]{1,0:T(8,128)(2,1)S(1)}, bf16[64,1024]{1,0:T(8,128)(2,1)S(1)}, u32[]{:S(2)}, u32[]{:S(2)}) collective-permute-start(bf16[64,1024]{1,0:T(8,128)(2,1)S(1)} %add.17.refs_4_), channel_id=1, source_target_pairs={{0,2},{1,3},{2,0},{3,1},{4,6},{5,7},{6,4},{7,5},{8,10},{9,11},{10,... | collective-permute-start | bytes 393224 | tf_op jit(solution)/shard_map/ppermute | solution.py:366
  28.4 1.0 %first.6 = (bf16[64,1024]{1,0:T(8,128)(2,1)S(1)}, f32[64,1024]{1,0:T(8,128)S(1)}) custom-call(s32[2]{0:T(128)S(1)} %pad_add_fusion.refs_0_, bf16[1024,1024]{1,0:T(8,128)(2,1)S(1)} %bitcast.13, bf16[128,1024]{1,0:T(8,128)(2,1)S(1)} %collective-permute-done.1.refs_2_.refs_5_, bf16[128,1024]{1,0:T(8,128)(2,1)S(1)} %collective-permute-done.2.refs_3_.refs_6_, ...), custom_call_target="tpu_custom_call" | custom-call | flops 5368709120 | bytes 17895696 | tf_op jit(solution)/shard_map/first/pallas_call | solution.py:41
  29.4 1.3 %collective-permute-start.9 = (bf16[64,1024]{1,0:T(8,128)(2,1)S(1)}, bf16[64,1024]{1,0:T(8,128)(2,1)S(1)}, u32[]{:S(2)}, u32[]{:S(2)}) collective-permute-start(bf16[64,1024]{1,0:T(8,128)(2,1)S(1)} %get-tuple-element.44.refs_4_), channel_id=1, source_target_pairs={{0,1},{1,0},{2,3},{3,2},{4,5},{5,4},{6,7},{7,6},{8,9},{9,8},{10,11... | collective-permute-start | bytes 393224 | tf_op jit(solution)/shard_map/ppermute | solution.py:366
  30.7 1.0 %first.7 = (bf16[64,1024]{1,0:T(8,128)(2,1)S(1)}, f32[64,1024]{1,0:T(8,128)S(1)}) custom-call(s32[2]{0:T(128)S(1)} %pad_add_fusion.refs_0_, bf16[1024,1024]{1,0:T(8,128)(2,1)S(1)} %bitcast.14, bf16[128,1024]{1,0:T(8,128)(2,1)S(1)} %collective-permute-done.1.refs_2_.refs_5_, bf16[128,1024]{1,0:T(8,128)(2,1)S(1)} %collective-permute-done.2.refs_3_.refs_6_, ...), custom_call_target="tpu_custom_call" | custom-call | flops 5368709120 | bytes 17895696 | tf_op jit(solution)/shard_map/first/pallas_call | solution.py:41
  31.7 0.9 %collective-permute-start.7 = (bf16[64,1024]{1,0:T(8,128)(2,1)S(1)}, bf16[64,1024]{1,0:T(8,128)(2,1)S(1)}, u32[]{:S(2)}, u32[]{:S(2)}) collective-permute-start(bf16[64,1024]{1,0:T(8,128)(2,1)S(1)} %get-tuple-element.46.refs_7_), channel_id=1, source_target_pairs={{0,1},{1,0},{2,3},{3,2},{4,5},{5,4},{6,7},{7,6},{8,9},{9,8},{10,11... | collective-permute-start | bytes 393224 | tf_op jit(solution)/shard_map/ppermute | solution.py:366
  32.5 1.3 %second.4 = (bf16[64,1024]{1,0:T(8,128)(2,1)S(1)}, bf16[64,1024]{1,0:T(8,128)(2,1)S(1)}) custom-call(s32[2]{0:T(128)S(1)} %pad_add_fusion.refs_0_, bf16[64,1024]{1,0:T(8,128)(2,1)S(1)} %add.16.refs_2_.refs_1_, bf16[64,1024]{1,0:T(8,128)(2,1)S(1)} %collective-permute-done.10.refs_2_, f32[512,1024]{1,0:T(8,128)S(1)} %get-tuple-element.48.refs_3_, ...), custom_call_target="tpu_custom_call" | custom-call | flops 10737418240 | bytes 35791392 | tf_op jit(solution)/shard_map/second/pallas_call | solution.py:41
  33.8 2.1 %collective-permute-done.9.refs_1_ = bf16[64,1024]{1,0:T(8,128)(2,1)S(1)} collective-permute-done((bf16[64,1024]{1,0:T(8,128)(2,1)S(1)}, bf16[64,1024]{1,0:T(8,128)(2,1)S(1)}, u32[]{:S(2)}, u32[]{:S(2)}) %collective-permute-start.9) | collective-permute-done | bytes 131104 | tf_op jit(solution)/shard_map/ppermute | solution.py:366
  36.0 2.4 %collective-permute-start.12 = (bf16[64,1024]{1,0:T(8,128)(2,1)S(1)}, bf16[64,1024]{1,0:T(8,128)(2,1)S(1)}, u32[]{:S(2)}, u32[]{:S(2)}) collective-permute-start(bf16[64,1024]{1,0:T(8,128)(2,1)S(1)} %add.18.refs_3_), channel_id=1, source_target_pairs={{0,2},{1,3},{2,0},{3,1},{4,6},{5,7},{6,4},{7,5},{8,10},{9,11},{10,... | collective-permute-start | bytes 393224 | tf_op jit(solution)/shard_map/ppermute | solution.py:366
  38.4 1.6 %collective-permute-start.13 = (bf16[64,1024]{1,0:T(8,128)(2,1)S(1)}, bf16[64,1024]{1,0:T(8,128)(2,1)S(1)}, u32[]{:S(2)}, u32[]{:S(2)}) collective-permute-start(bf16[64,1024]{1,0:T(8,128)(2,1)S(1)} %add.19.refs_2_.refs_1_), channel_id=1, source_target_pairs={{0,1},{1,0},{2,3},{3,2},{4,5},{5,4},{6,7},{7,6},{8,9},{9,8},{10,11... | collective-permute-start | bytes 393224 | tf_op jit(solution)/shard_map/ppermute | solution.py:366
  40.0 0.9 %collective-permute-start.11 = (bf16[64,1024]{1,0:T(8,128)(2,1)S(1)}, bf16[64,1024]{1,0:T(8,128)(2,1)S(1)}, u32[]{:S(2)}, u32[]{:S(2)}) collective-permute-start(bf16[64,1024]{1,0:T(8,128)(2,1)S(1)} %add.20.refs_8_), channel_id=1, source_target_pairs={{0,2},{1,3},{2,0},{3,1},{4,6},{5,7},{6,4},{7,5},{8,10},{9,11},{10,... | collective-permute-start | bytes 393224 | tf_op jit(solution)/shard_map/ppermute | solution.py:366
  40.9 3.0 %down.1 = (f32[1024,1024]{1,0:T(8,128)}, bf16[256,384]{1,0:T(8,128)(2,1)S(1)}, bf16[256,128]{1,0:T(8,128)(2,1)S(1)}) custom-call(s32[2]{0:T(128)S(1)} %pad_add_fusion.refs_0_, bf16[512,256]{1,0:T(8,128)(2,1)S(1)} %get-tuple-element.32.refs_4_.refs_1_, bf16[512,1024]{1,0:T(8,128)(2,1)S(1)} %get-tuple-element.36.refs_2_, ...), custom_call_target="tpu_custom_call" | custom-call | flops 21474836480 | bytes 71582784 | tf_op jit(solution)/shard_map/down/pallas_call | solution.py:41
  44.0 1.3 %second.5 = (bf16[64,1024]{1,0:T(8,128)(2,1)S(1)}, bf16[64,1024]{1,0:T(8,128)(2,1)S(1)}) custom-call(s32[2]{0:T(128)S(1)} %pad_add_fusion.refs_0_, bf16[64,1024]{1,0:T(8,128)(2,1)S(1)} %add.19.refs_2_.refs_1_, bf16[64,1024]{1,0:T(8,128)(2,1)S(1)} %collective-permute-done.13.refs_2_, f32[512,1024]{1,0:T(8,128)S(1)} %get-tuple-element.48.refs_3_, ...), custom_call_target="tpu_custom_call" | custom-call | flops 10737418240 | bytes 35791392 | tf_op jit(solution)/shard_map/second/pallas_call | solution.py:41
  45.3 0.7 %collective-permute-done.12.refs_2_ = bf16[64,1024]{1,0:T(8,128)(2,1)S(1)} collective-permute-done((bf16[64,1024]{1,0:T(8,128)(2,1)S(1)}, bf16[64,1024]{1,0:T(8,128)(2,1)S(1)}, u32[]{:S(2)}, u32[]{:S(2)}) %collective-permute-start.12) | collective-permute-done | bytes 131104 | tf_op jit(solution)/shard_map/ppermute | solution.py:366
  46.0 2.4 %collective-permute-start.15 = (bf16[64,1024]{1,0:T(8,128)(2,1)S(1)}, bf16[64,1024]{1,0:T(8,128)(2,1)S(1)}, u32[]{:S(2)}, u32[]{:S(2)}) collective-permute-start(bf16[64,1024]{1,0:T(8,128)(2,1)S(1)} %add.21.refs_3_.refs_1_), channel_id=1, source_target_pairs={{0,1},{1,0},{2,3},{3,2},{4,5},{5,4},{6,7},{7,6},{8,9},{9,8},{10,11... | collective-permute-start | bytes 393224 | tf_op jit(solution)/shard_map/ppermute | solution.py:366
  48.4 2.0 %collective-permute-start.19 = (bf16[64,1024]{1,0:T(8,128)(2,1)S(1)}, bf16[64,1024]{1,0:T(8,128)(2,1)S(1)}, u32[]{:S(2)}, u32[]{:S(2)}) collective-permute-start(bf16[64,1024]{1,0:T(8,128)(2,1)S(1)} %get-tuple-element.54.refs_3_), channel_id=1, source_target_pairs={{0,24},{4,28},{8,16},{12,20},{16,8},{20,12},{24,0},{28,4},{1,25},{... | collective-permute-start | bytes 393224 | tf_op jit(solution)/shard_map/ppermute | solution.py:366
  50.4 0.2 collective-permute-start.14
  50.6 0.7 %collective-permute-start.20 = (bf16[64,1024]{1,0:T(8,128)(2,1)S(1)}, bf16[64,1024]{1,0:T(8,128)(2,1)S(1)}, u32[]{:S(2)}, u32[]{:S(2)}) collective-permute-start(bf16[64,1024]{1,0:T(8,128)(2,1)S(1)} %get-tuple-element.59), channel_id=1, source_target_pairs={{0,28},{4,24},{8,20},{12,16},{16,12},{20,8},{24,4},{28,0},{1,29},{... | collective-permute-start | bytes 393224 | tf_op jit(solution)/shard_map/ppermute | solution.py:366
  51.3 1.3 %second.6 = (bf16[64,1024]{1,0:T(8,128)(2,1)S(1)}, bf16[64,1024]{1,0:T(8,128)(2,1)S(1)}) custom-call(s32[2]{0:T(128)S(1)} %pad_add_fusion.refs_0_, bf16[64,1024]{1,0:T(8,128)(2,1)S(1)} %add.21.refs_3_.refs_1_, bf16[64,1024]{1,0:T(8,128)(2,1)S(1)} %collective-permute-done.15.refs_2_, f32[512,1024]{1,0:T(8,128)S(1)} %get-tuple-element.48.refs_3_, ...), custom_call_target="tpu_custom_call" | custom-call | flops 10737418240 | bytes 35791392 | tf_op jit(solution)/shard_map/second/pallas_call | solution.py:41
  52.6 1.3 %collective-permute-start.21 = (bf16[64,1024]{1,0:T(8,128)(2,1)S(1)}, bf16[64,1024]{1,0:T(8,128)(2,1)S(1)}, u32[]{:S(2)}, u32[]{:S(2)}) collective-permute-start(bf16[64,1024]{1,0:T(8,128)(2,1)S(1)} %get-tuple-element.55.refs_7_), channel_id=1, source_target_pairs={{0,12},{4,8},{8,4},{12,0},{16,28},{20,24},{24,20},{28,16},{1,13},{... | collective-permute-start | bytes 393224 | tf_op jit(solution)/shard_map/ppermute | solution.py:366
  54.0 2.1 %collective-permute-done.14.refs_2_ = bf16[64,1024]{1,0:T(8,128)(2,1)S(1)} collective-permute-done((bf16[64,1024]{1,0:T(8,128)(2,1)S(1)}, bf16[64,1024]{1,0:T(8,128)(2,1)S(1)}, u32[]{:S(2)}, u32[]{:S(2)}) %collective-permute-start.14) | collective-permute-done | bytes 131104 | tf_op jit(solution)/shard_map/ppermute | solution.py:366
  56.1 1.3 %second.7 = (bf16[64,1024]{1,0:T(8,128)(2,1)S(1)}, bf16[64,1024]{1,0:T(8,128)(2,1)S(1)}) custom-call(s32[2]{0:T(128)S(1)} %pad_add_fusion.refs_0_, bf16[64,1024]{1,0:T(8,128)(2,1)S(1)} %add.22.refs_7_.refs_1_, bf16[64,1024]{1,0:T(8,128)(2,1)S(1)} %collective-permute-done.14.refs_2_, f32[512,1024]{1,0:T(8,128)S(1)} %get-tuple-element.48.refs_3_, ...), custom_call_target="tpu_custom_call" | custom-call | flops 10737418240 | bytes 35791392 | tf_op jit(solution)/shard_map/second/pallas_call | solution.py:41
  57.4 1.2 %collective-permute-start.16 = (bf16[64,1024]{1,0:T(8,128)(2,1)S(1)}, bf16[64,1024]{1,0:T(8,128)(2,1)S(1)}, u32[]{:S(2)}, u32[]{:S(2)}) collective-permute-start(bf16[64,1024]{1,0:T(8,128)(2,1)S(1)} %get-tuple-element.56.refs_7_), channel_id=1, source_target_pairs={{0,8},{4,12},{8,0},{12,4},{16,24},{20,28},{24,16},{28,20},{1,9},{5... | collective-permute-start | bytes 393224 | tf_op jit(solution)/shard_map/ppermute | solution.py:366
  58.6 1.0 %collective-permute-start.17 = (bf16[64,1024]{1,0:T(8,128)(2,1)S(1)}, bf16[64,1024]{1,0:T(8,128)(2,1)S(1)}, u32[]{:S(2)}, u32[]{:S(2)}) collective-permute-start(bf16[64,1024]{1,0:T(8,128)(2,1)S(1)} %get-tuple-element.57), channel_id=1, source_target_pairs={{0,16},{4,20},{8,24},{12,28},{16,0},{20,4},{24,8},{28,12},{1,17},{... | collective-permute-start | bytes 393224 | tf_op jit(solution)/shard_map/ppermute | solution.py:366
  59.6 1.0 %collective-permute-done.21.refs_5_ = bf16[64,1024]{1,0:T(8,128)(2,1)S(1)} collective-permute-done((bf16[64,1024]{1,0:T(8,128)(2,1)S(1)}, bf16[64,1024]{1,0:T(8,128)(2,1)S(1)}, u32[]{:S(2)}, u32[]{:S(2)}) %collective-permute-start.21) | collective-permute-done | bytes 131104 | tf_op jit(solution)/shard_map/ppermute | solution.py:366
  60.6 0.9 %collective-permute-done.22.refs_6_ = bf16[64,1024]{1,0:T(8,128)(2,1)S(1)} collective-permute-done((bf16[64,1024]{1,0:T(8,128)(2,1)S(1)}, bf16[64,1024]{1,0:T(8,128)(2,1)S(1)}, u32[]{:S(2)}, u32[]{:S(2)}) %collective-permute-start.22) | collective-permute-done | bytes 131104 | tf_op jit(solution)/shard_map/ppermute | solution.py:366
  61.5 0.4 gather.2.refs_3_
  61.9 1.9 %collective-permute-done.16.refs_1_ = bf16[64,1024]{1,0:T(8,128)(2,1)S(1)} collective-permute-done((bf16[64,1024]{1,0:T(8,128)(2,1)S(1)}, bf16[64,1024]{1,0:T(8,128)(2,1)S(1)}, u32[]{:S(2)}, u32[]{:S(2)}) %collective-permute-start.16) | collective-permute-done | bytes 131104 | tf_op jit(solution)/shard_map/ppermute | solution.py:366
  63.8 0.5 collective-permute-done.17.refs_2_
  64.3 1.1 %gather.3 = bf16[256,1024]{1,0:T(8,128)(2,1)} custom-call(bf16[256,128]{1,0:T(8,128)(2,1)S(1)} %get-tuple-element.52.refs_0_, bf16[64,1024]{1,0:T(8,128)(2,1)S(1)} %collective-permute-done.16.refs_1_, bf16[64,1024]{1,0:T(8,128)(2,1)S(1)} %collective-permute-done.17.refs_2_, bf16[256,1024]{1,0:T(8,128)(2,1)S(1)} %gather.2.refs_3_), custom_call_target="tpu_custom_call" | custom-call | flops 1342177280 | bytes 4473924 | tf_op jit(solution)/shard_map/gather/pallas_call | solution.py:41
  (30 shorter events, 0.3 us)
Async XLA Ops:
  1.4 4.2 %copy-start.3 = (bf16[1,1024,1024]{2,1,0:T(8,128)(2,1)S(1)}, bf16[1,1024,1024]{2,1,0:T(8,128)(2,1)}, u32[]{:S(2)}) copy-start(bf16[1,1024,1024]{2,1,0:T(8,128)(2,1)} %param.13) | copy-start | bytes 6291460
  3.6 2.1 %collective-permute-start = (bf16[256,1024]{1,0:T(8,128)(2,1)S(1)}, bf16[256,1024]{1,0:T(8,128)(2,1)S(1)}, u32[]{:S(2)}, u32[]{:S(2)}) collective-permute-start(bf16[256,1024]{1,0:T(8,128)(2,1)S(1)} %get-tuple-element.34), channel_id=1, source_target_pairs={{0,4},{4,0},{8,12},{12,8},{16,20},{20,16},{24,28},{28,24},{1,5},{5... | collective-permute-start | bytes 1572872 | tf_op jit(solution)/shard_map/ppermute | solution.py:366
  5.6 6.5 %copy-start = (bf16[512,2048]{1,0:T(8,128)(2,1)S(1)}, bf16[512,2048]{1,0:T(8,128)(2,1)}, u32[]{:S(2)}) copy-start(bf16[512,2048]{1,0:T(8,128)(2,1)} %refs_0_.1) | copy-start | bytes 6291460
  6.7 11.9 %collective-permute-start.3 = (bf16[128,1024]{1,0:T(8,128)(2,1)S(1)}, bf16[128,1024]{1,0:T(8,128)(2,1)S(1)}, u32[]{:S(2)}, u32[]{:S(2)}) collective-permute-start(bf16[128,1024]{1,0:T(8,128)(2,1)S(1)} %get-tuple-element.39), channel_id=1, source_target_pairs={{0,24},{4,28},{8,16},{12,20},{16,8},{20,12},{24,0},{28,4},{1,25},{... | collective-permute-start | bytes 786440 | tf_op jit(solution)/shard_map/ppermute | solution.py:366
  10.6 5.3 %collective-permute-start.4 = (bf16[64,1024]{1,0:T(8,128)(2,1)S(1)}, bf16[64,1024]{1,0:T(8,128)(2,1)S(1)}, u32[]{:S(2)}, u32[]{:S(2)}) collective-permute-start(bf16[64,1024]{1,0:T(8,128)(2,1)S(1)} %get-tuple-element.35.refs_1_), channel_id=1, source_target_pairs={{0,1},{1,0},{2,3},{3,2},{4,5},{5,4},{6,7},{7,6},{8,9},{9,8},{10,11... | collective-permute-start | bytes 393224 | tf_op jit(solution)/shard_map/ppermute | solution.py:366
  13.2 15.2 %collective-permute-start.1 = (bf16[128,1024]{1,0:T(8,128)(2,1)S(1)}, bf16[128,1024]{1,0:T(8,128)(2,1)S(1)}, u32[]{:S(2)}, u32[]{:S(2)}) collective-permute-start(bf16[128,1024]{1,0:T(8,128)(2,1)S(1)} %get-tuple-element.37), channel_id=1, source_target_pairs={{0,8},{4,12},{8,0},{12,4},{16,24},{20,28},{24,16},{28,20},{1,9},{5... | collective-permute-start | bytes 786440 | tf_op jit(solution)/shard_map/ppermute | solution.py:366
  13.8 14.6 %collective-permute-start.2 = (bf16[128,1024]{1,0:T(8,128)(2,1)S(1)}, bf16[128,1024]{1,0:T(8,128)(2,1)S(1)}, u32[]{:S(2)}, u32[]{:S(2)}) collective-permute-start(bf16[128,1024]{1,0:T(8,128)(2,1)S(1)} %get-tuple-element.38), channel_id=1, source_target_pairs={{0,16},{4,20},{8,24},{12,28},{16,0},{20,4},{24,8},{28,12},{1,17},{... | collective-permute-start | bytes 786440 | tf_op jit(solution)/shard_map/ppermute | solution.py:366
  15.9 5.3 %copy-start.1 = (bf16[1,1024,1024]{2,1,0:T(8,128)(2,1)S(1)}, bf16[1,1024,1024]{2,1,0:T(8,128)(2,1)}, u32[]{:S(2)}) copy-start(bf16[1,1024,1024]{2,1,0:T(8,128)(2,1)} %param.11) | copy-start | bytes 6291460
  15.9 5.3 %copy-start.2 = (bf16[1,1024,1024]{2,1,0:T(8,128)(2,1)S(1)}, bf16[1,1024,1024]{2,1,0:T(8,128)(2,1)}, u32[]{:S(2)}) copy-start(bf16[1,1024,1024]{2,1,0:T(8,128)(2,1)} %param.12) | copy-start | bytes 6291460
  15.9 8.3 %collective-permute-start.6 = (bf16[64,1024]{1,0:T(8,128)(2,1)S(1)}, bf16[64,1024]{1,0:T(8,128)(2,1)S(1)}, u32[]{:S(2)}, u32[]{:S(2)}) collective-permute-start(bf16[64,1024]{1,0:T(8,128)(2,1)S(1)} %add.15.refs_3_), channel_id=1, source_target_pairs={{0,2},{1,3},{2,0},{3,1},{4,6},{5,7},{6,4},{7,5},{8,10},{9,11},{10,... | collective-permute-start | bytes 393224 | tf_op jit(solution)/shard_map/ppermute | solution.py:366
  19.5 6.3 %collective-permute-start.5 = (bf16[64,1024]{1,0:T(8,128)(2,1)S(1)}, bf16[64,1024]{1,0:T(8,128)(2,1)S(1)}, u32[]{:S(2)}, u32[]{:S(2)}) collective-permute-start(bf16[64,1024]{1,0:T(8,128)(2,1)S(1)} %get-tuple-element.42.refs_2_), channel_id=1, source_target_pairs={{0,1},{1,0},{2,3},{3,2},{4,5},{5,4},{6,7},{7,6},{8,9},{9,8},{10,11... | collective-permute-start | bytes 393224 | tf_op jit(solution)/shard_map/ppermute | solution.py:366
  24.2 8.3 %collective-permute-start.10 = (bf16[64,1024]{1,0:T(8,128)(2,1)S(1)}, bf16[64,1024]{1,0:T(8,128)(2,1)S(1)}, u32[]{:S(2)}, u32[]{:S(2)}) collective-permute-start(bf16[64,1024]{1,0:T(8,128)(2,1)S(1)} %add.16.refs_2_.refs_1_), channel_id=1, source_target_pairs={{0,1},{1,0},{2,3},{3,2},{4,5},{5,4},{6,7},{7,6},{8,9},{9,8},{10,11... | collective-permute-start | bytes 393224 | tf_op jit(solution)/shard_map/ppermute | solution.py:366
  25.9 12.5 %collective-permute-start.8 = (bf16[64,1024]{1,0:T(8,128)(2,1)S(1)}, bf16[64,1024]{1,0:T(8,128)(2,1)S(1)}, u32[]{:S(2)}, u32[]{:S(2)}) collective-permute-start(bf16[64,1024]{1,0:T(8,128)(2,1)S(1)} %add.17.refs_4_), channel_id=1, source_target_pairs={{0,2},{1,3},{2,0},{3,1},{4,6},{5,7},{6,4},{7,5},{8,10},{9,11},{10,... | collective-permute-start | bytes 393224 | tf_op jit(solution)/shard_map/ppermute | solution.py:366
  29.4 6.6 %collective-permute-start.9 = (bf16[64,1024]{1,0:T(8,128)(2,1)S(1)}, bf16[64,1024]{1,0:T(8,128)(2,1)S(1)}, u32[]{:S(2)}, u32[]{:S(2)}) collective-permute-start(bf16[64,1024]{1,0:T(8,128)(2,1)S(1)} %get-tuple-element.44.refs_4_), channel_id=1, source_target_pairs={{0,1},{1,0},{2,3},{3,2},{4,5},{5,4},{6,7},{7,6},{8,9},{9,8},{10,11... | collective-permute-start | bytes 393224 | tf_op jit(solution)/shard_map/ppermute | solution.py:366
  31.7 8.3 %collective-permute-start.7 = (bf16[64,1024]{1,0:T(8,128)(2,1)S(1)}, bf16[64,1024]{1,0:T(8,128)(2,1)S(1)}, u32[]{:S(2)}, u32[]{:S(2)}) collective-permute-start(bf16[64,1024]{1,0:T(8,128)(2,1)S(1)} %get-tuple-element.46.refs_7_), channel_id=1, source_target_pairs={{0,1},{1,0},{2,3},{3,2},{4,5},{5,4},{6,7},{7,6},{8,9},{9,8},{10,11... | collective-permute-start | bytes 393224 | tf_op jit(solution)/shard_map/ppermute | solution.py:366
  36.0 10.0 %collective-permute-start.12 = (bf16[64,1024]{1,0:T(8,128)(2,1)S(1)}, bf16[64,1024]{1,0:T(8,128)(2,1)S(1)}, u32[]{:S(2)}, u32[]{:S(2)}) collective-permute-start(bf16[64,1024]{1,0:T(8,128)(2,1)S(1)} %add.18.refs_3_), channel_id=1, source_target_pairs={{0,2},{1,3},{2,0},{3,1},{4,6},{5,7},{6,4},{7,5},{8,10},{9,11},{10,... | collective-permute-start | bytes 393224 | tf_op jit(solution)/shard_map/ppermute | solution.py:366
  38.4 5.5 %collective-permute-start.13 = (bf16[64,1024]{1,0:T(8,128)(2,1)S(1)}, bf16[64,1024]{1,0:T(8,128)(2,1)S(1)}, u32[]{:S(2)}, u32[]{:S(2)}) collective-permute-start(bf16[64,1024]{1,0:T(8,128)(2,1)S(1)} %add.19.refs_2_.refs_1_), channel_id=1, source_target_pairs={{0,1},{1,0},{2,3},{3,2},{4,5},{5,4},{6,7},{7,6},{8,9},{9,8},{10,11... | collective-permute-start | bytes 393224 | tf_op jit(solution)/shard_map/ppermute | solution.py:366
  40.0 10.3 %collective-permute-start.11 = (bf16[64,1024]{1,0:T(8,128)(2,1)S(1)}, bf16[64,1024]{1,0:T(8,128)(2,1)S(1)}, u32[]{:S(2)}, u32[]{:S(2)}) collective-permute-start(bf16[64,1024]{1,0:T(8,128)(2,1)S(1)} %add.20.refs_8_), channel_id=1, source_target_pairs={{0,2},{1,3},{2,0},{3,1},{4,6},{5,7},{6,4},{7,5},{8,10},{9,11},{10,... | collective-permute-start | bytes 393224 | tf_op jit(solution)/shard_map/ppermute | solution.py:366
  46.0 5.3 %collective-permute-start.15 = (bf16[64,1024]{1,0:T(8,128)(2,1)S(1)}, bf16[64,1024]{1,0:T(8,128)(2,1)S(1)}, u32[]{:S(2)}, u32[]{:S(2)}) collective-permute-start(bf16[64,1024]{1,0:T(8,128)(2,1)S(1)} %add.21.refs_3_.refs_1_), channel_id=1, source_target_pairs={{0,1},{1,0},{2,3},{3,2},{4,5},{5,4},{6,7},{7,6},{8,9},{9,8},{10,11... | collective-permute-start | bytes 393224 | tf_op jit(solution)/shard_map/ppermute | solution.py:366
  48.4 9.0 %collective-permute-start.18 = (bf16[64,1024]{1,0:T(8,128)(2,1)S(1)}, bf16[64,1024]{1,0:T(8,128)(2,1)S(1)}, u32[]{:S(2)}, u32[]{:S(2)}) collective-permute-start(bf16[64,1024]{1,0:T(8,128)(2,1)S(1)} %get-tuple-element.58), channel_id=1, source_target_pairs={{0,4},{4,0},{8,12},{12,8},{16,20},{20,16},{24,28},{28,24},{1,5},{5... | collective-permute-start | bytes 393224 | tf_op jit(solution)/shard_map/ppermute | solution.py:366
  48.4 10.2 %collective-permute-start.19 = (bf16[64,1024]{1,0:T(8,128)(2,1)S(1)}, bf16[64,1024]{1,0:T(8,128)(2,1)S(1)}, u32[]{:S(2)}, u32[]{:S(2)}) collective-permute-start(bf16[64,1024]{1,0:T(8,128)(2,1)S(1)} %get-tuple-element.54.refs_3_), channel_id=1, source_target_pairs={{0,24},{4,28},{8,16},{12,20},{16,8},{20,12},{24,0},{28,4},{1,25},{... | collective-permute-start | bytes 393224 | tf_op jit(solution)/shard_map/ppermute | solution.py:366
  50.4 5.7 %collective-permute-start.14 = (bf16[64,1024]{1,0:T(8,128)(2,1)S(1)}, bf16[64,1024]{1,0:T(8,128)(2,1)S(1)}, u32[]{:S(2)}, u32[]{:S(2)}) collective-permute-start(bf16[64,1024]{1,0:T(8,128)(2,1)S(1)} %add.22.refs_7_.refs_1_), channel_id=1, source_target_pairs={{0,1},{1,0},{2,3},{3,2},{4,5},{5,4},{6,7},{7,6},{8,9},{9,8},{10,11... | collective-permute-start | bytes 393224 | tf_op jit(solution)/shard_map/ppermute | solution.py:366
  50.6 9.0 %collective-permute-start.20 = (bf16[64,1024]{1,0:T(8,128)(2,1)S(1)}, bf16[64,1024]{1,0:T(8,128)(2,1)S(1)}, u32[]{:S(2)}, u32[]{:S(2)}) collective-permute-start(bf16[64,1024]{1,0:T(8,128)(2,1)S(1)} %get-tuple-element.59), channel_id=1, source_target_pairs={{0,28},{4,24},{8,20},{12,16},{16,12},{20,8},{24,4},{28,0},{1,29},{... | collective-permute-start | bytes 393224 | tf_op jit(solution)/shard_map/ppermute | solution.py:366
  52.6 8.0 %collective-permute-start.21 = (bf16[64,1024]{1,0:T(8,128)(2,1)S(1)}, bf16[64,1024]{1,0:T(8,128)(2,1)S(1)}, u32[]{:S(2)}, u32[]{:S(2)}) collective-permute-start(bf16[64,1024]{1,0:T(8,128)(2,1)S(1)} %get-tuple-element.55.refs_7_), channel_id=1, source_target_pairs={{0,12},{4,8},{8,4},{12,0},{16,28},{20,24},{24,20},{28,16},{1,13},{... | collective-permute-start | bytes 393224 | tf_op jit(solution)/shard_map/ppermute | solution.py:366
  56.1 5.4 %collective-permute-start.22 = (bf16[64,1024]{1,0:T(8,128)(2,1)S(1)}, bf16[64,1024]{1,0:T(8,128)(2,1)S(1)}, u32[]{:S(2)}, u32[]{:S(2)}) collective-permute-start(bf16[64,1024]{1,0:T(8,128)(2,1)S(1)} %get-tuple-element.60), channel_id=1, source_target_pairs={{0,20},{4,16},{8,28},{12,24},{16,4},{20,0},{24,12},{28,8},{1,21},{... | collective-permute-start | bytes 393224 | tf_op jit(solution)/shard_map/ppermute | solution.py:366
  57.4 6.4 %collective-permute-start.16 = (bf16[64,1024]{1,0:T(8,128)(2,1)S(1)}, bf16[64,1024]{1,0:T(8,128)(2,1)S(1)}, u32[]{:S(2)}, u32[]{:S(2)}) collective-permute-start(bf16[64,1024]{1,0:T(8,128)(2,1)S(1)} %get-tuple-element.56.refs_7_), channel_id=1, source_target_pairs={{0,8},{4,12},{8,0},{12,4},{16,24},{20,28},{24,16},{28,20},{1,9},{5... | collective-permute-start | bytes 393224 | tf_op jit(solution)/shard_map/ppermute | solution.py:366
  58.6 5.7 %collective-permute-start.17 = (bf16[64,1024]{1,0:T(8,128)(2,1)S(1)}, bf16[64,1024]{1,0:T(8,128)(2,1)S(1)}, u32[]{:S(2)}, u32[]{:S(2)}) collective-permute-start(bf16[64,1024]{1,0:T(8,128)(2,1)S(1)} %get-tuple-element.57), channel_id=1, source_target_pairs={{0,16},{4,20},{8,24},{12,28},{16,0},{20,4},{24,8},{28,12},{1,17},{... | collective-permute-start | bytes 393224 | tf_op jit(solution)/shard_map/ppermute | solution.py:366

commit v2 on v1

v2 whole, which is shorter than its diff:
```python
import functools

import jax
import jax.numpy as jnp
from jax import lax
from jax.experimental import pallas as pl
from jax.experimental.pallas import tpu as pltpu
from jax.sharding import PartitionSpec as P

CHUNKS = ((0, 1), (6, 7), (2, 4), (3, 5))
LATER = (2, 4, 3, 5, 0)
PARTS = (CHUNKS[2], CHUNKS[0] + CHUNKS[1], CHUNKS[3])
ORDER = (
    ("first", 0), ("diagonal", 0), ("add", 0), ("prep", 0), ("turn", 0), ("first", 1),
    ("first", 2), ("add", 0), ("add", 1), ("first", 3), ("add", 2), ("add", 1), ("down", 0),
    ("add", 3), ("release", 0), ("add", 2), ("second", 1), ("add", 3), ("second", 0),
    ("second", 2), ("cross", 0), ("second", 3), ("gather", 0), ("gather", 1),
)
HELD = (0,)
COST = {
    "place": 10**10, "pack": 10**10, "rest": 1, "first": 1, "prep": 1, "turn": 1,
    "add": 10**9, "release": 1, "pair": 1, "second": 10**10, "down": 1, "gather": 1, "finish": 1,
}
MIB = 1 << 20
BF16, F32 = jnp.bfloat16, jnp.float32
TRANSPOSED = (((1,), (1,)), ((), ()))
BY_ROWS = (((0,), (0,)), ((), ()))


VMEM, HBM, ANY = (
    pl.BlockSpec(memory_space=space) for space in (pltpu.VMEM, pltpu.HBM, pl.ANY)
)


def call(body, name, operands, specs, outs, out_specs, vmem=16, scratch=(), after=()):
    count, waits = len(operands), len(after)

    def run(*refs):
        body(*refs[:count], *refs[count + waits :])

    return pl.pallas_call(
        run,
        name=name,
        out_shape=outs,
        in_specs=list(specs) + [ANY] * waits,
        out_specs=out_specs,
        scratch_shapes=scratch,
        compiler_params=pltpu.CompilerParams(vmem_limit_bytes=vmem * MIB),
        cost_estimate=pl.CostEstimate(flops=COST[name], bytes_accessed=0, transcendentals=0),
    )(*operands, *after)


def in_hbm(array):
    return pltpu.with_memory_space_constraint(array, pltpu.HBM)


def swish_parts(pre, width):
    gate, up = pre[:, :width].astype(F32), pre[:, width:].astype(F32)
    sigmoid = jax.nn.sigmoid(gate)
    return gate, up, sigmoid


def tiles(size):
    step = 256 if size % 256 == 0 else size
    return [slice(i, i + step) for i in range(0, size, step)]


def arrays_of(blocks):
    found = []
    for array, _ in blocks:
        if not any(array is other for other in found):
            found.append(array)
    return found


def spots_of(blocks, arrays):
    return [(next(i for i, x in enumerate(arrays) if x is array), row) for array, row in blocks]


def rows_at(refs, spots, cap):
    return jnp.concatenate([refs[i][row : row + cap] for i, row in spots], axis=0)


def place_body(groups, cap, ids, place, ids_in, sems):
    bring = pltpu.make_async_copy(ids, ids_in, sems.at[0])
    bring.start()
    rows, slots, lines = ids.shape[1], groups * cap, max(8, groups)
    line = lax.broadcasted_iota(jnp.int32, (lines, rows), 0)
    sooner = lax.broadcasted_iota(jnp.int32, (rows, rows), 0)
    later = lax.broadcasted_iota(jnp.int32, (rows, rows), 1)
    before = jnp.where(sooner < later, 1.0, 0.0).astype(BF16)
    bring.wait()
    route = ids_in[...]
    onehot = jnp.where(line == route, 1.0, 0.0)
    earlier = jnp.dot(onehot.astype(BF16), before, preferred_element_type=F32)
    rank = jnp.sum(earlier * onehot, axis=0, keepdims=True).astype(jnp.int32)
    position = (route ^ lax.axis_index("expert")) * cap + rank
    slot = lax.broadcasted_iota(jnp.int32, (slots, rows), 0)
    place[...] = jnp.where(slot == position, 1.0, 0.0).astype(BF16)


def find_place(ids, groups, cap):
    rows = ids.shape[0]
    return call(
        functools.partial(place_body, groups, cap),
        "place",
        (in_hbm(ids.T),),
        (HBM,),
        [jax.ShapeDtypeStruct((groups * cap, rows), BF16)],
        [VMEM],
        16,
        [pltpu.VMEM((1, rows), jnp.int32), pltpu.SemaphoreType.DMA((1,))],
    )[0]


def put_blocks(place, rows, outs, groups, cap):
    chosen = rows_at([place], [(0, k * cap) for group in groups for k in group], cap)
    for part in tiles(rows.shape[1]):
        packed = jnp.dot(chosen, rows[:, part], preferred_element_type=F32).astype(BF16)
        start = 0
        for group, out in zip(groups, outs):
            out[:, part] = packed[start : start + len(group) * cap]
            start += len(group) * cap


def pack_body(groups, cap, place, scales, values, scaled, *outs):
    features, count = values.shape[1], scales.shape[0]
    owner = lax.broadcasted_iota(jnp.int32, (count, features), 1) // (features // count)
    spread = jnp.where(owner == lax.broadcasted_iota(jnp.int32, (count, features), 0), 1.0, 0.0)
    spread = spread.astype(BF16)
    for part in tiles(features):
        factor = lax.dot_general(
            scales[...], spread[:, part], BY_ROWS, preferred_element_type=F32
        )
        scaled[:, part] = (values[:, part].astype(F32) * factor).astype(BF16)
    put_blocks(place, scaled, outs, groups, cap)


def rest_body(groups, cap, place, scaled, *outs):
    put_blocks(place, scaled, outs, groups, cap)


def pack(place, values, scales, groups, cap):
    rows, features = values.shape
    return call(
        functools.partial(pack_body, groups, cap),
        "pack",
        (place, scales.T, values),
        [VMEM] * 3,
        [jax.ShapeDtypeStruct((rows, features), BF16)]
        + [jax.ShapeDtypeStruct((len(group) * cap, features), BF16) for group in groups],
        [VMEM] * (1 + len(groups)),
    )


def pack_rest(place, scaled, groups, cap, after):
    features = scaled.shape[1]
    return call(
        functools.partial(rest_body, groups, cap),
        "rest",
        (place, scaled),
        [VMEM] * 2,
        [jax.ShapeDtypeStruct((len(group) * cap, features), BF16) for group in groups],
        [VMEM] * len(groups),
        after=after,
    )


def pair_body(count, spots, cap, *refs):
    refs[count][...] = rows_at(refs[:count], spots, cap)


def pair(blocks, cap, after):
    arrays = arrays_of(blocks)
    shape = jax.ShapeDtypeStruct((len(blocks) * cap, arrays[0].shape[1]), BF16)
    return call(
        functools.partial(pair_body, len(arrays), spots_of(blocks, arrays), cap),
        "pair",
        arrays,
        [VMEM] * len(arrays),
        [shape],
        [VMEM],
        after=after,
    )[0]


def first_body(count, spots, cap, weight, *refs):
    arrays, send, keep, both = refs[:count], *refs[count:]
    rows = rows_at(arrays, spots, cap)
    width = weight.shape[1]
    for part in tiles(width):
        both[:, part] = jnp.dot(rows, weight[:, part], preferred_element_type=F32)
    halves = [slice(0, width // 2), slice(width // 2, width)]
    for odd, (theirs, mine) in enumerate((reversed(halves), halves)):

        @pl.when(lax.axis_index("dp") % 2 == odd)
        def _():
            send[...] = both[:, theirs].astype(BF16)
            keep[...] = both[:, mine]


def first(blocks, weight, cap, after):
    arrays = arrays_of(blocks)
    features, width = weight.shape
    size = len(blocks) * cap
    return call(
        functools.partial(first_body, len(arrays), spots_of(blocks, arrays), cap),
        "first",
        (weight, *arrays),
        [VMEM] * (1 + len(arrays)),
        [jax.ShapeDtypeStruct((size, width // 2), dtype) for dtype in (BF16, F32)],
        [VMEM] * 2,
        16,
        [pltpu.VMEM((size, width), F32)],
        after=after,
    )


def add_body(count, keep, *refs):
    total = keep[...]
    for got in refs[:count]:
        total = total + got[...].astype(F32)
    refs[count][...] = total.astype(BF16)


def add(keep, gots, after):
    return call(
        functools.partial(add_body, len(gots)),
        "add",
        (keep, *gots),
        [VMEM] * (1 + len(gots)),
        [jax.ShapeDtypeStruct(keep.shape, BF16)],
        [VMEM],
        16,
        after=after,
    )[0]


def release_body(total, out):
    out[...] = total[...]


def release(total, after):
    shape = jax.ShapeDtypeStruct(total.shape, total.dtype)
    return call(release_body, "release", (total,), [VMEM], [shape], [VMEM], after=after)[0]


def prep_body(saved, gate_factor, up_factor, hidden):
    slots, width = hidden.shape
    step = 32 if slots % 32 == 0 else slots

    def some(i, carry):
        at = pl.ds(pl.multiple_of(i * step, step), step)
        gate, up, sigmoid = swish_parts(saved[at, :], width)
        silu = gate * sigmoid
        gate_factor[at, :] = up * sigmoid * (1.0 + gate * (1.0 - sigmoid))
        up_factor[at, :] = silu
        hidden[at, :] = (silu * up).astype(BF16)
        return carry

    lax.fori_loop(0, slots // step, some, 0)


def prep(saved_pre, after):
    slots, width = saved_pre.shape[0], saved_pre.shape[1] // 2
    return call(
        prep_body,
        "prep",
        (saved_pre,),
        [VMEM],
        [jax.ShapeDtypeStruct((slots, width), dtype) for dtype in (F32, F32, BF16)],
        [VMEM] * 3,
        16,
        after=after,
    )


def turn_body(count, cap, groups, place, *refs):
    weights, turned, places = refs[:count], refs[count : 2 * count], refs[2 * count :]
    for weight, out in zip(weights, turned):
        for part in tiles(weight.shape[0]):
            out[:, part] = weight[part, :].T
    for group, out in zip(groups, places):
        out[...] = rows_at([place], [(0, k * cap) for k in group], cap).T


def turn(weights, place, groups, cap, after):
    count, rows = len(weights), place.shape[1]
    return call(
        functools.partial(turn_body, count, cap, groups),
        "turn",
        (place, *weights),
        [VMEM] * (1 + count),
        [jax.ShapeDtypeStruct(x.shape[::-1], x.dtype) for x in weights]
        + [jax.ShapeDtypeStruct((rows, len(group) * cap), BF16) for group in groups],
        [VMEM] * (count + len(groups)),
        16,
        after=after,
    )


def slots_of(ref, k, cap):
    start = pl.multiple_of((lax.axis_index("expert") ^ k) * cap, cap)
    return ref[pl.ds(start, cap), :]


def second_body(chunk, cap, own, other, gate_factor, up_factor, w_gate, w_up, *refs):
    outs, grads = refs[:-1], refs[-1]
    width, features = w_gate.shape
    halves = [slice(0, width // 2), slice(width // 2, width)]
    for odd, (theirs, mine) in enumerate((reversed(halves), halves)):

        @pl.when(lax.axis_index("dp") % 2 == odd)
        def _():
            grads[:, mine] = own[...]
            grads[:, theirs] = other[...]

    grad = grads[...].astype(F32)
    d_gate, d_up = (
        (grad * jnp.concatenate([slots_of(factor, k, cap) for k in chunk], axis=0))
        .astype(BF16)
        for factor in (gate_factor, up_factor)
    )
    for part in tiles(features):
        result = jnp.dot(d_gate, w_gate[:, part], preferred_element_type=F32)
        result += jnp.dot(d_up, w_up[:, part], preferred_element_type=F32)
        result = result.astype(BF16)
        size = result.shape[0] // len(outs)
        for i, out in enumerate(outs):
            out[:, part] = result[i * size : (i + 1) * size]


def second(own, other, factors, weights, chunk, cap, together, after):
    width, features = weights[0].shape
    count = 1 if together else len(chunk)
    size = len(chunk) // count * cap
    return call(
        functools.partial(second_body, chunk, cap),
        "second",
        (own, other, *factors, *weights),
        [VMEM] * 6,
        [jax.ShapeDtypeStruct((size, features), BF16)] * count,
        [VMEM] * count,
        24,
        [pltpu.VMEM((len(chunk) * cap, width), BF16)],
        after=after,
    )


def down_body(count, spots, hidden, *refs):
    arrays, out, flag, sums, sems = refs[:count], *refs[count:]
    flag[...] = jnp.zeros_like(flag)
    cap = hidden.shape[0] // len(spots)
    features, width = out.shape
    mine = jnp.concatenate([slots_of(hidden, k, cap) for k in range(len(spots))], axis=0)
    tile = sums.shape[1]
    copies = []
    for i in range(features // tile):
        part = [arrays[a][row : row + cap, i * tile : (i + 1) * tile] for a, row in spots]
        part = jnp.concatenate(part, axis=0)
        sums[i] = lax.dot_general(part, mine, BY_ROWS, preferred_element_type=F32)
        copies.append(
            pltpu.make_async_copy(sums.at[i], out.at[pl.ds(i * tile, tile)], sems.at[i])
        )
        copies[-1].start()
    for copy in copies:
        copy.wait()


def down(blocks, hidden, features, after):
    arrays = arrays_of(blocks)
    slots, width = hidden.shape
    tile = min(features, 256)
    steps = features // tile
    return call(
        functools.partial(down_body, len(arrays), spots_of(blocks, arrays)),
        "down",
        (hidden, *arrays),
        [VMEM] * (1 + len(arrays)),
        [jax.ShapeDtypeStruct((features, width), F32), jax.ShapeDtypeStruct((8, 128), F32)],
        [HBM, VMEM],
        24,
        [pltpu.VMEM((steps, tile, width), F32), pltpu.SemaphoreType.DMA((steps,))],
        after=after,
    )


def rows_of(place, arrays, spots, cap, part):
    returned = [arrays[i][row : row + cap, part] for i, row in spots]
    returned = jnp.concatenate(returned, axis=0)
    return jnp.dot(place[...], returned, preferred_element_type=F32).astype(BF16)


def gather_body(count, spots, cap, place, *refs):
    arrays, sooner, out = refs[:count], refs[count:-1], refs[-1]
    for part in tiles(out.shape[1]):
        rows = rows_of(place, arrays, spots, cap, part)
        for others in sooner:
            rows += others[:, part]
        out[:, part] = rows


def gather(place, blocks, cap, sooner, after):
    arrays = arrays_of(blocks)
    rows, features = place.shape[0], arrays[0].shape[1]
    return call(
        functools.partial(gather_body, len(arrays), spots_of(blocks, arrays), cap),
        "gather",
        (place, *arrays, *sooner),
        [VMEM] * (1 + len(arrays) + len(sooner)),
        [jax.ShapeDtypeStruct((rows, features), BF16)],
        [VMEM],
        16,
        after=after,
    )[0]


def finish_body(count, spots, cap, place, sooner, *refs):
    arrays, out, whole, sems = refs[:count], *refs[count:]
    copies = []
    for i, part in enumerate(tiles(out.shape[1])):
        whole[:, part] = rows_of(place, arrays, spots, cap, part) + sooner[:, part]
        copies.append(pltpu.make_async_copy(whole.at[:, part], out.at[:, part], sems.at[i]))
        copies[-1].start()
    for copy in copies:
        copy.wait()


def finish(place, blocks, cap, sooner, after):
    arrays, (rows, features) = arrays_of(blocks), sooner.shape
    return call(
        functools.partial(finish_body, len(arrays), spots_of(blocks, arrays), cap),
        "finish",
        (place, sooner, *arrays),
        [VMEM] * (2 + len(arrays)),
        [jax.ShapeDtypeStruct((rows, features), BF16)],
        [HBM],
        16,
        [
            pltpu.VMEM((rows, features), BF16),
            pltpu.SemaphoreType.DMA((len(tiles(features)),)),
        ],
        after=after,
    )[0]


def swap(block, axis, k):
    size = lax.axis_size(axis)
    return lax.ppermute(block, axis, [(i, i ^ k) for i in range(size)])


def near_device(dy_values, dy_scales, expert_ids, saved_pre, w_gate, w_up, w_down):
    groups = lax.axis_size("expert")
    cap = saved_pre.shape[0] // groups
    features = dy_values.shape[1]
    keeps, gots, owns, others, returned, result = {}, {}, {}, {}, {}, {}

    place = find_place(expert_ids, groups, cap)
    last, sooner = [place], []
    scaled, crossing, ahead = pack(place, dy_values, dy_scales, ((1, 7), (6,)), cap)
    side = swap(crossing, "expert", 1)
    rest = pack_rest(place, scaled, [(k,) for k in LATER], cap, [crossing])
    last[:] = rest[-1:]
    blocks = {1: (side, 0)}
    for k, block in zip(LATER, rest):
        blocks[k] = (swap(block, "expert", k) if k else block, 0)

    def do_diagonal(_):
        both = pair([(ahead, 0), (side, cap)], cap, last)
        last[:] = [both]
        got = swap(both, "expert", 6)
        blocks.update({6: (got, 0), 7: (got, cap)})

    def do_first(c):
        send, keeps[c] = first([blocks[k] for k in CHUNKS[c]], w_down[0], cap, last)
        last[:] = [send]
        gots[c] = [swap(send, "dp", 1)]

    def do_add(c):
        part = add(keeps[c], gots[c], last)
        last[:] = [part]
        if len(gots[c]) == 1:
            gots[c].append(swap(part, "dp", 2))
        elif c in HELD:
            owns[c] = part
        else:
            owns[c], others[c] = part, swap(part, "dp", 1)

    def do_release(c):
        owns[c] = release(owns[c], last)
        last[:] = [owns[c]]
        others[c] = swap(owns[c], "dp", 1)

    def do_prep(_):
        *result["factors"], result["hidden"] = prep(saved_pre, last)
        last[:] = [result["hidden"]]

    def do_turn(_):
        turned = turn((w_gate[0], w_up[0]), place, PARTS, cap, last)
        result["weights"], result["places"] = turned[:2], turned[2:]
        last[:] = turned[:1]

    def do_second(c):
        chunk = CHUNKS[c]
        grads = second(
            owns[c], others[c], result["factors"], result["weights"], chunk, cap, 6 in chunk, last
        )
        last[:] = [grads[0]]
        if 6 in chunk:
            result["back"] = swap(grads[0], "expert", 6)
            returned[6] = (result["back"], 0)
        elif 0 in chunk:
            returned[0], result["near"] = (grads[0], 0), grads[1]
        else:
            returned.update({k: (swap(grad, "expert", k), 0) for k, grad in zip(chunk, grads)})

    def do_cross(_):
        both = pair([(result["near"], 0), (result["back"], cap)], cap, last)
        last[:] = [both]
        got = swap(both, "expert", 1)
        returned.update({1: (got, 0), 7: (got, cap)})

    def do_down(_):
        every = [blocks[k] for k in range(groups)]
        result["down"], flag = down(every, result["hidden"], features, last)
        last[:] = [flag]

    def do_gather(part):
        came = [returned[k] for k in PARTS[part]]
        sooner[:] = [gather(result["places"][part], came, cap, sooner, last)]
        last[:] = sooner

    steps = {
        "first": do_first,
        "add": do_add,
        "release": do_release,
        "diagonal": do_diagonal,
        "cross": do_cross,
        "prep": do_prep,
        "turn": do_turn,
        "second": do_second,
        "down": do_down,
        "gather": do_gather,
    }
    for step, c in ORDER:
        steps[step](c)
    came = [returned[k] for k in PARTS[-1]]
    grad_input = finish(result["places"][-1], came, cap, sooner[0], last)
    return (grad_input, result["down"][None])


def far_device(dy_values, dy_scales, expert_ids, saved_pre, w_gate, w_up, w_down):
    groups, width = lax.axis_size("expert"), w_down.shape[2]
    slots = saved_pre.shape[0]
    cap = slots // groups
    route = expert_ids[:, 0]
    rows, count = route.shape[0], dy_scales.shape[1]
    onehot = (route[:, None] == jnp.arange(groups, dtype=jnp.int32)[None, :]).astype(BF16)
    earlier = jnp.dot(jnp.tri(rows, k=-1, dtype=BF16), onehot, preferred_element_type=F32)
    rank = jnp.sum(earlier * onehot.astype(F32), axis=1).astype(jnp.int32)
    place = route * cap + rank
    chosen = (place[:, None] == jnp.arange(slots, dtype=jnp.int32)[None, :]).astype(BF16)
    scaled = dy_values.astype(F32).reshape(rows, count, -1) * dy_scales.astype(F32)[:, :, None]
    scaled = scaled.reshape(dy_values.shape).astype(BF16)
    packed = lax.dot_general(chosen, scaled, BY_ROWS, preferred_element_type=F32).astype(BF16)
    received = lax.all_to_all(packed, "expert", split_axis=0, concat_axis=0, tiled=True)
    gate, up, sigmoid = swish_parts(saved_pre, width)
    hidden = (gate * sigmoid * up).astype(BF16)
    partial = jnp.dot(received, w_down[0], preferred_element_type=F32)
    grad = lax.psum(partial, "dp")
    d_gate = (grad * up * sigmoid * (1.0 + gate * (1.0 - sigmoid))).astype(BF16)
    d_up = (grad * (gate * sigmoid)).astype(BF16)
    result = lax.dot_general(d_gate, w_gate[0], TRANSPOSED, preferred_element_type=F32)
    result += lax.dot_general(d_up, w_up[0], TRANSPOSED, preferred_element_type=F32)
    returned = lax.all_to_all(
        result.astype(BF16), "expert", split_axis=0, concat_axis=0, tiled=True
    )
    grad_input = jnp.dot(chosen, returned, preferred_element_type=F32).astype(BF16)
    grad_down = lax.dot_general(received, hidden, BY_ROWS, preferred_element_type=F32)
    return (grad_input, grad_down[None])


def solution(mesh):
    near = mesh.shape["expert"] == 8 and mesh.shape["dp"] == 4
    return jax.shard_map(
        near_device if near else far_device,
        mesh=mesh,
        in_specs=(
            P("expert", "dp"),
            P("expert", "dp"),
            P("expert", None),
            P("expert", None),
            P("expert", "dp", None),
            P("expert", "dp", None),
            P("expert", "dp", None),
        ),
        out_specs=(P("expert", "dp"), P("expert", "dp", None)),
        check_vma=False,
    )
```

time: 65.6 us -> 60.1 us (0.916)
  Pallas kernels: 18.4 us -> 13.5 us
  starting transfers between devices: 30.3 us -> 33.6 us
  waiting for transfers between devices: 15.1 us -> 11.9 us
  other arithmetic: 0.76 us -> 0 us
    pallas_call x22 -> x28, Pallas kernels: 18.4 us -> 13.5 us  [call(): pl.pallas_call(run, name=name, out_shape=outs, in_specs=list(specs) + [AN...]
    ppermute x23 -> x24, starting transfers between devices: 30.3 us -> 33.6 us  [swap(): return lax.ppermute(block, axis, [(i, i ^ k) for i in range(size)])]
    ppermute x23 -> x24, waiting for transfers between devices: 15.1 us -> 11.9 us  [swap(): return lax.ppermute(block, axis, [(i, i ^ k) for i in range(size)])]
    convert_element_type x1 -> x0, other arithmetic: 0.69 us -> none  [pack(): scales.T.astype(F32)]
  transfers between devices with their start and end apart: 23 -> 24, of which waited for: 11 -> 12; matrix products, arithmetic and copies ran while one was open for 0% -> 0% of each run, Pallas kernels for 22% -> 18%
where the time goes in v2:
time: 60.1 us; the launch traced here: 59.9 us
  starting transfers between devices  33.6 us (56%)
  Pallas kernels  13.5 us (22%)
  waiting for transfers between devices  11.9 us (20%)
  between operations  0.89 us (1%)
    ppermute x24, starting transfers between devices, swap(): return lax.ppermute(block, axis, [(i, i ^ k) for i in range(size)])  33.6 us
    pallas_call x28, Pallas kernels, call(): pl.pallas_call(run, name=name, out_shape=outs, in_specs=list(specs) + [AN...  13.5 us
    ppermute x24, waiting for transfers between devices, swap(): return lax.ppermute(block, axis, [(i, i ^ k) for i in range(size)])  11.9 us
  transfers between devices with their start and end apart: 24, of which 12 were waited for; matrix products, arithmetic and copies ran while one was open for 0% of the time, Pallas kernels for 18%

profile of v2, /device:TPU:0, one launch (start us, length us, event | category | flops | bytes accessed | tf_op | source)
XLA Modules:
  0.0 59.9 jit_solution(10215528947057757207)
XLA Ops:
  0.6 1.0 %place.1.refs_0_ = bf16[512,256]{1,0:T(8,128)(2,1)S(1)} custom-call(s32[1,256]{1,0:T(1,128)} %bitcast.14), custom_call_target="tpu_custom_call" | custom-call | flops 10000000000 | tf_op jit(solution)/shard_map/place/pallas_call | solution.py:41
  1.7 0.5 pack.1
  2.2 0.5 collective-permute-start
  2.7 0.3 rest.1
  3.1 0.8 %collective-permute-done.refs_2_.refs_1_ = bf16[128,1024]{1,0:T(8,128)(2,1)S(1)} collective-permute-done((bf16[128,1024]{1,0:T(8,128)(2,1)S(1)}, bf16[128,1024]{1,0:T(8,128)(2,1)S(1)}, u32[]{:S(2)}, u32[]{:S(2)}) %collective-permute-start) | collective-permute-done | bytes 262176 | tf_op jit(solution)/shard_map/ppermute | solution.py:449
  3.9 0.5 first.4
  4.4 3.0 %collective-permute-start.1 = (bf16[128,512]{1,0:T(8,128)(2,1)S(1)}, bf16[128,512]{1,0:T(8,128)(2,1)S(1)}, u32[]{:S(2)}, u32[]{:S(2)}) collective-permute-start(bf16[128,512]{1,0:T(8,128)(2,1)S(1)} %get-tuple-element.38.refs_2_), channel_id=1, source_target_pairs={{0,1},{1,0},{2,3},{3,2},{4,5},{5,4},{6,7},{7,6},{8,9},{9,8},{10,11... | collective-permute-start | bytes 393224 | tf_op jit(solution)/shard_map/ppermute | solution.py:449
  7.4 2.5 %collective-permute-start.5 = (bf16[128,1024]{1,0:T(8,128)(2,1)S(1)}, bf16[128,1024]{1,0:T(8,128)(2,1)S(1)}, u32[]{:S(2)}, u32[]{:S(2)}) collective-permute-start(bf16[128,1024]{1,0:T(8,128)(2,1)S(1)} %pair.2.refs_2_), channel_id=1, source_target_pairs={{0,24},{4,28},{8,16},{12,20},{16,8},{20,12},{24,0},{28,4},{1,25},{... | collective-permute-start | bytes 786440 | tf_op jit(solution)/shard_map/ppermute | solution.py:449
  9.9 0.5 collective-permute-start.3
  10.5 0.5 collective-permute-start.4
  11.0 0.2 collective-permute-done.1.refs_1_
  11.2 2.8 %collective-permute-start.2 = (bf16[128,512]{1,0:T(8,128)(2,1)S(1)}, bf16[128,512]{1,0:T(8,128)(2,1)S(1)}, u32[]{:S(2)}, u32[]{:S(2)}) collective-permute-start(bf16[128,512]{1,0:T(8,128)(2,1)S(1)} %add.8.refs_1_), channel_id=1, source_target_pairs={{0,2},{1,3},{2,0},{3,1},{4,6},{5,7},{6,4},{7,5},{8,10},{9,11},{10,... | collective-permute-start | bytes 393224 | tf_op jit(solution)/shard_map/ppermute | solution.py:449
  14.0 1.0 %prep.1 = (f32[512,1024]{1,0:T(8,128)S(1)}, f32[512,1024]{1,0:T(8,128)S(1)}, bf16[512,1024]{1,0:T(8,128)(2,1)S(1)}) custom-call(bf16[512,2048]{1,0:T(8,128)(2,1)S(1)} %copy-done.1, bf16[128,512]{1,0:T(8,128)(2,1)S(1)} %add.8.refs_1_), custom_call_target="tpu_custom_call" | custom-call | flops 1 | tf_op jit(solution)/shard_map/prep/pallas_call | solution.py:41
  15.1 1.3 %turn.1 = (bf16[1024,1024]{1,0:T(8,128)(2,1)S(1)}, bf16[1024,1024]{1,0:T(8,128)(2,1)S(1)}, bf16[256,128]{1,0:T(8,128)(2,1)S(1)}, bf16[256,256]{1,0:T(8,128)(2,1)S(1)}, bf16[256,128]{1,0:T(8,128)(2,1)S(1)}) custom-call(bf16[512,256]{1,0:T(8,128)(2,1)S(1)} %place.1.refs_0_, bf16[1024,1024]{1,0:T(8,128)(2,1)S(1)} %bitcast.10, bf16[1024,1024]{1,0:T(8,128)(2,1)S(1)} %bitcast.11, ...), custom_call_target="tpu_custom_call" | custom-call | flops 1 | tf_op jit(solution)/shard_map/turn/pallas_call | solution.py:41
  16.4 1.2 %collective-permute-done.5.refs_1_.refs_7_ = bf16[128,1024]{1,0:T(8,128)(2,1)S(1)} collective-permute-done((bf16[128,1024]{1,0:T(8,128)(2,1)S(1)}, bf16[128,1024]{1,0:T(8,128)(2,1)S(1)}, u32[]{:S(2)}, u32[]{:S(2)}) %collective-permute-start.5) | collective-permute-done | bytes 262176 | tf_op jit(solution)/shard_map/ppermute | solution.py:449
  17.6 0.5 first.5
  18.1 0.5 collective-permute-start.8
  18.6 0.8 %collective-permute-done.3.refs_1_.refs_3_ = bf16[64,1024]{1,0:T(8,128)(2,1)S(1)} collective-permute-done((bf16[64,1024]{1,0:T(8,128)(2,1)S(1)}, bf16[64,1024]{1,0:T(8,128)(2,1)S(1)}, u32[]{:S(2)}, u32[]{:S(2)}) %collective-permute-start.3) | collective-permute-done | bytes 131104 | tf_op jit(solution)/shard_map/ppermute | solution.py:449
  19.4 2.0 %collective-permute-start.7 = (bf16[64,1024]{1,0:T(8,128)(2,1)S(1)}, bf16[64,1024]{1,0:T(8,128)(2,1)S(1)}, u32[]{:S(2)}, u32[]{:S(2)}) collective-permute-start(bf16[64,1024]{1,0:T(8,128)(2,1)S(1)} %get-tuple-element.49), channel_id=1, source_target_pairs={{0,20},{4,16},{8,28},{12,24},{16,4},{20,0},{24,12},{28,8},{1,21},{... | collective-permute-start | bytes 393224 | tf_op jit(solution)/shard_map/ppermute | solution.py:449
  21.4 0.5 first.6
  21.8 1.6 %collective-permute-start.11 = (bf16[128,512]{1,0:T(8,128)(2,1)S(1)}, bf16[128,512]{1,0:T(8,128)(2,1)S(1)}, u32[]{:S(2)}, u32[]{:S(2)}) collective-permute-start(bf16[128,512]{1,0:T(8,128)(2,1)S(1)} %get-tuple-element.47.refs_3_), channel_id=1, source_target_pairs={{0,1},{1,0},{2,3},{3,2},{4,5},{5,4},{6,7},{7,6},{8,9},{9,8},{10,11... | collective-permute-start | bytes 393224 | tf_op jit(solution)/shard_map/ppermute | solution.py:449
  23.6 2.7 %collective-permute-start.10 = (bf16[128,512]{1,0:T(8,128)(2,1)S(1)}, bf16[128,512]{1,0:T(8,128)(2,1)S(1)}, u32[]{:S(2)}, u32[]{:S(2)}) collective-permute-start(bf16[128,512]{1,0:T(8,128)(2,1)S(1)} %add.10.refs_3_), channel_id=1, source_target_pairs={{0,2},{1,3},{2,0},{3,1},{4,6},{5,7},{6,4},{7,5},{8,10},{9,11},{10,... | collective-permute-start | bytes 393224 | tf_op jit(solution)/shard_map/ppermute | solution.py:449
  26.3 0.5 first.7
  26.7 0.6 %collective-permute-start.9 = (bf16[128,512]{1,0:T(8,128)(2,1)S(1)}, bf16[128,512]{1,0:T(8,128)(2,1)S(1)}, u32[]{:S(2)}, u32[]{:S(2)}) collective-permute-start(bf16[128,512]{1,0:T(8,128)(2,1)S(1)} %get-tuple-element.52.refs_2_), channel_id=1, source_target_pairs={{0,1},{1,0},{2,3},{3,2},{4,5},{5,4},{6,7},{7,6},{8,9},{9,8},{10,11... | collective-permute-start | bytes 393224 | tf_op jit(solution)/shard_map/ppermute | solution.py:449
  27.4 0.8 %collective-permute-done.11.refs_1_ = bf16[128,512]{1,0:T(8,128)(2,1)S(1)} collective-permute-done((bf16[128,512]{1,0:T(8,128)(2,1)S(1)}, bf16[128,512]{1,0:T(8,128)(2,1)S(1)}, u32[]{:S(2)}, u32[]{:S(2)}) %collective-permute-start.11) | collective-permute-done | bytes 131104 | tf_op jit(solution)/shard_map/ppermute | solution.py:449
  28.2 2.1 %collective-permute-start.15 = (bf16[128,512]{1,0:T(8,128)(2,1)S(1)}, bf16[128,512]{1,0:T(8,128)(2,1)S(1)}, u32[]{:S(2)}, u32[]{:S(2)}) collective-permute-start(bf16[128,512]{1,0:T(8,128)(2,1)S(1)} %add.11.refs_3_), channel_id=1, source_target_pairs={{0,2},{1,3},{2,0},{3,1},{4,6},{5,7},{6,4},{7,5},{8,10},{9,11},{10,... | collective-permute-start | bytes 393224 | tf_op jit(solution)/shard_map/ppermute | solution.py:449
  30.3 1.5 %collective-permute-done.10.refs_2_ = bf16[128,512]{1,0:T(8,128)(2,1)S(1)} collective-permute-done((bf16[128,512]{1,0:T(8,128)(2,1)S(1)}, bf16[128,512]{1,0:T(8,128)(2,1)S(1)}, u32[]{:S(2)}, u32[]{:S(2)}) %collective-permute-start.10) | collective-permute-done | bytes 131104 | tf_op jit(solution)/shard_map/ppermute | solution.py:449
  31.8 1.1 %collective-permute-start.14 = (bf16[128,512]{1,0:T(8,128)(2,1)S(1)}, bf16[128,512]{1,0:T(8,128)(2,1)S(1)}, u32[]{:S(2)}, u32[]{:S(2)}) collective-permute-start(bf16[128,512]{1,0:T(8,128)(2,1)S(1)} %add.12.refs_8_.refs_0_), channel_id=1, source_target_pairs={{0,1},{1,0},{2,3},{3,2},{4,5},{5,4},{6,7},{7,6},{8,9},{9,8},{10,11... | collective-permute-start | bytes 393224 | tf_op jit(solution)/shard_map/ppermute | solution.py:449
  32.9 2.5 %down.1 = (f32[1024,1024]{1,0:T(8,128)}, f32[8,128]{1,0:T(8,128)S(1)}) custom-call(bf16[512,1024]{1,0:T(8,128)(2,1)S(1)} %get-tuple-element.40.refs_3_.refs_0_, bf16[64,1024]{1,0:T(8,128)(2,1)S(1)} %get-tuple-element.36.refs_1_.refs_3_, bf16[128,1024]{1,0:T(8,128)(2,1)S(1)} %collective-permute-done.refs_2_.refs_1_, ...), custom_call_target="tpu_custom_call" | custom-call | flops 1 | tf_op jit(solution)/shard_map/down/pallas_call | solution.py:41
  35.5 0.6 collective-permute-done.9.refs_1_
  36.1 3.4 %collective-permute-start.13 = (bf16[128,512]{1,0:T(8,128)(2,1)S(1)}, bf16[128,512]{1,0:T(8,128)(2,1)S(1)}, u32[]{:S(2)}, u32[]{:S(2)}) collective-permute-start(bf16[128,512]{1,0:T(8,128)(2,1)S(1)} %add.13.refs_1_), channel_id=1, source_target_pairs={{0,2},{1,3},{2,0},{3,1},{4,6},{5,7},{6,4},{7,5},{8,10},{9,11},{10,... | collective-permute-start | bytes 393224 | tf_op jit(solution)/shard_map/ppermute | solution.py:449
  39.5 2.1 %collective-permute-start.17 = (bf16[128,512]{1,0:T(8,128)(2,1)S(1)}, bf16[128,512]{1,0:T(8,128)(2,1)S(1)}, u32[]{:S(2)}, u32[]{:S(2)}) collective-permute-start(bf16[128,512]{1,0:T(8,128)(2,1)S(1)} %add.14.refs_6_.refs_0_), channel_id=1, source_target_pairs={{0,1},{1,0},{2,3},{3,2},{4,5},{5,4},{6,7},{7,6},{8,9},{9,8},{10,11... | collective-permute-start | bytes 393224 | tf_op jit(solution)/shard_map/ppermute | solution.py:449
  41.6 0.7 %second.4.refs_3_ = bf16[128,1024]{1,0:T(8,128)(2,1)S(1)} custom-call(bf16[128,512]{1,0:T(8,128)(2,1)S(1)} %add.12.refs_8_.refs_0_, bf16[128,512]{1,0:T(8,128)(2,1)S(1)} %collective-permute-done.14.refs_1_, f32[512,1024]{1,0:T(8,128)S(1)} %get-tuple-element.55.refs_2_, f32[512,1024]{1,0:T(8,128)S(1)} %get-tuple-element.56.refs_3_, ...), custom_call_target="tpu_custom_call" | custom-call | flops 10000000000 | tf_op jit(solution)/shard_map/second/pallas_call | solution.py:41
  42.4 2.7 %collective-permute-start.16 = (bf16[128,1024]{1,0:T(8,128)(2,1)S(1)}, bf16[128,1024]{1,0:T(8,128)(2,1)S(1)}, u32[]{:S(2)}, u32[]{:S(2)}) collective-permute-start(bf16[128,1024]{1,0:T(8,128)(2,1)S(1)} %second.4.refs_3_), channel_id=1, source_target_pairs={{0,24},{4,28},{8,16},{12,20},{16,8},{20,12},{24,0},{28,4},{1,25},{... | collective-permute-start | bytes 786440 | tf_op jit(solution)/shard_map/ppermute | solution.py:449
  45.3 1.1 %collective-permute-done.12.refs_1_ = bf16[128,512]{1,0:T(8,128)(2,1)S(1)} collective-permute-done((bf16[128,512]{1,0:T(8,128)(2,1)S(1)}, bf16[128,512]{1,0:T(8,128)(2,1)S(1)}, u32[]{:S(2)}, u32[]{:S(2)}) %collective-permute-start.12) | collective-permute-done | bytes 131104 | tf_op jit(solution)/shard_map/ppermute | solution.py:449
  46.4 0.7 %second.5 = (bf16[64,1024]{1,0:T(8,128)(2,1)S(1)}, bf16[64,1024]{1,0:T(8,128)(2,1)S(1)}) custom-call(bf16[128,512]{1,0:T(8,128)(2,1)S(1)} %release.1.refs_3_.refs_0_, bf16[128,512]{1,0:T(8,128)(2,1)S(1)} %collective-permute-done.12.refs_1_, f32[512,1024]{1,0:T(8,128)S(1)} %get-tuple-element.55.refs_2_, f32[512,1024]{1,0:T(8,128)S(1)} %get-tuple-element.56.refs_3_, ...), custom_call_target="tpu_custom_call" | custom-call | flops 10000000000 | tf_op jit(solution)/shard_map/second/pallas_call | solution.py:41
  47.1 0.9 %collective-permute-done.17.refs_1_ = bf16[128,512]{1,0:T(8,128)(2,1)S(1)} collective-permute-done((bf16[128,512]{1,0:T(8,128)(2,1)S(1)}, bf16[128,512]{1,0:T(8,128)(2,1)S(1)}, u32[]{:S(2)}, u32[]{:S(2)}) %collective-permute-start.17) | collective-permute-done | bytes 131104 | tf_op jit(solution)/shard_map/ppermute | solution.py:449
  48.0 0.7 %second.6 = (bf16[64,1024]{1,0:T(8,128)(2,1)S(1)}, bf16[64,1024]{1,0:T(8,128)(2,1)S(1)}) custom-call(bf16[128,512]{1,0:T(8,128)(2,1)S(1)} %add.14.refs_6_.refs_0_, bf16[128,512]{1,0:T(8,128)(2,1)S(1)} %collective-permute-done.17.refs_1_, f32[512,1024]{1,0:T(8,128)S(1)} %get-tuple-element.55.refs_2_, f32[512,1024]{1,0:T(8,128)S(1)} %get-tuple-element.56.refs_3_, ...), custom_call_target="tpu_custom_call" | custom-call | flops 10000000000 | tf_op jit(solution)/shard_map/second/pallas_call | solution.py:41
  48.8 1.5 %collective-permute-start.19 = (bf16[64,1024]{1,0:T(8,128)(2,1)S(1)}, bf16[64,1024]{1,0:T(8,128)(2,1)S(1)}, u32[]{:S(2)}, u32[]{:S(2)}) collective-permute-start(bf16[64,1024]{1,0:T(8,128)(2,1)S(1)} %get-tuple-element.60.refs_2_), channel_id=1, source_target_pairs={{0,8},{4,12},{8,0},{12,4},{16,24},{20,28},{24,16},{28,20},{1,9},{5... | collective-permute-start | bytes 393224 | tf_op jit(solution)/shard_map/ppermute | solution.py:449
  50.3 2.3 %collective-permute-start.20 = (bf16[64,1024]{1,0:T(8,128)(2,1)S(1)}, bf16[64,1024]{1,0:T(8,128)(2,1)S(1)}, u32[]{:S(2)}, u32[]{:S(2)}) collective-permute-start(bf16[64,1024]{1,0:T(8,128)(2,1)S(1)} %get-tuple-element.62), channel_id=1, source_target_pairs={{0,16},{4,20},{8,24},{12,28},{16,0},{20,4},{24,8},{28,12},{1,17},{... | collective-permute-start | bytes 393224 | tf_op jit(solution)/shard_map/ppermute | solution.py:449
  52.7 0.8 %second.7 = (bf16[64,1024]{1,0:T(8,128)(2,1)S(1)}, bf16[64,1024]{1,0:T(8,128)(2,1)S(1)}) custom-call(bf16[128,512]{1,0:T(8,128)(2,1)S(1)} %add.15.refs_6_.refs_0_, bf16[128,512]{1,0:T(8,128)(2,1)S(1)} %collective-permute-done.21.refs_1_, f32[512,1024]{1,0:T(8,128)S(1)} %get-tuple-element.55.refs_2_, f32[512,1024]{1,0:T(8,128)S(1)} %get-tuple-element.56.refs_3_, ...), custom_call_target="tpu_custom_call" | custom-call | flops 10000000000 | tf_op jit(solution)/shard_map/second/pallas_call | solution.py:41
  53.4 0.2 collective-permute-start.22
  53.6 0.7 %collective-permute-start.23 = (bf16[64,1024]{1,0:T(8,128)(2,1)S(1)}, bf16[64,1024]{1,0:T(8,128)(2,1)S(1)}, u32[]{:S(2)}, u32[]{:S(2)}) collective-permute-start(bf16[64,1024]{1,0:T(8,128)(2,1)S(1)} %get-tuple-element.64), channel_id=1, source_target_pairs={{0,20},{4,16},{8,28},{12,24},{16,4},{20,0},{24,12},{28,8},{1,21},{... | collective-permute-start | bytes 393224 | tf_op jit(solution)/shard_map/ppermute | solution.py:449
  54.3 1.2 %collective-permute-done.20.refs_2_ = bf16[64,1024]{1,0:T(8,128)(2,1)S(1)} collective-permute-done((bf16[64,1024]{1,0:T(8,128)(2,1)S(1)}, bf16[64,1024]{1,0:T(8,128)(2,1)S(1)}, u32[]{:S(2)}, u32[]{:S(2)}) %collective-permute-start.20) | collective-permute-done | bytes 131104 | tf_op jit(solution)/shard_map/ppermute | solution.py:449
  55.5 0.3 gather.2.refs_4_.refs_5_
  55.8 0.3 gather.3.refs_1_.refs_4_
  56.1 2.6 %collective-permute-done.22.refs_2_ = bf16[64,1024]{1,0:T(8,128)(2,1)S(1)} collective-permute-done((bf16[64,1024]{1,0:T(8,128)(2,1)S(1)}, bf16[64,1024]{1,0:T(8,128)(2,1)S(1)}, u32[]{:S(2)}, u32[]{:S(2)}) %collective-permute-start.22) | collective-permute-done | bytes 131104 | tf_op jit(solution)/shard_map/ppermute | solution.py:449
  58.9 1.0 %finish.1 = bf16[256,1024]{1,0:T(8,128)(2,1)} custom-call(bf16[256,128]{1,0:T(8,128)(2,1)S(1)} %get-tuple-element.41.refs_0_, bf16[256,1024]{1,0:T(8,128)(2,1)S(1)} %gather.3.refs_1_.refs_4_, bf16[64,1024]{1,0:T(8,128)(2,1)S(1)} %collective-permute-done.22.refs_2_, bf16[64,1024]{1,0:T(8,128)(2,1)S(1)} %collective-permute-done.23.refs_3_, ...), custom_call_target="tpu_custom_call" | custom-call | flops 1 | tf_op jit(solution)/shard_map/finish/pallas_call | solution.py:41
  (40 shorter events, 0.8 us)
Async XLA Ops:
  0.6 1.1 %copy-start.4 = (bf16[256,1024]{1,0:T(8,128)(2,1)S(1)}, bf16[256,1024]{1,0:T(8,128)(2,1)}, u32[]{:S(2)}) copy-start(bf16[256,1024]{1,0:T(8,128)(2,1)} %refs_2_.1) | copy-start | bytes 1572868
  0.6 1.1 %copy-start.5 = (bf16[256,8]{0,1:T(8,128)(2,1)S(1)}, bf16[256,8]{0,1:T(8,128)(2,1)}, u32[]{:S(2)}) copy-start(bf16[256,8]{0,1:T(8,128)(2,1)} %param.8) | copy-start | bytes 12292
  1.7 2.2 %copy-start = (bf16[1,1024,1024]{2,1,0:T(8,128)(2,1)S(1)}, bf16[1,1024,1024]{2,1,0:T(8,128)(2,1)}, u32[]{:S(2)}) copy-start(bf16[1,1024,1024]{2,1,0:T(8,128)(2,1)} %param.13) | copy-start | bytes 6291460
  2.2 1.7 %collective-permute-start = (bf16[128,1024]{1,0:T(8,128)(2,1)S(1)}, bf16[128,1024]{1,0:T(8,128)(2,1)S(1)}, u32[]{:S(2)}, u32[]{:S(2)}) collective-permute-start(bf16[128,1024]{1,0:T(8,128)(2,1)S(1)} %get-tuple-element.35.refs_2_), channel_id=1, source_target_pairs={{0,4},{4,0},{8,12},{12,8},{16,20},{20,16},{24,28},{28,24},{1,5},{5... | collective-permute-start | bytes 786440 | tf_op jit(solution)/shard_map/ppermute | solution.py:449
  4.4 6.8 %collective-permute-start.1 = (bf16[128,512]{1,0:T(8,128)(2,1)S(1)}, bf16[128,512]{1,0:T(8,128)(2,1)S(1)}, u32[]{:S(2)}, u32[]{:S(2)}) collective-permute-start(bf16[128,512]{1,0:T(8,128)(2,1)S(1)} %get-tuple-element.38.refs_2_), channel_id=1, source_target_pairs={{0,1},{1,0},{2,3},{3,2},{4,5},{5,4},{6,7},{7,6},{8,9},{9,8},{10,11... | collective-permute-start | bytes 393224 | tf_op jit(solution)/shard_map/ppermute | solution.py:449
  7.4 6.7 %copy-start.1 = (bf16[512,2048]{1,0:T(8,128)(2,1)S(1)}, bf16[512,2048]{1,0:T(8,128)(2,1)}, u32[]{:S(2)}) copy-start(bf16[512,2048]{1,0:T(8,128)(2,1)} %refs_0_.1) | copy-start | bytes 6291460
  7.4 10.2 %collective-permute-start.5 = (bf16[128,1024]{1,0:T(8,128)(2,1)S(1)}, bf16[128,1024]{1,0:T(8,128)(2,1)S(1)}, u32[]{:S(2)}, u32[]{:S(2)}) collective-permute-start(bf16[128,1024]{1,0:T(8,128)(2,1)S(1)} %pair.2.refs_2_), channel_id=1, source_target_pairs={{0,24},{4,28},{8,16},{12,20},{16,8},{20,12},{24,0},{28,4},{1,25},{... | collective-permute-start | bytes 786440 | tf_op jit(solution)/shard_map/ppermute | solution.py:449
  9.9 9.4 %collective-permute-start.3 = (bf16[64,1024]{1,0:T(8,128)(2,1)S(1)}, bf16[64,1024]{1,0:T(8,128)(2,1)S(1)}, u32[]{:S(2)}, u32[]{:S(2)}) collective-permute-start(bf16[64,1024]{1,0:T(8,128)(2,1)S(1)} %get-tuple-element.43), channel_id=1, source_target_pairs={{0,8},{4,12},{8,0},{12,4},{16,24},{20,28},{24,16},{28,20},{1,9},{5... | collective-permute-start | bytes 393224 | tf_op jit(solution)/shard_map/ppermute | solution.py:449
  10.5 10.9 %collective-permute-start.4 = (bf16[64,1024]{1,0:T(8,128)(2,1)S(1)}, bf16[64,1024]{1,0:T(8,128)(2,1)S(1)}, u32[]{:S(2)}, u32[]{:S(2)}) collective-permute-start(bf16[64,1024]{1,0:T(8,128)(2,1)S(1)} %get-tuple-element.44), channel_id=1, source_target_pairs={{0,16},{4,20},{8,24},{12,28},{16,0},{20,4},{24,8},{28,12},{1,17},{... | collective-permute-start | bytes 393224 | tf_op jit(solution)/shard_map/ppermute | solution.py:449
  11.2 3.9 %copy-start.2 = (bf16[1,1024,1024]{2,1,0:T(8,128)(2,1)S(1)}, bf16[1,1024,1024]{2,1,0:T(8,128)(2,1)}, u32[]{:S(2)}) copy-start(bf16[1,1024,1024]{2,1,0:T(8,128)(2,1)} %param.11) | copy-start | bytes 6291460
  11.2 3.9 %copy-start.3 = (bf16[1,1024,1024]{2,1,0:T(8,128)(2,1)S(1)}, bf16[1,1024,1024]{2,1,0:T(8,128)(2,1)}, u32[]{:S(2)}) copy-start(bf16[1,1024,1024]{2,1,0:T(8,128)(2,1)} %param.12) | copy-start | bytes 6291460
  11.2 12.3 %collective-permute-start.2 = (bf16[128,512]{1,0:T(8,128)(2,1)S(1)}, bf16[128,512]{1,0:T(8,128)(2,1)S(1)}, u32[]{:S(2)}, u32[]{:S(2)}) collective-permute-start(bf16[128,512]{1,0:T(8,128)(2,1)S(1)} %add.8.refs_1_), channel_id=1, source_target_pairs={{0,2},{1,3},{2,0},{3,1},{4,6},{5,7},{6,4},{7,5},{8,10},{9,11},{10,... | collective-permute-start | bytes 393224 | tf_op jit(solution)/shard_map/ppermute | solution.py:449
  18.1 5.5 %collective-permute-start.8 = (bf16[128,512]{1,0:T(8,128)(2,1)S(1)}, bf16[128,512]{1,0:T(8,128)(2,1)S(1)}, u32[]{:S(2)}, u32[]{:S(2)}) collective-permute-start(bf16[128,512]{1,0:T(8,128)(2,1)S(1)} %get-tuple-element.46.refs_3_), channel_id=1, source_target_pairs={{0,1},{1,0},{2,3},{3,2},{4,5},{5,4},{6,7},{7,6},{8,9},{9,8},{10,11... | collective-permute-start | bytes 393224 | tf_op jit(solution)/shard_map/ppermute | solution.py:449
  18.6 7.7 %collective-permute-start.6 = (bf16[64,1024]{1,0:T(8,128)(2,1)S(1)}, bf16[64,1024]{1,0:T(8,128)(2,1)S(1)}, u32[]{:S(2)}, u32[]{:S(2)}) collective-permute-start(bf16[64,1024]{1,0:T(8,128)(2,1)S(1)} %get-tuple-element.48), channel_id=1, source_target_pairs={{0,12},{4,8},{8,4},{12,0},{16,28},{20,24},{24,20},{28,16},{1,13},{... | collective-permute-start | bytes 393224 | tf_op jit(solution)/shard_map/ppermute | solution.py:449
  19.4 6.9 %collective-permute-start.7 = (bf16[64,1024]{1,0:T(8,128)(2,1)S(1)}, bf16[64,1024]{1,0:T(8,128)(2,1)S(1)}, u32[]{:S(2)}, u32[]{:S(2)}) collective-permute-start(bf16[64,1024]{1,0:T(8,128)(2,1)S(1)} %get-tuple-element.49), channel_id=1, source_target_pairs={{0,20},{4,16},{8,28},{12,24},{16,4},{20,0},{24,12},{28,8},{1,21},{... | collective-permute-start | bytes 393224 | tf_op jit(solution)/shard_map/ppermute | solution.py:449
  21.8 6.4 %collective-permute-start.11 = (bf16[128,512]{1,0:T(8,128)(2,1)S(1)}, bf16[128,512]{1,0:T(8,128)(2,1)S(1)}, u32[]{:S(2)}, u32[]{:S(2)}) collective-permute-start(bf16[128,512]{1,0:T(8,128)(2,1)S(1)} %get-tuple-element.47.refs_3_), channel_id=1, source_target_pairs={{0,1},{1,0},{2,3},{3,2},{4,5},{5,4},{6,7},{7,6},{8,9},{9,8},{10,11... | collective-permute-start | bytes 393224 | tf_op jit(solution)/shard_map/ppermute | solution.py:449
  23.6 8.2 %collective-permute-start.10 = (bf16[128,512]{1,0:T(8,128)(2,1)S(1)}, bf16[128,512]{1,0:T(8,128)(2,1)S(1)}, u32[]{:S(2)}, u32[]{:S(2)}) collective-permute-start(bf16[128,512]{1,0:T(8,128)(2,1)S(1)} %add.10.refs_3_), channel_id=1, source_target_pairs={{0,2},{1,3},{2,0},{3,1},{4,6},{5,7},{6,4},{7,5},{8,10},{9,11},{10,... | collective-permute-start | bytes 393224 | tf_op jit(solution)/shard_map/ppermute | solution.py:449
  26.7 9.3 %collective-permute-start.9 = (bf16[128,512]{1,0:T(8,128)(2,1)S(1)}, bf16[128,512]{1,0:T(8,128)(2,1)S(1)}, u32[]{:S(2)}, u32[]{:S(2)}) collective-permute-start(bf16[128,512]{1,0:T(8,128)(2,1)S(1)} %get-tuple-element.52.refs_2_), channel_id=1, source_target_pairs={{0,1},{1,0},{2,3},{3,2},{4,5},{5,4},{6,7},{7,6},{8,9},{9,8},{10,11... | collective-permute-start | bytes 393224 | tf_op jit(solution)/shard_map/ppermute | solution.py:449
  28.2 11.3 %collective-permute-start.15 = (bf16[128,512]{1,0:T(8,128)(2,1)S(1)}, bf16[128,512]{1,0:T(8,128)(2,1)S(1)}, u32[]{:S(2)}, u32[]{:S(2)}) collective-permute-start(bf16[128,512]{1,0:T(8,128)(2,1)S(1)} %add.11.refs_3_), channel_id=1, source_target_pairs={{0,2},{1,3},{2,0},{3,1},{4,6},{5,7},{6,4},{7,5},{8,10},{9,11},{10,... | collective-permute-start | bytes 393224 | tf_op jit(solution)/shard_map/ppermute | solution.py:449
  31.8 9.8 %collective-permute-start.14 = (bf16[128,512]{1,0:T(8,128)(2,1)S(1)}, bf16[128,512]{1,0:T(8,128)(2,1)S(1)}, u32[]{:S(2)}, u32[]{:S(2)}) collective-permute-start(bf16[128,512]{1,0:T(8,128)(2,1)S(1)} %add.12.refs_8_.refs_0_), channel_id=1, source_target_pairs={{0,1},{1,0},{2,3},{3,2},{4,5},{5,4},{6,7},{7,6},{8,9},{9,8},{10,11... | collective-permute-start | bytes 393224 | tf_op jit(solution)/shard_map/ppermute | solution.py:449
  36.1 9.1 %collective-permute-start.13 = (bf16[128,512]{1,0:T(8,128)(2,1)S(1)}, bf16[128,512]{1,0:T(8,128)(2,1)S(1)}, u32[]{:S(2)}, u32[]{:S(2)}) collective-permute-start(bf16[128,512]{1,0:T(8,128)(2,1)S(1)} %add.13.refs_1_), channel_id=1, source_target_pairs={{0,2},{1,3},{2,0},{3,1},{4,6},{5,7},{6,4},{7,5},{8,10},{9,11},{10,... | collective-permute-start | bytes 393224 | tf_op jit(solution)/shard_map/ppermute | solution.py:449
  39.5 6.9 %collective-permute-start.12 = (bf16[128,512]{1,0:T(8,128)(2,1)S(1)}, bf16[128,512]{1,0:T(8,128)(2,1)S(1)}, u32[]{:S(2)}, u32[]{:S(2)}) collective-permute-start(bf16[128,512]{1,0:T(8,128)(2,1)S(1)} %release.1.refs_3_.refs_0_), channel_id=1, source_target_pairs={{0,1},{1,0},{2,3},{3,2},{4,5},{5,4},{6,7},{7,6},{8,9},{9,8},{10,11... | collective-permute-start | bytes 393224 | tf_op jit(solution)/shard_map/ppermute | solution.py:449
  39.5 8.5 %collective-permute-start.17 = (bf16[128,512]{1,0:T(8,128)(2,1)S(1)}, bf16[128,512]{1,0:T(8,128)(2,1)S(1)}, u32[]{:S(2)}, u32[]{:S(2)}) collective-permute-start(bf16[128,512]{1,0:T(8,128)(2,1)S(1)} %add.14.refs_6_.refs_0_), channel_id=1, source_target_pairs={{0,1},{1,0},{2,3},{3,2},{4,5},{5,4},{6,7},{7,6},{8,9},{9,8},{10,11... | collective-permute-start | bytes 393224 | tf_op jit(solution)/shard_map/ppermute | solution.py:449
  42.4 10.2 %collective-permute-start.16 = (bf16[128,1024]{1,0:T(8,128)(2,1)S(1)}, bf16[128,1024]{1,0:T(8,128)(2,1)S(1)}, u32[]{:S(2)}, u32[]{:S(2)}) collective-permute-start(bf16[128,1024]{1,0:T(8,128)(2,1)S(1)} %second.4.refs_3_), channel_id=1, source_target_pairs={{0,24},{4,28},{8,16},{12,20},{16,8},{20,12},{24,0},{28,4},{1,25},{... | collective-permute-start | bytes 786440 | tf_op jit(solution)/shard_map/ppermute | solution.py:449
  45.2 7.5 %collective-permute-start.21 = (bf16[128,512]{1,0:T(8,128)(2,1)S(1)}, bf16[128,512]{1,0:T(8,128)(2,1)S(1)}, u32[]{:S(2)}, u32[]{:S(2)}) collective-permute-start(bf16[128,512]{1,0:T(8,128)(2,1)S(1)} %add.15.refs_6_.refs_0_), channel_id=1, source_target_pairs={{0,1},{1,0},{2,3},{3,2},{4,5},{5,4},{6,7},{7,6},{8,9},{9,8},{10,11... | collective-permute-start | bytes 393224 | tf_op jit(solution)/shard_map/ppermute | solution.py:449
  48.8 5.5 %collective-permute-start.19 = (bf16[64,1024]{1,0:T(8,128)(2,1)S(1)}, bf16[64,1024]{1,0:T(8,128)(2,1)S(1)}, u32[]{:S(2)}, u32[]{:S(2)}) collective-permute-start(bf16[64,1024]{1,0:T(8,128)(2,1)S(1)} %get-tuple-element.60.refs_2_), channel_id=1, source_target_pairs={{0,8},{4,12},{8,0},{12,4},{16,24},{20,28},{24,16},{28,20},{1,9},{5... | collective-permute-start | bytes 393224 | tf_op jit(solution)/shard_map/ppermute | solution.py:449
  50.3 5.2 %collective-permute-start.20 = (bf16[64,1024]{1,0:T(8,128)(2,1)S(1)}, bf16[64,1024]{1,0:T(8,128)(2,1)S(1)}, u32[]{:S(2)}, u32[]{:S(2)}) collective-permute-start(bf16[64,1024]{1,0:T(8,128)(2,1)S(1)} %get-tuple-element.62), channel_id=1, source_target_pairs={{0,16},{4,20},{8,24},{12,28},{16,0},{20,4},{24,8},{28,12},{1,17},{... | collective-permute-start | bytes 393224 | tf_op jit(solution)/shard_map/ppermute | solution.py:449
  52.6 3.2 %collective-permute-start.18 = (bf16[128,1024]{1,0:T(8,128)(2,1)S(1)}, bf16[128,1024]{1,0:T(8,128)(2,1)S(1)}, u32[]{:S(2)}, u32[]{:S(2)}) collective-permute-start(bf16[128,1024]{1,0:T(8,128)(2,1)S(1)} %pair.3.refs_6_), channel_id=1, source_target_pairs={{0,4},{4,0},{8,12},{12,8},{16,20},{20,16},{24,28},{28,24},{1,5},{5... | collective-permute-start | bytes 786440 | tf_op jit(solution)/shard_map/ppermute | solution.py:449
  53.4 5.3 %collective-permute-start.22 = (bf16[64,1024]{1,0:T(8,128)(2,1)S(1)}, bf16[64,1024]{1,0:T(8,128)(2,1)S(1)}, u32[]{:S(2)}, u32[]{:S(2)}) collective-permute-start(bf16[64,1024]{1,0:T(8,128)(2,1)S(1)} %get-tuple-element.63.refs_3_), channel_id=1, source_target_pairs={{0,12},{4,8},{8,4},{12,0},{16,28},{20,24},{24,20},{28,16},{1,13},{... | collective-permute-start | bytes 393224 | tf_op jit(solution)/shard_map/ppermute | solution.py:449
  53.6 5.2 %collective-permute-start.23 = (bf16[64,1024]{1,0:T(8,128)(2,1)S(1)}, bf16[64,1024]{1,0:T(8,128)(2,1)S(1)}, u32[]{:S(2)}, u32[]{:S(2)}) collective-permute-start(bf16[64,1024]{1,0:T(8,128)(2,1)S(1)} %get-tuple-element.64), channel_id=1, source_target_pairs={{0,20},{4,16},{8,28},{12,24},{16,4},{20,0},{24,12},{28,8},{1,21},{... | collective-permute-start | bytes 393224 | tf_op jit(solution)/shard_map/ppermute | solution.py:449

commit v3 on v2

--- a/solution.py
+++ b/solution.py
@@ -8,18 +8,18 @@
 from jax.sharding import PartitionSpec as P
 
 CHUNKS = ((0, 1), (6, 7), (2, 4), (3, 5))
-LATER = (2, 4, 3, 5, 0)
-PARTS = (CHUNKS[2], CHUNKS[0] + CHUNKS[1], CHUNKS[3])
+CROSSING, STRAIGHT = (1, 7, 3, 5), (6, 2, 4, 0)
+PARTS = (CHUNKS[2], CHUNKS[3], CHUNKS[0] + CHUNKS[1])
 ORDER = (
-    ("first", 0), ("diagonal", 0), ("add", 0), ("prep", 0), ("turn", 0), ("first", 1),
-    ("first", 2), ("add", 0), ("add", 1), ("first", 3), ("add", 2), ("add", 1), ("down", 0),
-    ("add", 3), ("release", 0), ("add", 2), ("second", 1), ("add", 3), ("second", 0),
-    ("second", 2), ("cross", 0), ("second", 3), ("gather", 0), ("gather", 1),
+    ("first", 0), ("bundle", 0), ("add", 0), ("prep", 0), ("turn", 0), ("first", 1),
+    ("first", 2), ("add", 0), ("add", 1), ("first", 3), ("add", 2), ("add", 1), ("add", 3),
+    ("release", 0), ("add", 2), ("second", 1), ("add", 3), ("second", 2), ("second", 3),
+    ("second", 0), ("cross", 0), ("down", 0), ("gather", 0), ("gather", 1),
 )
 HELD = (0,)
 COST = {
     "place": 10**10, "pack": 10**10, "rest": 1, "first": 1, "prep": 1, "turn": 1,
-    "add": 10**9, "release": 1, "pair": 1, "second": 10**10, "down": 1, "gather": 1, "finish": 1,
+    "add": 10**9, "bundle": 1, "second": 10**10, "down": 10**10, "gather": 5 * 10**9, "finish": 1,
 }
 MIB = 1 << 20
 BF16, F32 = jnp.bfloat16, jnp.float32
@@ -166,22 +166,25 @@
     )
 
 
-def pair_body(count, spots, cap, *refs):
-    refs[count][...] = rows_at(refs[:count], spots, cap)
-
-
-def pair(blocks, cap, after):
-    arrays = arrays_of(blocks)
-    shape = jax.ShapeDtypeStruct((len(blocks) * cap, arrays[0].shape[1]), BF16)
-    return call(
-        functools.partial(pair_body, len(arrays), spots_of(blocks, arrays), cap),
-        "pair",
+def bundle_body(count, groups, cap, *refs):
+    for spots, out in zip(groups, refs[count:]):
+        out[...] = rows_at(refs[:count], spots, cap)
+
+
+def bundle(groups, cap, after):
+    arrays = arrays_of([block for blocks in groups for block in blocks])
+    width = arrays[0].shape[1]
+    return call(
+        functools.partial(
+            bundle_body, len(arrays), [spots_of(blocks, arrays) for blocks in groups], cap
+        ),
+        "bundle",
         arrays,
         [VMEM] * len(arrays),
-        [shape],
-        [VMEM],
-        after=after,
-    )[0]
+        [jax.ShapeDtypeStruct((len(blocks) * cap, width), BF16) for blocks in groups],
+        [VMEM] * len(groups),
+        after=after,
+    )
 
 
 def first_body(count, spots, cap, weight, *refs):
@@ -216,33 +219,24 @@
     )
 
 
-def add_body(count, keep, *refs):
-    total = keep[...]
-    for got in refs[:count]:
-        total = total + got[...].astype(F32)
-    refs[count][...] = total.astype(BF16)
-
-
-def add(keep, gots, after):
-    return call(
-        functools.partial(add_body, len(gots)),
+def add_body(rows, *refs):
+    total = 0.0
+    for ref, row in zip(refs, rows):
+        total += ref[row : row + refs[-1].shape[0]].astype(F32)
+    refs[-1][...] = total.astype(BF16)
+
+
+def add(terms, size, after):
+    return call(
+        functools.partial(add_body, [row for _, row in terms]),
         "add",
-        (keep, *gots),
-        [VMEM] * (1 + len(gots)),
-        [jax.ShapeDtypeStruct(keep.shape, BF16)],
+        [array for array, _ in terms],
+        [VMEM] * len(terms),
+        [jax.ShapeDtypeStruct((size, terms[0][0].shape[1]), BF16)],
         [VMEM],
-        16,
+        8,
         after=after,
     )[0]
-
-
-def release_body(total, out):
-    out[...] = total[...]
-
-
-def release(total, after):
-    shape = jax.ShapeDtypeStruct(total.shape, total.dtype)
-    return call(release_body, "release", (total,), [VMEM], [shape], [VMEM], after=after)[0]
 
 
 def prep_body(saved, gate_factor, up_factor, hidden):
@@ -304,7 +298,7 @@
     return ref[pl.ds(start, cap), :]
 
 
-def second_body(chunk, cap, own, other, gate_factor, up_factor, w_gate, w_up, *refs):
+def second_body(chunk, cap, row, own, other, gate_factor, up_factor, w_gate, w_up, *refs):
     outs, grads = refs[:-1], refs[-1]
     width, features = w_gate.shape
     halves = [slice(0, width // 2), slice(width // 2, width)]
@@ -313,7 +307,7 @@
         @pl.when(lax.axis_index("dp") % 2 == odd)
         def _():
             grads[:, mine] = own[...]
-            grads[:, theirs] = other[...]
+            grads[:, theirs] = other[row : row + own.shape[0]]
 
     grad = grads[...].astype(F32)
     d_gate, d_up = (
@@ -335,9 +329,9 @@
     count = 1 if together else len(chunk)
     size = len(chunk) // count * cap
     return call(
-        functools.partial(second_body, chunk, cap),
+        functools.partial(second_body, chunk, cap, other[1]),
         "second",
-        (own, other, *factors, *weights),
+        (own, other[0], *factors, *weights),
         [VMEM] * 6,
         [jax.ShapeDtypeStruct((size, features), BF16)] * count,
         [VMEM] * count,
@@ -453,43 +447,47 @@
     groups = lax.axis_size("expert")
     cap = saved_pre.shape[0] // groups
     features = dy_values.shape[1]
-    keeps, gots, owns, others, returned, result = {}, {}, {}, {}, {}, {}
+    terms, owns, others, returned, result = {}, {}, {}, {}, {}
 
     place = find_place(expert_ids, groups, cap)
     last, sooner = [place], []
-    scaled, crossing, ahead = pack(place, dy_values, dy_scales, ((1, 7), (6,)), cap)
+    scaled, crossing = pack(place, dy_values, dy_scales, (CROSSING,), cap)
     side = swap(crossing, "expert", 1)
-    rest = pack_rest(place, scaled, [(k,) for k in LATER], cap, [crossing])
-    last[:] = rest[-1:]
-    blocks = {1: (side, 0)}
-    for k, block in zip(LATER, rest):
-        blocks[k] = (swap(block, "expert", k) if k else block, 0)
-
-    def do_diagonal(_):
-        both = pair([(ahead, 0), (side, cap)], cap, last)
-        last[:] = [both]
-        got = swap(both, "expert", 6)
-        blocks.update({6: (got, 0), 7: (got, cap)})
+    (ahead,) = pack_rest(place, scaled, (STRAIGHT,), cap, [crossing])
+    last[:] = [ahead]
+    blocks = {1: (side, 0), 0: (ahead, STRAIGHT.index(0) * cap)}
+
+    def do_bundle(_):
+        chips = [k for k in STRAIGHT if k]
+        groups = [
+            ((ahead, STRAIGHT.index(k) * cap), (side, CROSSING.index(k + 1) * cap)) for k in chips
+        ]
+        bundles = bundle(groups, cap, last)
+        last[:] = bundles[:1]
+        for k, both in zip(chips, bundles):
+            got = swap(both, "expert", k)
+            blocks.update({k: (got, 0), k + 1: (got, cap)})
 
     def do_first(c):
-        send, keeps[c] = first([blocks[k] for k in CHUNKS[c]], w_down[0], cap, last)
+        send, keep = first([blocks[k] for k in CHUNKS[c]], w_down[0], cap, last)
         last[:] = [send]
-        gots[c] = [swap(send, "dp", 1)]
+        terms[c] = [(keep, 0), (swap(send, "dp", 1), 0)]
 
     def do_add(c):
-        part = add(keeps[c], gots[c], last)
+        size = len(CHUNKS[c]) * cap
+        part = add(terms[c], size, last)
         last[:] = [part]
-        if len(gots[c]) == 1:
-            gots[c].append(swap(part, "dp", 2))
-        elif c in HELD:
+        if len(terms[c]) == 2:
+            terms[c].append((swap(part, "dp", 2), 0))
+        else:
             owns[c] = part
-        else:
-            owns[c], others[c] = part, swap(part, "dp", 1)
+            if c not in HELD:
+                others[c] = (swap(part, "dp", 1), 0)
 
     def do_release(c):
-        owns[c] = release(owns[c], last)
-        last[:] = [owns[c]]
-        others[c] = swap(owns[c], "dp", 1)
+        (total,) = bundle([[(owns[c], 0)]], len(CHUNKS[c]) * cap, last)
+        last[:] = [total]
+        others[c] = (swap(total, "dp", 1), 0)
 
     def do_prep(_):
         *result["factors"], result["hidden"] = prep(saved_pre, last)
@@ -515,7 +513,7 @@
             returned.update({k: (swap(grad, "expert", k), 0) for k, grad in zip(chunk, grads)})
 
     def do_cross(_):
-        both = pair([(result["near"], 0), (result["back"], cap)], cap, last)
+        (both,) = bundle([[(result["near"], 0), (result["back"], cap)]], cap, last)
         last[:] = [both]
         got = swap(both, "expert", 1)
         returned.update({1: (got, 0), 7: (got, cap)})
@@ -534,7 +532,7 @@
         "first": do_first,
         "add": do_add,
         "release": do_release,
-        "diagonal": do_diagonal,
+        "bundle": do_bundle,
         "cross": do_cross,
         "prep": do_prep,
         "turn": do_turn,

time: 60.1 us -> 60.9 us (1.013)
  waiting for transfers between devices: 11.9 us -> 16.8 us
  starting transfers between devices: 33.6 us -> 29.5 us
    ppermute x24 -> x22, waiting for transfers between devices: 11.9 us -> 16.8 us  [swap(): return lax.ppermute(block, axis, [(i, i ^ k) for i in range(size)])]
    ppermute x24 -> x22, starting transfers between devices: 33.6 us -> 29.5 us  [swap(): return lax.ppermute(block, axis, [(i, i ^ k) for i in range(size)])]
  transfers between devices with their start and end apart: 24 -> 22, of which waited for: 12 -> 10; matrix products, arithmetic and copies ran while one was open for 0% -> 0% of each run, Pallas kernels for 18% -> 17%
where the time goes in v3:
time: 60.9 us; the launch traced here: 60.8 us
  starting transfers between devices  29.5 us (48%)
  waiting for transfers between devices  16.8 us (28%)
  Pallas kernels  13.5 us (22%)
  between operations  0.95 us (2%)
    ppermute x22, starting transfers between devices, swap(): return lax.ppermute(block, axis, [(i, i ^ k) for i in range(size)])  29.5 us
    ppermute x22, waiting for transfers between devices, swap(): return lax.ppermute(block, axis, [(i, i ^ k) for i in range(size)])  16.8 us
    pallas_call x28, Pallas kernels, call(): pl.pallas_call(run, name=name, out_shape=outs, in_specs=list(specs) + [AN...  13.5 us
  transfers between devices with their start and end apart: 22, of which 10 were waited for; matrix products, arithmetic and copies ran while one was open for 0% of the time, Pallas kernels for 17%

profile of v3, /device:TPU:0, one launch (start us, length us, event | category | flops | bytes accessed | tf_op | source)
XLA Modules:
  0.0 60.8 jit_solution(7272181980970888442)
XLA Ops:
  0.6 1.0 %place.1.refs_0_ = bf16[512,256]{1,0:T(8,128)(2,1)S(1)} custom-call(s32[1,256]{1,0:T(1,128)} %bitcast.13), custom_call_target="tpu_custom_call" | custom-call | flops 10000000000 | tf_op jit(solution)/shard_map/place/pallas_call | solution.py:41
  1.7 0.5 pack.1
  2.2 0.5 collective-permute-start
  2.7 0.3 rest.1.refs_1_.refs_3_.refs_0_
  3.1 1.2 %collective-permute-done.refs_2_.refs_1_ = bf16[256,1024]{1,0:T(8,128)(2,1)S(1)} collective-permute-done((bf16[256,1024]{1,0:T(8,128)(2,1)S(1)}, bf16[256,1024]{1,0:T(8,128)(2,1)S(1)}, u32[]{:S(2)}, u32[]{:S(2)}) %collective-permute-start) | collective-permute-done | bytes 524320 | tf_op jit(solution)/shard_map/ppermute | solution.py:443
  4.3 0.5 first.4
  4.8 3.0 %collective-permute-start.1 = (bf16[128,512]{1,0:T(8,128)(2,1)S(1)}, bf16[128,512]{1,0:T(8,128)(2,1)S(1)}, u32[]{:S(2)}, u32[]{:S(2)}) collective-permute-start(bf16[128,512]{1,0:T(8,128)(2,1)S(1)} %get-tuple-element.34.refs_2_), channel_id=1, source_target_pairs={{0,1},{1,0},{2,3},{3,2},{4,5},{5,4},{6,7},{7,6},{8,9},{9,8},{10,11... | collective-permute-start | bytes 393224 | tf_op jit(solution)/shard_map/ppermute | solution.py:443
  7.8 2.5 %collective-permute-start.4 = (bf16[128,1024]{1,0:T(8,128)(2,1)S(1)}, bf16[128,1024]{1,0:T(8,128)(2,1)S(1)}, u32[]{:S(2)}, u32[]{:S(2)}) collective-permute-start(bf16[128,1024]{1,0:T(8,128)(2,1)S(1)} %get-tuple-element.35.refs_2_), channel_id=1, source_target_pairs={{0,24},{4,28},{8,16},{12,20},{16,8},{20,12},{24,0},{28,4},{1,25},{... | collective-permute-start | bytes 786440 | tf_op jit(solution)/shard_map/ppermute | solution.py:443
  10.4 0.5 collective-permute-start.2
  10.9 0.5 collective-permute-start.3
  11.4 0.2 collective-permute-done.1.refs_1_
  11.6 2.8 %collective-permute-start.6 = (bf16[128,512]{1,0:T(8,128)(2,1)S(1)}, bf16[128,512]{1,0:T(8,128)(2,1)S(1)}, u32[]{:S(2)}, u32[]{:S(2)}) collective-permute-start(bf16[128,512]{1,0:T(8,128)(2,1)S(1)} %add.8.refs_1_), channel_id=1, source_target_pairs={{0,2},{1,3},{2,0},{3,1},{4,6},{5,7},{6,4},{7,5},{8,10},{9,11},{10,... | collective-permute-start | bytes 393224 | tf_op jit(solution)/shard_map/ppermute | solution.py:443
  14.4 1.0 %prep.1 = (f32[512,1024]{1,0:T(8,128)S(1)}, f32[512,1024]{1,0:T(8,128)S(1)}, bf16[512,1024]{1,0:T(8,128)(2,1)S(1)}) custom-call(bf16[512,2048]{1,0:T(8,128)(2,1)S(1)} %copy-done.1, bf16[128,512]{1,0:T(8,128)(2,1)S(1)} %add.8.refs_1_), custom_call_target="tpu_custom_call" | custom-call | flops 1 | tf_op jit(solution)/shard_map/prep/pallas_call | solution.py:41
  15.5 1.3 %turn.1 = (bf16[1024,1024]{1,0:T(8,128)(2,1)S(1)}, bf16[1024,1024]{1,0:T(8,128)(2,1)S(1)}, bf16[256,128]{1,0:T(8,128)(2,1)S(1)}, bf16[256,128]{1,0:T(8,128)(2,1)S(1)}, bf16[256,256]{1,0:T(8,128)(2,1)S(1)}) custom-call(bf16[512,256]{1,0:T(8,128)(2,1)S(1)} %place.1.refs_0_, bf16[1024,1024]{1,0:T(8,128)(2,1)S(1)} %bitcast.10, bf16[1024,1024]{1,0:T(8,128)(2,1)S(1)} %bitcast.11, ...), custom_call_target="tpu_custom_call" | custom-call | flops 1 | tf_op jit(solution)/shard_map/turn/pallas_call | solution.py:41
  16.8 1.2 %collective-permute-done.4.refs_1_.refs_5_ = bf16[128,1024]{1,0:T(8,128)(2,1)S(1)} collective-permute-done((bf16[128,1024]{1,0:T(8,128)(2,1)S(1)}, bf16[128,1024]{1,0:T(8,128)(2,1)S(1)}, u32[]{:S(2)}, u32[]{:S(2)}) %collective-permute-start.4) | collective-permute-done | bytes 262176 | tf_op jit(solution)/shard_map/ppermute | solution.py:443
  18.0 0.5 first.5
  18.5 0.4 collective-permute-start.5
  18.9 3.7 %collective-permute-done.2.refs_1_.refs_3_ = bf16[128,1024]{1,0:T(8,128)(2,1)S(1)} collective-permute-done((bf16[128,1024]{1,0:T(8,128)(2,1)S(1)}, bf16[128,1024]{1,0:T(8,128)(2,1)S(1)}, u32[]{:S(2)}, u32[]{:S(2)}) %collective-permute-start.2) | collective-permute-done | bytes 262176 | tf_op jit(solution)/shard_map/ppermute | solution.py:443
  22.6 0.5 first.6
  23.1 0.5 collective-permute-start.9
  23.7 2.7 %collective-permute-start.8 = (bf16[128,512]{1,0:T(8,128)(2,1)S(1)}, bf16[128,512]{1,0:T(8,128)(2,1)S(1)}, u32[]{:S(2)}, u32[]{:S(2)}) collective-permute-start(bf16[128,512]{1,0:T(8,128)(2,1)S(1)} %add.10.refs_3_), channel_id=1, source_target_pairs={{0,2},{1,3},{2,0},{3,1},{4,6},{5,7},{6,4},{7,5},{8,10},{9,11},{10,... | collective-permute-start | bytes 393224 | tf_op jit(solution)/shard_map/ppermute | solution.py:443
  26.4 0.5 first.7
  26.8 1.6 %collective-permute-start.7 = (bf16[128,512]{1,0:T(8,128)(2,1)S(1)}, bf16[128,512]{1,0:T(8,128)(2,1)S(1)}, u32[]{:S(2)}, u32[]{:S(2)}) collective-permute-start(bf16[128,512]{1,0:T(8,128)(2,1)S(1)} %get-tuple-element.46.refs_2_), channel_id=1, source_target_pairs={{0,1},{1,0},{2,3},{3,2},{4,5},{5,4},{6,7},{7,6},{8,9},{9,8},{10,11... | collective-permute-start | bytes 393224 | tf_op jit(solution)/shard_map/ppermute | solution.py:443
  28.5 3.8 %collective-permute-done.9.refs_1_ = bf16[128,512]{1,0:T(8,128)(2,1)S(1)} collective-permute-done((bf16[128,512]{1,0:T(8,128)(2,1)S(1)}, bf16[128,512]{1,0:T(8,128)(2,1)S(1)}, u32[]{:S(2)}, u32[]{:S(2)}) %collective-permute-start.9) | collective-permute-done | bytes 131104 | tf_op jit(solution)/shard_map/ppermute | solution.py:443
  32.4 0.1 collective-permute-start.12
  32.5 2.5 %collective-permute-start.11 = (bf16[128,512]{1,0:T(8,128)(2,1)S(1)}, bf16[128,512]{1,0:T(8,128)(2,1)S(1)}, u32[]{:S(2)}, u32[]{:S(2)}) collective-permute-start(bf16[128,512]{1,0:T(8,128)(2,1)S(1)} %add.12.refs_2_.refs_0_), channel_id=1, source_target_pairs={{0,1},{1,0},{2,3},{3,2},{4,5},{5,4},{6,7},{7,6},{8,9},{9,8},{10,11... | collective-permute-start | bytes 393224 | tf_op jit(solution)/shard_map/ppermute | solution.py:443
  35.1 3.1 %collective-permute-start.10 = (bf16[128,512]{1,0:T(8,128)(2,1)S(1)}, bf16[128,512]{1,0:T(8,128)(2,1)S(1)}, u32[]{:S(2)}, u32[]{:S(2)}) collective-permute-start(bf16[128,512]{1,0:T(8,128)(2,1)S(1)} %add.13.refs_1_), channel_id=1, source_target_pairs={{0,2},{1,3},{2,0},{3,1},{4,6},{5,7},{6,4},{7,5},{8,10},{9,11},{10,... | collective-permute-start | bytes 393224 | tf_op jit(solution)/shard_map/ppermute | solution.py:443
  38.2 3.8 %collective-permute-done.12.refs_2_ = bf16[128,512]{1,0:T(8,128)(2,1)S(1)} collective-permute-done((bf16[128,512]{1,0:T(8,128)(2,1)S(1)}, bf16[128,512]{1,0:T(8,128)(2,1)S(1)}, u32[]{:S(2)}, u32[]{:S(2)}) %collective-permute-start.12) | collective-permute-done | bytes 131104 | tf_op jit(solution)/shard_map/ppermute | solution.py:443
  42.1 0.1 collective-permute-start.14
  42.2 0.8 %second.4.refs_3_ = bf16[128,1024]{1,0:T(8,128)(2,1)S(1)} custom-call(bf16[128,512]{1,0:T(8,128)(2,1)S(1)} %add.12.refs_2_.refs_0_, bf16[128,512]{1,0:T(8,128)(2,1)S(1)} %collective-permute-done.11.refs_1_, f32[512,1024]{1,0:T(8,128)S(1)} %get-tuple-element.48.refs_2_, f32[512,1024]{1,0:T(8,128)S(1)} %get-tuple-element.49.refs_3_, ...), custom_call_target="tpu_custom_call" | custom-call | flops 10000000000 | tf_op jit(solution)/shard_map/second/pallas_call | solution.py:41
  42.9 2.6 %collective-permute-start.20 = (bf16[128,1024]{1,0:T(8,128)(2,1)S(1)}, bf16[128,1024]{1,0:T(8,128)(2,1)S(1)}, u32[]{:S(2)}, u32[]{:S(2)}) collective-permute-start(bf16[128,1024]{1,0:T(8,128)(2,1)S(1)} %second.4.refs_3_), channel_id=1, source_target_pairs={{0,24},{4,28},{8,16},{12,20},{16,8},{20,12},{24,0},{28,4},{1,25},{... | collective-permute-start | bytes 786440 | tf_op jit(solution)/shard_map/ppermute | solution.py:443
  45.5 0.4 collective-permute-done.10.refs_2_
  46.0 1.7 %collective-permute-start.13 = (bf16[128,512]{1,0:T(8,128)(2,1)S(1)}, bf16[128,512]{1,0:T(8,128)(2,1)S(1)}, u32[]{:S(2)}, u32[]{:S(2)}) collective-permute-start(bf16[128,512]{1,0:T(8,128)(2,1)S(1)} %add.15.refs_6_.refs_0_), channel_id=1, source_target_pairs={{0,1},{1,0},{2,3},{3,2},{4,5},{5,4},{6,7},{7,6},{8,9},{9,8},{10,11... | collective-permute-start | bytes 393224 | tf_op jit(solution)/shard_map/ppermute | solution.py:443
  47.7 1.6 %collective-permute-done.14.refs_1_ = bf16[128,512]{1,0:T(8,128)(2,1)S(1)} collective-permute-done((bf16[128,512]{1,0:T(8,128)(2,1)S(1)}, bf16[128,512]{1,0:T(8,128)(2,1)S(1)}, u32[]{:S(2)}, u32[]{:S(2)}) %collective-permute-start.14) | collective-permute-done | bytes 131104 | tf_op jit(solution)/shard_map/ppermute | solution.py:443
  49.2 0.7 %second.5 = (bf16[64,1024]{1,0:T(8,128)(2,1)S(1)}, bf16[64,1024]{1,0:T(8,128)(2,1)S(1)}) custom-call(bf16[128,512]{1,0:T(8,128)(2,1)S(1)} %add.14.refs_6_.refs_0_, bf16[128,512]{1,0:T(8,128)(2,1)S(1)} %collective-permute-done.14.refs_1_, f32[512,1024]{1,0:T(8,128)S(1)} %get-tuple-element.48.refs_2_, f32[512,1024]{1,0:T(8,128)S(1)} %get-tuple-element.49.refs_3_, ...), custom_call_target="tpu_custom_call" | custom-call | flops 10000000000 | tf_op jit(solution)/shard_map/second/pallas_call | solution.py:41
  49.9 1.9 %collective-permute-start.18 = (bf16[64,1024]{1,0:T(8,128)(2,1)S(1)}, bf16[64,1024]{1,0:T(8,128)(2,1)S(1)}, u32[]{:S(2)}, u32[]{:S(2)}) collective-permute-start(bf16[64,1024]{1,0:T(8,128)(2,1)S(1)} %get-tuple-element.55), channel_id=1, source_target_pairs={{0,16},{4,20},{8,24},{12,28},{16,0},{20,4},{24,8},{28,12},{1,17},{... | collective-permute-start | bytes 393224 | tf_op jit(solution)/shard_map/ppermute | solution.py:443
  51.8 1.4 %collective-permute-start.17 = (bf16[64,1024]{1,0:T(8,128)(2,1)S(1)}, bf16[64,1024]{1,0:T(8,128)(2,1)S(1)}, u32[]{:S(2)}, u32[]{:S(2)}) collective-permute-start(bf16[64,1024]{1,0:T(8,128)(2,1)S(1)} %get-tuple-element.51.refs_6_), channel_id=1, source_target_pairs={{0,8},{4,12},{8,0},{12,4},{16,24},{20,28},{24,16},{28,20},{1,9},{5... | collective-permute-start | bytes 393224 | tf_op jit(solution)/shard_map/ppermute | solution.py:443
  53.3 0.7 %second.6 = (bf16[64,1024]{1,0:T(8,128)(2,1)S(1)}, bf16[64,1024]{1,0:T(8,128)(2,1)S(1)}) custom-call(bf16[128,512]{1,0:T(8,128)(2,1)S(1)} %add.15.refs_6_.refs_0_, bf16[128,512]{1,0:T(8,128)(2,1)S(1)} %collective-permute-done.13.refs_1_, f32[512,1024]{1,0:T(8,128)S(1)} %get-tuple-element.48.refs_2_, f32[512,1024]{1,0:T(8,128)S(1)} %get-tuple-element.49.refs_3_, ...), custom_call_target="tpu_custom_call" | custom-call | flops 10000000000 | tf_op jit(solution)/shard_map/second/pallas_call | solution.py:41
  54.0 0.1 collective-permute-start.16
  54.1 0.5 collective-permute-start.15
  54.6 0.7 %second.7 = (bf16[64,1024]{1,0:T(8,128)(2,1)S(1)}, bf16[64,1024]{1,0:T(8,128)(2,1)S(1)}) custom-call(bf16[128,512]{1,0:T(8,128)(2,1)S(1)} %add.9.refs_2_.refs_0_, bf16[128,512]{1,0:T(8,128)(2,1)S(1)} %collective-permute-done.19.refs_1_, f32[512,1024]{1,0:T(8,128)S(1)} %get-tuple-element.48.refs_2_, f32[512,1024]{1,0:T(8,128)S(1)} %get-tuple-element.49.refs_3_, ...), custom_call_target="tpu_custom_call" | custom-call | flops 10000000000 | tf_op jit(solution)/shard_map/second/pallas_call | solution.py:41
  55.4 0.4 collective-permute-start.21
  55.8 2.5 %down.1 = (f32[1024,1024]{1,0:T(8,128)}, f32[8,128]{1,0:T(8,128)S(1)}) custom-call(bf16[512,1024]{1,0:T(8,128)(2,1)S(1)} %get-tuple-element.36.refs_3_.refs_0_, bf16[256,1024]{1,0:T(8,128)(2,1)S(1)} %rest.1.refs_1_.refs_3_.refs_0_, bf16[256,1024]{1,0:T(8,128)(2,1)S(1)} %collective-permute-done.refs_2_.refs_1_, ...), custom_call_target="tpu_custom_call" | custom-call | flops 10000000000 | tf_op jit(solution)/shard_map/down/pallas_call | solution.py:41
  58.3 0.3 gather.2.refs_3_.refs_4_
  58.6 0.2 collective-permute-done.16.refs_2_
  58.8 0.6 collective-permute-done.15.refs_1_
  59.4 0.3 gather.3.refs_1_.refs_5_
  59.7 1.1 %finish.1 = bf16[256,1024]{1,0:T(8,128)(2,1)} custom-call(bf16[256,256]{1,0:T(8,128)(2,1)S(1)} %get-tuple-element.37.refs_0_, bf16[256,1024]{1,0:T(8,128)(2,1)S(1)} %gather.3.refs_1_.refs_5_, bf16[64,1024]{1,0:T(8,128)(2,1)S(1)} %get-tuple-element.57.refs_2_, bf16[128,1024]{1,0:T(8,128)(2,1)S(1)} %collective-permute-done.21.refs_3_, ...), custom_call_target="tpu_custom_call" | custom-call | flops 1 | tf_op jit(solution)/shard_map/finish/pallas_call | solution.py:41
  (36 shorter events, 0.5 us)
Async XLA Ops:
  0.6 1.1 %copy-start.4 = (bf16[256,1024]{1,0:T(8,128)(2,1)S(1)}, bf16[256,1024]{1,0:T(8,128)(2,1)}, u32[]{:S(2)}) copy-start(bf16[256,1024]{1,0:T(8,128)(2,1)} %refs_2_.1) | copy-start | bytes 1572868
  0.6 1.1 %copy-start.5 = (bf16[256,8]{0,1:T(8,128)(2,1)S(1)}, bf16[256,8]{0,1:T(8,128)(2,1)}, u32[]{:S(2)}) copy-start(bf16[256,8]{0,1:T(8,128)(2,1)} %param.8) | copy-start | bytes 12292
  1.7 2.6 %copy-start = (bf16[1,1024,1024]{2,1,0:T(8,128)(2,1)S(1)}, bf16[1,1024,1024]{2,1,0:T(8,128)(2,1)}, u32[]{:S(2)}) copy-start(bf16[1,1024,1024]{2,1,0:T(8,128)(2,1)} %param.13) | copy-start | bytes 6291460
  2.2 2.1 %collective-permute-start = (bf16[256,1024]{1,0:T(8,128)(2,1)S(1)}, bf16[256,1024]{1,0:T(8,128)(2,1)S(1)}, u32[]{:S(2)}, u32[]{:S(2)}) collective-permute-start(bf16[256,1024]{1,0:T(8,128)(2,1)S(1)} %get-tuple-element.32.refs_2_), channel_id=1, source_target_pairs={{0,4},{4,0},{8,12},{12,8},{16,20},{20,16},{24,28},{28,24},{1,5},{5... | collective-permute-start | bytes 1572872 | tf_op jit(solution)/shard_map/ppermute | solution.py:443
  4.8 6.8 %collective-permute-start.1 = (bf16[128,512]{1,0:T(8,128)(2,1)S(1)}, bf16[128,512]{1,0:T(8,128)(2,1)S(1)}, u32[]{:S(2)}, u32[]{:S(2)}) collective-permute-start(bf16[128,512]{1,0:T(8,128)(2,1)S(1)} %get-tuple-element.34.refs_2_), channel_id=1, source_target_pairs={{0,1},{1,0},{2,3},{3,2},{4,5},{5,4},{6,7},{7,6},{8,9},{9,8},{10,11... | collective-permute-start | bytes 393224 | tf_op jit(solution)/shard_map/ppermute | solution.py:443
  7.8 7.7 %copy-start.3 = (bf16[1,1024,1024]{2,1,0:T(8,128)(2,1)S(1)}, bf16[1,1024,1024]{2,1,0:T(8,128)(2,1)}, u32[]{:S(2)}) copy-start(bf16[1,1024,1024]{2,1,0:T(8,128)(2,1)} %param.12) | copy-start | bytes 6291460
  7.8 6.6 %copy-start.1 = (bf16[512,2048]{1,0:T(8,128)(2,1)S(1)}, bf16[512,2048]{1,0:T(8,128)(2,1)}, u32[]{:S(2)}) copy-start(bf16[512,2048]{1,0:T(8,128)(2,1)} %refs_0_.1) | copy-start | bytes 6291460
  7.8 10.2 %collective-permute-start.4 = (bf16[128,1024]{1,0:T(8,128)(2,1)S(1)}, bf16[128,1024]{1,0:T(8,128)(2,1)S(1)}, u32[]{:S(2)}, u32[]{:S(2)}) collective-permute-start(bf16[128,1024]{1,0:T(8,128)(2,1)S(1)} %get-tuple-element.35.refs_2_), channel_id=1, source_target_pairs={{0,24},{4,28},{8,16},{12,20},{16,8},{20,12},{24,0},{28,4},{1,25},{... | collective-permute-start | bytes 786440 | tf_op jit(solution)/shard_map/ppermute | solution.py:443
  10.4 12.2 %collective-permute-start.2 = (bf16[128,1024]{1,0:T(8,128)(2,1)S(1)}, bf16[128,1024]{1,0:T(8,128)(2,1)S(1)}, u32[]{:S(2)}, u32[]{:S(2)}) collective-permute-start(bf16[128,1024]{1,0:T(8,128)(2,1)S(1)} %get-tuple-element.39), channel_id=1, source_target_pairs={{0,8},{4,12},{8,0},{12,4},{16,24},{20,28},{24,16},{28,20},{1,9},{5... | collective-permute-start | bytes 786440 | tf_op jit(solution)/shard_map/ppermute | solution.py:443
  10.9 11.7 %collective-permute-start.3 = (bf16[128,1024]{1,0:T(8,128)(2,1)S(1)}, bf16[128,1024]{1,0:T(8,128)(2,1)S(1)}, u32[]{:S(2)}, u32[]{:S(2)}) collective-permute-start(bf16[128,1024]{1,0:T(8,128)(2,1)S(1)} %get-tuple-element.40), channel_id=1, source_target_pairs={{0,16},{4,20},{8,24},{12,28},{16,0},{20,4},{24,8},{28,12},{1,17},{... | collective-permute-start | bytes 786440 | tf_op jit(solution)/shard_map/ppermute | solution.py:443
  11.6 3.9 %copy-start.2 = (bf16[1,1024,1024]{2,1,0:T(8,128)(2,1)S(1)}, bf16[1,1024,1024]{2,1,0:T(8,128)(2,1)}, u32[]{:S(2)}) copy-start(bf16[1,1024,1024]{2,1,0:T(8,128)(2,1)} %param.11) | copy-start | bytes 6291460
  11.6 12.0 %collective-permute-start.6 = (bf16[128,512]{1,0:T(8,128)(2,1)S(1)}, bf16[128,512]{1,0:T(8,128)(2,1)S(1)}, u32[]{:S(2)}, u32[]{:S(2)}) collective-permute-start(bf16[128,512]{1,0:T(8,128)(2,1)S(1)} %add.8.refs_1_), channel_id=1, source_target_pairs={{0,2},{1,3},{2,0},{3,1},{4,6},{5,7},{6,4},{7,5},{8,10},{9,11},{10,... | collective-permute-start | bytes 393224 | tf_op jit(solution)/shard_map/ppermute | solution.py:443
  18.5 5.1 %collective-permute-start.5 = (bf16[128,512]{1,0:T(8,128)(2,1)S(1)}, bf16[128,512]{1,0:T(8,128)(2,1)S(1)}, u32[]{:S(2)}, u32[]{:S(2)}) collective-permute-start(bf16[128,512]{1,0:T(8,128)(2,1)S(1)} %get-tuple-element.43.refs_3_), channel_id=1, source_target_pairs={{0,1},{1,0},{2,3},{3,2},{4,5},{5,4},{6,7},{7,6},{8,9},{9,8},{10,11... | collective-permute-start | bytes 393224 | tf_op jit(solution)/shard_map/ppermute | solution.py:443
  23.1 9.2 %collective-permute-start.9 = (bf16[128,512]{1,0:T(8,128)(2,1)S(1)}, bf16[128,512]{1,0:T(8,128)(2,1)S(1)}, u32[]{:S(2)}, u32[]{:S(2)}) collective-permute-start(bf16[128,512]{1,0:T(8,128)(2,1)S(1)} %get-tuple-element.44.refs_3_), channel_id=1, source_target_pairs={{0,1},{1,0},{2,3},{3,2},{4,5},{5,4},{6,7},{7,6},{8,9},{9,8},{10,11... | collective-permute-start | bytes 393224 | tf_op jit(solution)/shard_map/ppermute | solution.py:443
  23.7 8.7 %collective-permute-start.8 = (bf16[128,512]{1,0:T(8,128)(2,1)S(1)}, bf16[128,512]{1,0:T(8,128)(2,1)S(1)}, u32[]{:S(2)}, u32[]{:S(2)}) collective-permute-start(bf16[128,512]{1,0:T(8,128)(2,1)S(1)} %add.10.refs_3_), channel_id=1, source_target_pairs={{0,2},{1,3},{2,0},{3,1},{4,6},{5,7},{6,4},{7,5},{8,10},{9,11},{10,... | collective-permute-start | bytes 393224 | tf_op jit(solution)/shard_map/ppermute | solution.py:443
  26.8 8.2 %collective-permute-start.7 = (bf16[128,512]{1,0:T(8,128)(2,1)S(1)}, bf16[128,512]{1,0:T(8,128)(2,1)S(1)}, u32[]{:S(2)}, u32[]{:S(2)}) collective-permute-start(bf16[128,512]{1,0:T(8,128)(2,1)S(1)} %get-tuple-element.46.refs_2_), channel_id=1, source_target_pairs={{0,1},{1,0},{2,3},{3,2},{4,5},{5,4},{6,7},{7,6},{8,9},{9,8},{10,11... | collective-permute-start | bytes 393224 | tf_op jit(solution)/shard_map/ppermute | solution.py:443
  32.4 9.7 %collective-permute-start.12 = (bf16[128,512]{1,0:T(8,128)(2,1)S(1)}, bf16[128,512]{1,0:T(8,128)(2,1)S(1)}, u32[]{:S(2)}, u32[]{:S(2)}) collective-permute-start(bf16[128,512]{1,0:T(8,128)(2,1)S(1)} %add.11.refs_3_), channel_id=1, source_target_pairs={{0,2},{1,3},{2,0},{3,1},{4,6},{5,7},{6,4},{7,5},{8,10},{9,11},{10,... | collective-permute-start | bytes 393224 | tf_op jit(solution)/shard_map/ppermute | solution.py:443
  32.5 9.6 %collective-permute-start.11 = (bf16[128,512]{1,0:T(8,128)(2,1)S(1)}, bf16[128,512]{1,0:T(8,128)(2,1)S(1)}, u32[]{:S(2)}, u32[]{:S(2)}) collective-permute-start(bf16[128,512]{1,0:T(8,128)(2,1)S(1)} %add.12.refs_2_.refs_0_), channel_id=1, source_target_pairs={{0,1},{1,0},{2,3},{3,2},{4,5},{5,4},{6,7},{7,6},{8,9},{9,8},{10,11... | collective-permute-start | bytes 393224 | tf_op jit(solution)/shard_map/ppermute | solution.py:443
  35.1 10.8 %collective-permute-start.10 = (bf16[128,512]{1,0:T(8,128)(2,1)S(1)}, bf16[128,512]{1,0:T(8,128)(2,1)S(1)}, u32[]{:S(2)}, u32[]{:S(2)}) collective-permute-start(bf16[128,512]{1,0:T(8,128)(2,1)S(1)} %add.13.refs_1_), channel_id=1, source_target_pairs={{0,2},{1,3},{2,0},{3,1},{4,6},{5,7},{6,4},{7,5},{8,10},{9,11},{10,... | collective-permute-start | bytes 393224 | tf_op jit(solution)/shard_map/ppermute | solution.py:443
  38.2 15.9 %collective-permute-start.19 = (bf16[128,512]{1,0:T(8,128)(2,1)S(1)}, bf16[128,512]{1,0:T(8,128)(2,1)S(1)}, u32[]{:S(2)}, u32[]{:S(2)}) collective-permute-start(bf16[128,512]{1,0:T(8,128)(2,1)S(1)} %bundle.4.refs_3_), channel_id=1, source_target_pairs={{0,1},{1,0},{2,3},{3,2},{4,5},{5,4},{6,7},{7,6},{8,9},{9,8},{10,11... | collective-permute-start | bytes 393224 | tf_op jit(solution)/shard_map/ppermute | solution.py:443
  42.1 7.1 %collective-permute-start.14 = (bf16[128,512]{1,0:T(8,128)(2,1)S(1)}, bf16[128,512]{1,0:T(8,128)(2,1)S(1)}, u32[]{:S(2)}, u32[]{:S(2)}) collective-permute-start(bf16[128,512]{1,0:T(8,128)(2,1)S(1)} %add.14.refs_6_.refs_0_), channel_id=1, source_target_pairs={{0,1},{1,0},{2,3},{3,2},{4,5},{5,4},{6,7},{7,6},{8,9},{9,8},{10,11... | collective-permute-start | bytes 393224 | tf_op jit(solution)/shard_map/ppermute | solution.py:443
  42.9 12.4 %collective-permute-start.20 = (bf16[128,1024]{1,0:T(8,128)(2,1)S(1)}, bf16[128,1024]{1,0:T(8,128)(2,1)S(1)}, u32[]{:S(2)}, u32[]{:S(2)}) collective-permute-start(bf16[128,1024]{1,0:T(8,128)(2,1)S(1)} %second.4.refs_3_), channel_id=1, source_target_pairs={{0,24},{4,28},{8,16},{12,20},{16,8},{20,12},{24,0},{28,4},{1,25},{... | collective-permute-start | bytes 786440 | tf_op jit(solution)/shard_map/ppermute | solution.py:443
  46.0 7.3 %collective-permute-start.13 = (bf16[128,512]{1,0:T(8,128)(2,1)S(1)}, bf16[128,512]{1,0:T(8,128)(2,1)S(1)}, u32[]{:S(2)}, u32[]{:S(2)}) collective-permute-start(bf16[128,512]{1,0:T(8,128)(2,1)S(1)} %add.15.refs_6_.refs_0_), channel_id=1, source_target_pairs={{0,1},{1,0},{2,3},{3,2},{4,5},{5,4},{6,7},{7,6},{8,9},{9,8},{10,11... | collective-permute-start | bytes 393224 | tf_op jit(solution)/shard_map/ppermute | solution.py:443
  49.9 8.3 %collective-permute-start.18 = (bf16[64,1024]{1,0:T(8,128)(2,1)S(1)}, bf16[64,1024]{1,0:T(8,128)(2,1)S(1)}, u32[]{:S(2)}, u32[]{:S(2)}) collective-permute-start(bf16[64,1024]{1,0:T(8,128)(2,1)S(1)} %get-tuple-element.55), channel_id=1, source_target_pairs={{0,16},{4,20},{8,24},{12,28},{16,0},{20,4},{24,8},{28,12},{1,17},{... | collective-permute-start | bytes 393224 | tf_op jit(solution)/shard_map/ppermute | solution.py:443
  51.8 6.5 %collective-permute-start.17 = (bf16[64,1024]{1,0:T(8,128)(2,1)S(1)}, bf16[64,1024]{1,0:T(8,128)(2,1)S(1)}, u32[]{:S(2)}, u32[]{:S(2)}) collective-permute-start(bf16[64,1024]{1,0:T(8,128)(2,1)S(1)} %get-tuple-element.51.refs_6_), channel_id=1, source_target_pairs={{0,8},{4,12},{8,0},{12,4},{16,24},{20,28},{24,16},{28,20},{1,9},{5... | collective-permute-start | bytes 393224 | tf_op jit(solution)/shard_map/ppermute | solution.py:443
  54.0 4.8 %collective-permute-start.16 = (bf16[64,1024]{1,0:T(8,128)(2,1)S(1)}, bf16[64,1024]{1,0:T(8,128)(2,1)S(1)}, u32[]{:S(2)}, u32[]{:S(2)}) collective-permute-start(bf16[64,1024]{1,0:T(8,128)(2,1)S(1)} %get-tuple-element.53), channel_id=1, source_target_pairs={{0,20},{4,16},{8,28},{12,24},{16,4},{20,0},{24,12},{28,8},{1,21},{... | collective-permute-start | bytes 393224 | tf_op jit(solution)/shard_map/ppermute | solution.py:443
  54.1 5.3 %collective-permute-start.15 = (bf16[64,1024]{1,0:T(8,128)(2,1)S(1)}, bf16[64,1024]{1,0:T(8,128)(2,1)S(1)}, u32[]{:S(2)}, u32[]{:S(2)}) collective-permute-start(bf16[64,1024]{1,0:T(8,128)(2,1)S(1)} %get-tuple-element.52.refs_6_), channel_id=1, source_target_pairs={{0,12},{4,8},{8,4},{12,0},{16,28},{20,24},{24,20},{28,16},{1,13},{... | collective-permute-start | bytes 393224 | tf_op jit(solution)/shard_map/ppermute | solution.py:443
  55.4 4.3 %collective-permute-start.21 = (bf16[128,1024]{1,0:T(8,128)(2,1)S(1)}, bf16[128,1024]{1,0:T(8,128)(2,1)S(1)}, u32[]{:S(2)}, u32[]{:S(2)}) collective-permute-start(bf16[128,1024]{1,0:T(8,128)(2,1)S(1)} %bundle.5.refs_6_), channel_id=1, source_target_pairs={{0,4},{4,0},{8,12},{12,8},{16,20},{20,16},{24,28},{28,24},{1,5},{5... | collective-permute-start | bytes 786440 | tf_op jit(solution)/shard_map/ppermute | solution.py:443

commit v4 on v2

--- a/solution.py
+++ b/solution.py
@@ -12,14 +12,14 @@
 PARTS = (CHUNKS[2], CHUNKS[0] + CHUNKS[1], CHUNKS[3])
 ORDER = (
     ("first", 0), ("diagonal", 0), ("add", 0), ("prep", 0), ("turn", 0), ("first", 1),
-    ("first", 2), ("add", 0), ("add", 1), ("first", 3), ("add", 2), ("add", 1), ("down", 0),
-    ("add", 3), ("release", 0), ("add", 2), ("second", 1), ("add", 3), ("second", 0),
-    ("second", 2), ("cross", 0), ("second", 3), ("gather", 0), ("gather", 1),
+    ("first", 2), ("add", 0), ("add", 1), ("first", 3), ("add", 2), ("add", 1), ("add", 3),
+    ("down", 0), ("add", 2), ("release", 0), ("add", 3), ("second", 1), ("second", 2),
+    ("second", 3), ("second", 0), ("cross", 0), ("gather", 0), ("gather", 1),
 )
 HELD = (0,)
 COST = {
     "place": 10**10, "pack": 10**10, "rest": 1, "first": 1, "prep": 1, "turn": 1,
-    "add": 10**9, "release": 1, "pair": 1, "second": 10**10, "down": 1, "gather": 1, "finish": 1,
+    "add": 10**9, "release": 1, "pair": 1, "second": 10**10, "down": 1, "gather": 5 * 10**9, "finish": 1,
 }
 MIB = 1 << 20
 BF16, F32 = jnp.bfloat16, jnp.float32

time: 60.1 us -> 60 us (level)
  waiting for transfers between devices: 11.9 us -> 11.2 us
    ppermute x24, waiting for transfers between devices: 11.9 us -> 11.2 us  [swap(): return lax.ppermute(block, axis, [(i, i ^ k) for i in range(size)])]
where the time goes in v4:
time: 60 us; the launch traced here: 59.6 us
  starting transfers between devices  34 us (57%)
  Pallas kernels  13.5 us (22%)
  waiting for transfers between devices  11.2 us (19%)
  between operations  0.94 us (2%)
    ppermute x24, starting transfers between devices, swap(): return lax.ppermute(block, axis, [(i, i ^ k) for i in range(size)])  34 us
    pallas_call x28, Pallas kernels, call(): pl.pallas_call(run, name=name, out_shape=outs, in_specs=list(specs) + [AN...  13.5 us
    ppermute x24, waiting for transfers between devices, swap(): return lax.ppermute(block, axis, [(i, i ^ k) for i in range(size)])  11.2 us
  transfers between devices with their start and end apart: 24, of which 12 were waited for; matrix products, arithmetic and copies ran while one was open for 0% of the time, Pallas kernels for 18%

profile of v4, /device:TPU:0, one launch (start us, length us, event | category | flops | bytes accessed | tf_op | source)
XLA Modules:
  0.0 59.6 jit_solution(9013072787964743378)
XLA Ops:
  0.6 1.0 %place.1.refs_0_ = bf16[512,256]{1,0:T(8,128)(2,1)S(1)} custom-call(s32[1,256]{1,0:T(1,128)} %bitcast.14), custom_call_target="tpu_custom_call" | custom-call | flops 10000000000 | tf_op jit(solution)/shard_map/place/pallas_call | solution.py:41
  1.7 0.5 pack.1
  2.2 0.5 collective-permute-start
  2.7 0.3 rest.1
  3.1 0.8 %collective-permute-done.refs_2_.refs_1_ = bf16[128,1024]{1,0:T(8,128)(2,1)S(1)} collective-permute-done((bf16[128,1024]{1,0:T(8,128)(2,1)S(1)}, bf16[128,1024]{1,0:T(8,128)(2,1)S(1)}, u32[]{:S(2)}, u32[]{:S(2)}) %collective-permute-start) | collective-permute-done | bytes 262176 | tf_op jit(solution)/shard_map/ppermute | solution.py:449
  3.9 0.5 first.4
  4.4 3.0 %collective-permute-start.1 = (bf16[128,512]{1,0:T(8,128)(2,1)S(1)}, bf16[128,512]{1,0:T(8,128)(2,1)S(1)}, u32[]{:S(2)}, u32[]{:S(2)}) collective-permute-start(bf16[128,512]{1,0:T(8,128)(2,1)S(1)} %get-tuple-element.38.refs_2_), channel_id=1, source_target_pairs={{0,1},{1,0},{2,3},{3,2},{4,5},{5,4},{6,7},{7,6},{8,9},{9,8},{10,11... | collective-permute-start | bytes 393224 | tf_op jit(solution)/shard_map/ppermute | solution.py:449
  7.4 2.5 %collective-permute-start.5 = (bf16[128,1024]{1,0:T(8,128)(2,1)S(1)}, bf16[128,1024]{1,0:T(8,128)(2,1)S(1)}, u32[]{:S(2)}, u32[]{:S(2)}) collective-permute-start(bf16[128,1024]{1,0:T(8,128)(2,1)S(1)} %pair.2.refs_2_), channel_id=1, source_target_pairs={{0,24},{4,28},{8,16},{12,20},{16,8},{20,12},{24,0},{28,4},{1,25},{... | collective-permute-start | bytes 786440 | tf_op jit(solution)/shard_map/ppermute | solution.py:449
  9.9 0.5 collective-permute-start.3
  10.5 0.5 collective-permute-start.4
  11.0 0.2 collective-permute-done.1.refs_1_
  11.2 2.8 %collective-permute-start.2 = (bf16[128,512]{1,0:T(8,128)(2,1)S(1)}, bf16[128,512]{1,0:T(8,128)(2,1)S(1)}, u32[]{:S(2)}, u32[]{:S(2)}) collective-permute-start(bf16[128,512]{1,0:T(8,128)(2,1)S(1)} %add.8.refs_1_), channel_id=1, source_target_pairs={{0,2},{1,3},{2,0},{3,1},{4,6},{5,7},{6,4},{7,5},{8,10},{9,11},{10,... | collective-permute-start | bytes 393224 | tf_op jit(solution)/shard_map/ppermute | solution.py:449
  14.0 1.0 %prep.1 = (f32[512,1024]{1,0:T(8,128)S(1)}, f32[512,1024]{1,0:T(8,128)S(1)}, bf16[512,1024]{1,0:T(8,128)(2,1)S(1)}) custom-call(bf16[512,2048]{1,0:T(8,128)(2,1)S(1)} %copy-done.1, bf16[128,512]{1,0:T(8,128)(2,1)S(1)} %add.8.refs_1_), custom_call_target="tpu_custom_call" | custom-call | flops 1 | tf_op jit(solution)/shard_map/prep/pallas_call | solution.py:41
  15.1 1.3 %turn.1 = (bf16[1024,1024]{1,0:T(8,128)(2,1)S(1)}, bf16[1024,1024]{1,0:T(8,128)(2,1)S(1)}, bf16[256,128]{1,0:T(8,128)(2,1)S(1)}, bf16[256,256]{1,0:T(8,128)(2,1)S(1)}, bf16[256,128]{1,0:T(8,128)(2,1)S(1)}) custom-call(bf16[512,256]{1,0:T(8,128)(2,1)S(1)} %place.1.refs_0_, bf16[1024,1024]{1,0:T(8,128)(2,1)S(1)} %bitcast.10, bf16[1024,1024]{1,0:T(8,128)(2,1)S(1)} %bitcast.11, ...), custom_call_target="tpu_custom_call" | custom-call | flops 1 | tf_op jit(solution)/shard_map/turn/pallas_call | solution.py:41
  16.4 1.2 %collective-permute-done.5.refs_1_.refs_7_ = bf16[128,1024]{1,0:T(8,128)(2,1)S(1)} collective-permute-done((bf16[128,1024]{1,0:T(8,128)(2,1)S(1)}, bf16[128,1024]{1,0:T(8,128)(2,1)S(1)}, u32[]{:S(2)}, u32[]{:S(2)}) %collective-permute-start.5) | collective-permute-done | bytes 262176 | tf_op jit(solution)/shard_map/ppermute | solution.py:449
  17.6 0.5 first.5
  18.1 0.5 collective-permute-start.9
  18.6 0.8 %collective-permute-done.3.refs_1_.refs_3_ = bf16[64,1024]{1,0:T(8,128)(2,1)S(1)} collective-permute-done((bf16[64,1024]{1,0:T(8,128)(2,1)S(1)}, bf16[64,1024]{1,0:T(8,128)(2,1)S(1)}, u32[]{:S(2)}, u32[]{:S(2)}) %collective-permute-start.3) | collective-permute-done | bytes 131104 | tf_op jit(solution)/shard_map/ppermute | solution.py:449
  19.4 2.0 %collective-permute-start.8 = (bf16[64,1024]{1,0:T(8,128)(2,1)S(1)}, bf16[64,1024]{1,0:T(8,128)(2,1)S(1)}, u32[]{:S(2)}, u32[]{:S(2)}) collective-permute-start(bf16[64,1024]{1,0:T(8,128)(2,1)S(1)} %get-tuple-element.50), channel_id=1, source_target_pairs={{0,20},{4,16},{8,28},{12,24},{16,4},{20,0},{24,12},{28,8},{1,21},{... | collective-permute-start | bytes 393224 | tf_op jit(solution)/shard_map/ppermute | solution.py:449
  21.4 0.5 first.6
  21.8 1.6 %collective-permute-start.6 = (bf16[128,512]{1,0:T(8,128)(2,1)S(1)}, bf16[128,512]{1,0:T(8,128)(2,1)S(1)}, u32[]{:S(2)}, u32[]{:S(2)}) collective-permute-start(bf16[128,512]{1,0:T(8,128)(2,1)S(1)} %get-tuple-element.47.refs_3_), channel_id=1, source_target_pairs={{0,1},{1,0},{2,3},{3,2},{4,5},{5,4},{6,7},{7,6},{8,9},{9,8},{10,11... | collective-permute-start | bytes 393224 | tf_op jit(solution)/shard_map/ppermute | solution.py:449
  23.6 2.7 %collective-permute-start.12 = (bf16[128,512]{1,0:T(8,128)(2,1)S(1)}, bf16[128,512]{1,0:T(8,128)(2,1)S(1)}, u32[]{:S(2)}, u32[]{:S(2)}) collective-permute-start(bf16[128,512]{1,0:T(8,128)(2,1)S(1)} %add.10.refs_3_), channel_id=1, source_target_pairs={{0,2},{1,3},{2,0},{3,1},{4,6},{5,7},{6,4},{7,5},{8,10},{9,11},{10,... | collective-permute-start | bytes 393224 | tf_op jit(solution)/shard_map/ppermute | solution.py:449
  26.3 0.5 first.7
  26.7 0.6 %collective-permute-start.11 = (bf16[128,512]{1,0:T(8,128)(2,1)S(1)}, bf16[128,512]{1,0:T(8,128)(2,1)S(1)}, u32[]{:S(2)}, u32[]{:S(2)}) collective-permute-start(bf16[128,512]{1,0:T(8,128)(2,1)S(1)} %get-tuple-element.52.refs_2_), channel_id=1, source_target_pairs={{0,1},{1,0},{2,3},{3,2},{4,5},{5,4},{6,7},{7,6},{8,9},{9,8},{10,11... | collective-permute-start | bytes 393224 | tf_op jit(solution)/shard_map/ppermute | solution.py:449
  27.4 0.8 %collective-permute-done.6.refs_1_ = bf16[128,512]{1,0:T(8,128)(2,1)S(1)} collective-permute-done((bf16[128,512]{1,0:T(8,128)(2,1)S(1)}, bf16[128,512]{1,0:T(8,128)(2,1)S(1)}, u32[]{:S(2)}, u32[]{:S(2)}) %collective-permute-start.6) | collective-permute-done | bytes 131104 | tf_op jit(solution)/shard_map/ppermute | solution.py:449
  28.2 2.1 %collective-permute-start.10 = (bf16[128,512]{1,0:T(8,128)(2,1)S(1)}, bf16[128,512]{1,0:T(8,128)(2,1)S(1)}, u32[]{:S(2)}, u32[]{:S(2)}) collective-permute-start(bf16[128,512]{1,0:T(8,128)(2,1)S(1)} %add.11.refs_3_), channel_id=1, source_target_pairs={{0,2},{1,3},{2,0},{3,1},{4,6},{5,7},{6,4},{7,5},{8,10},{9,11},{10,... | collective-permute-start | bytes 393224 | tf_op jit(solution)/shard_map/ppermute | solution.py:449
  30.3 1.5 %collective-permute-done.12.refs_2_ = bf16[128,512]{1,0:T(8,128)(2,1)S(1)} collective-permute-done((bf16[128,512]{1,0:T(8,128)(2,1)S(1)}, bf16[128,512]{1,0:T(8,128)(2,1)S(1)}, u32[]{:S(2)}, u32[]{:S(2)}) %collective-permute-start.12) | collective-permute-done | bytes 131104 | tf_op jit(solution)/shard_map/ppermute | solution.py:449
  31.8 3.2 %collective-permute-done.11.refs_1_ = bf16[128,512]{1,0:T(8,128)(2,1)S(1)} collective-permute-done((bf16[128,512]{1,0:T(8,128)(2,1)S(1)}, bf16[128,512]{1,0:T(8,128)(2,1)S(1)}, u32[]{:S(2)}, u32[]{:S(2)}) %collective-permute-start.11) | collective-permute-done | bytes 131104 | tf_op jit(solution)/shard_map/ppermute | solution.py:449
  35.1 0.6 %collective-permute-start.14 = (bf16[128,512]{1,0:T(8,128)(2,1)S(1)}, bf16[128,512]{1,0:T(8,128)(2,1)S(1)}, u32[]{:S(2)}, u32[]{:S(2)}) collective-permute-start(bf16[128,512]{1,0:T(8,128)(2,1)S(1)} %add.13.refs_8_), channel_id=1, source_target_pairs={{0,2},{1,3},{2,0},{3,1},{4,6},{5,7},{6,4},{7,5},{8,10},{9,11},{10,... | collective-permute-start | bytes 393224 | tf_op jit(solution)/shard_map/ppermute | solution.py:449
  35.7 2.4 %collective-permute-start.17 = (bf16[128,512]{1,0:T(8,128)(2,1)S(1)}, bf16[128,512]{1,0:T(8,128)(2,1)S(1)}, u32[]{:S(2)}, u32[]{:S(2)}) collective-permute-start(bf16[128,512]{1,0:T(8,128)(2,1)S(1)} %add.12.refs_2_.refs_0_), channel_id=1, source_target_pairs={{0,1},{1,0},{2,3},{3,2},{4,5},{5,4},{6,7},{7,6},{8,9},{9,8},{10,11... | collective-permute-start | bytes 393224 | tf_op jit(solution)/shard_map/ppermute | solution.py:449
  38.1 2.5 %down.1 = (f32[1024,1024]{1,0:T(8,128)}, f32[8,128]{1,0:T(8,128)S(1)}) custom-call(bf16[512,1024]{1,0:T(8,128)(2,1)S(1)} %get-tuple-element.40.refs_3_.refs_0_, bf16[64,1024]{1,0:T(8,128)(2,1)S(1)} %get-tuple-element.36.refs_1_.refs_3_, bf16[128,1024]{1,0:T(8,128)(2,1)S(1)} %collective-permute-done.refs_2_.refs_1_, ...), custom_call_target="tpu_custom_call" | custom-call | flops 1 | tf_op jit(solution)/shard_map/down/pallas_call | solution.py:41
  40.8 2.0 %collective-permute-start.13 = (bf16[128,512]{1,0:T(8,128)(2,1)S(1)}, bf16[128,512]{1,0:T(8,128)(2,1)S(1)}, u32[]{:S(2)}, u32[]{:S(2)}) collective-permute-start(bf16[128,512]{1,0:T(8,128)(2,1)S(1)} %release.1.refs_3_.refs_0_), channel_id=1, source_target_pairs={{0,1},{1,0},{2,3},{3,2},{4,5},{5,4},{6,7},{7,6},{8,9},{9,8},{10,11... | collective-permute-start | bytes 393224 | tf_op jit(solution)/shard_map/ppermute | solution.py:449
  43.0 0.2 collective-permute-start.15
  43.2 0.7 %second.4.refs_6_ = bf16[128,1024]{1,0:T(8,128)(2,1)S(1)} custom-call(bf16[128,512]{1,0:T(8,128)(2,1)S(1)} %add.12.refs_2_.refs_0_, bf16[128,512]{1,0:T(8,128)(2,1)S(1)} %collective-permute-done.17.refs_1_, f32[512,1024]{1,0:T(8,128)S(1)} %get-tuple-element.55.refs_2_, f32[512,1024]{1,0:T(8,128)S(1)} %get-tuple-element.56.refs_3_, ...), custom_call_target="tpu_custom_call" | custom-call | flops 10000000000 | tf_op jit(solution)/shard_map/second/pallas_call | solution.py:41
  43.9 2.8 %collective-permute-start.18 = (bf16[128,1024]{1,0:T(8,128)(2,1)S(1)}, bf16[128,1024]{1,0:T(8,128)(2,1)S(1)}, u32[]{:S(2)}, u32[]{:S(2)}) collective-permute-start(bf16[128,1024]{1,0:T(8,128)(2,1)S(1)} %second.4.refs_6_), channel_id=1, source_target_pairs={{0,24},{4,28},{8,16},{12,20},{16,8},{20,12},{24,0},{28,4},{1,25},{... | collective-permute-start | bytes 786440 | tf_op jit(solution)/shard_map/ppermute | solution.py:449
  46.7 0.5 collective-permute-done.16.refs_1_
  47.2 0.7 %second.5 = (bf16[64,1024]{1,0:T(8,128)(2,1)S(1)}, bf16[64,1024]{1,0:T(8,128)(2,1)S(1)}) custom-call(bf16[128,512]{1,0:T(8,128)(2,1)S(1)} %add.14.refs_1_.refs_0_, bf16[128,512]{1,0:T(8,128)(2,1)S(1)} %collective-permute-done.16.refs_1_, f32[512,1024]{1,0:T(8,128)S(1)} %get-tuple-element.55.refs_2_, f32[512,1024]{1,0:T(8,128)S(1)} %get-tuple-element.56.refs_3_, ...), custom_call_target="tpu_custom_call" | custom-call | flops 10000000000 | tf_op jit(solution)/shard_map/second/pallas_call | solution.py:41
  48.0 2.3 %collective-permute-start.20 = (bf16[64,1024]{1,0:T(8,128)(2,1)S(1)}, bf16[64,1024]{1,0:T(8,128)(2,1)S(1)}, u32[]{:S(2)}, u32[]{:S(2)}) collective-permute-start(bf16[64,1024]{1,0:T(8,128)(2,1)S(1)} %get-tuple-element.58.refs_6_), channel_id=1, source_target_pairs={{0,8},{4,12},{8,0},{12,4},{16,24},{20,28},{24,16},{28,20},{1,9},{5... | collective-permute-start | bytes 393224 | tf_op jit(solution)/shard_map/ppermute | solution.py:449
  50.3 1.0 %collective-permute-start.21 = (bf16[64,1024]{1,0:T(8,128)(2,1)S(1)}, bf16[64,1024]{1,0:T(8,128)(2,1)S(1)}, u32[]{:S(2)}, u32[]{:S(2)}) collective-permute-start(bf16[64,1024]{1,0:T(8,128)(2,1)S(1)} %get-tuple-element.63), channel_id=1, source_target_pairs={{0,16},{4,20},{8,24},{12,28},{16,0},{20,4},{24,8},{28,12},{1,17},{... | collective-permute-start | bytes 393224 | tf_op jit(solution)/shard_map/ppermute | solution.py:449
  51.3 0.2 collective-permute-done.15.refs_1_
  51.5 0.7 %second.6 = (bf16[64,1024]{1,0:T(8,128)(2,1)S(1)}, bf16[64,1024]{1,0:T(8,128)(2,1)S(1)}) custom-call(bf16[128,512]{1,0:T(8,128)(2,1)S(1)} %add.15.refs_6_.refs_0_, bf16[128,512]{1,0:T(8,128)(2,1)S(1)} %collective-permute-done.15.refs_1_, f32[512,1024]{1,0:T(8,128)S(1)} %get-tuple-element.55.refs_2_, f32[512,1024]{1,0:T(8,128)S(1)} %get-tuple-element.56.refs_3_, ...), custom_call_target="tpu_custom_call" | custom-call | flops 10000000000 | tf_op jit(solution)/shard_map/second/pallas_call | solution.py:41
  52.3 3.0 %collective-permute-start.23 = (bf16[64,1024]{1,0:T(8,128)(2,1)S(1)}, bf16[64,1024]{1,0:T(8,128)(2,1)S(1)}, u32[]{:S(2)}, u32[]{:S(2)}) collective-permute-start(bf16[64,1024]{1,0:T(8,128)(2,1)S(1)} %get-tuple-element.64), channel_id=1, source_target_pairs={{0,20},{4,16},{8,28},{12,24},{16,4},{20,0},{24,12},{28,8},{1,21},{... | collective-permute-start | bytes 393224 | tf_op jit(solution)/shard_map/ppermute | solution.py:449
  55.3 0.7 %second.7 = (bf16[64,1024]{1,0:T(8,128)(2,1)S(1)}, bf16[64,1024]{1,0:T(8,128)(2,1)S(1)}) custom-call(bf16[128,512]{1,0:T(8,128)(2,1)S(1)} %release.1.refs_3_.refs_0_, bf16[128,512]{1,0:T(8,128)(2,1)S(1)} %collective-permute-done.13.refs_1_, f32[512,1024]{1,0:T(8,128)S(1)} %get-tuple-element.55.refs_2_, f32[512,1024]{1,0:T(8,128)S(1)} %get-tuple-element.56.refs_3_, ...), custom_call_target="tpu_custom_call" | custom-call | flops 10000000000 | tf_op jit(solution)/shard_map/second/pallas_call | solution.py:41
  56.2 0.3 gather.2.refs_4_.refs_5_
  56.5 1.2 %collective-permute-done.19.refs_2_ = bf16[128,1024]{1,0:T(8,128)(2,1)S(1)} collective-permute-done((bf16[128,1024]{1,0:T(8,128)(2,1)S(1)}, bf16[128,1024]{1,0:T(8,128)(2,1)S(1)}, u32[]{:S(2)}, u32[]{:S(2)}) %collective-permute-start.19) | collective-permute-done | bytes 262176 | tf_op jit(solution)/shard_map/ppermute | solution.py:449
  57.7 0.3 gather.3.refs_1_.refs_4_
  58.1 0.5 collective-permute-done.23.refs_3_
  58.6 1.0 %finish.1 = bf16[256,1024]{1,0:T(8,128)(2,1)} custom-call(bf16[256,128]{1,0:T(8,128)(2,1)S(1)} %get-tuple-element.41.refs_0_, bf16[256,1024]{1,0:T(8,128)(2,1)S(1)} %gather.3.refs_1_.refs_4_, bf16[64,1024]{1,0:T(8,128)(2,1)S(1)} %collective-permute-done.22.refs_2_, bf16[64,1024]{1,0:T(8,128)(2,1)S(1)} %collective-permute-done.23.refs_3_, ...), custom_call_target="tpu_custom_call" | custom-call | flops 1 | tf_op jit(solution)/shard_map/finish/pallas_call | solution.py:41
  (40 shorter events, 0.8 us)
Async XLA Ops:
  0.6 1.1 %copy-start.4 = (bf16[256,1024]{1,0:T(8,128)(2,1)S(1)}, bf16[256,1024]{1,0:T(8,128)(2,1)}, u32[]{:S(2)}) copy-start(bf16[256,1024]{1,0:T(8,128)(2,1)} %refs_2_.1) | copy-start | bytes 1572868
  0.6 1.1 %copy-start.5 = (bf16[256,8]{0,1:T(8,128)(2,1)S(1)}, bf16[256,8]{0,1:T(8,128)(2,1)}, u32[]{:S(2)}) copy-start(bf16[256,8]{0,1:T(8,128)(2,1)} %param.8) | copy-start | bytes 12292
  1.7 2.2 %copy-start = (bf16[1,1024,1024]{2,1,0:T(8,128)(2,1)S(1)}, bf16[1,1024,1024]{2,1,0:T(8,128)(2,1)}, u32[]{:S(2)}) copy-start(bf16[1,1024,1024]{2,1,0:T(8,128)(2,1)} %param.13) | copy-start | bytes 6291460
  2.2 1.7 %collective-permute-start = (bf16[128,1024]{1,0:T(8,128)(2,1)S(1)}, bf16[128,1024]{1,0:T(8,128)(2,1)S(1)}, u32[]{:S(2)}, u32[]{:S(2)}) collective-permute-start(bf16[128,1024]{1,0:T(8,128)(2,1)S(1)} %get-tuple-element.35.refs_2_), channel_id=1, source_target_pairs={{0,4},{4,0},{8,12},{12,8},{16,20},{20,16},{24,28},{28,24},{1,5},{5... | collective-permute-start | bytes 786440 | tf_op jit(solution)/shard_map/ppermute | solution.py:449
  4.4 6.8 %collective-permute-start.1 = (bf16[128,512]{1,0:T(8,128)(2,1)S(1)}, bf16[128,512]{1,0:T(8,128)(2,1)S(1)}, u32[]{:S(2)}, u32[]{:S(2)}) collective-permute-start(bf16[128,512]{1,0:T(8,128)(2,1)S(1)} %get-tuple-element.38.refs_2_), channel_id=1, source_target_pairs={{0,1},{1,0},{2,3},{3,2},{4,5},{5,4},{6,7},{7,6},{8,9},{9,8},{10,11... | collective-permute-start | bytes 393224 | tf_op jit(solution)/shard_map/ppermute | solution.py:449
  7.4 6.7 %copy-start.1 = (bf16[512,2048]{1,0:T(8,128)(2,1)S(1)}, bf16[512,2048]{1,0:T(8,128)(2,1)}, u32[]{:S(2)}) copy-start(bf16[512,2048]{1,0:T(8,128)(2,1)} %refs_0_.1) | copy-start | bytes 6291460
  7.4 10.2 %collective-permute-start.5 = (bf16[128,1024]{1,0:T(8,128)(2,1)S(1)}, bf16[128,1024]{1,0:T(8,128)(2,1)S(1)}, u32[]{:S(2)}, u32[]{:S(2)}) collective-permute-start(bf16[128,1024]{1,0:T(8,128)(2,1)S(1)} %pair.2.refs_2_), channel_id=1, source_target_pairs={{0,24},{4,28},{8,16},{12,20},{16,8},{20,12},{24,0},{28,4},{1,25},{... | collective-permute-start | bytes 786440 | tf_op jit(solution)/shard_map/ppermute | solution.py:449
  9.9 9.4 %collective-permute-start.3 = (bf16[64,1024]{1,0:T(8,128)(2,1)S(1)}, bf16[64,1024]{1,0:T(8,128)(2,1)S(1)}, u32[]{:S(2)}, u32[]{:S(2)}) collective-permute-start(bf16[64,1024]{1,0:T(8,128)(2,1)S(1)} %get-tuple-element.43), channel_id=1, source_target_pairs={{0,8},{4,12},{8,0},{12,4},{16,24},{20,28},{24,16},{28,20},{1,9},{5... | collective-permute-start | bytes 393224 | tf_op jit(solution)/shard_map/ppermute | solution.py:449
  10.5 10.9 %collective-permute-start.4 = (bf16[64,1024]{1,0:T(8,128)(2,1)S(1)}, bf16[64,1024]{1,0:T(8,128)(2,1)S(1)}, u32[]{:S(2)}, u32[]{:S(2)}) collective-permute-start(bf16[64,1024]{1,0:T(8,128)(2,1)S(1)} %get-tuple-element.44), channel_id=1, source_target_pairs={{0,16},{4,20},{8,24},{12,28},{16,0},{20,4},{24,8},{28,12},{1,17},{... | collective-permute-start | bytes 393224 | tf_op jit(solution)/shard_map/ppermute | solution.py:449
  11.2 3.9 %copy-start.2 = (bf16[1,1024,1024]{2,1,0:T(8,128)(2,1)S(1)}, bf16[1,1024,1024]{2,1,0:T(8,128)(2,1)}, u32[]{:S(2)}) copy-start(bf16[1,1024,1024]{2,1,0:T(8,128)(2,1)} %param.11) | copy-start | bytes 6291460
  11.2 3.9 %copy-start.3 = (bf16[1,1024,1024]{2,1,0:T(8,128)(2,1)S(1)}, bf16[1,1024,1024]{2,1,0:T(8,128)(2,1)}, u32[]{:S(2)}) copy-start(bf16[1,1024,1024]{2,1,0:T(8,128)(2,1)} %param.12) | copy-start | bytes 6291460
  11.2 12.3 %collective-permute-start.2 = (bf16[128,512]{1,0:T(8,128)(2,1)S(1)}, bf16[128,512]{1,0:T(8,128)(2,1)S(1)}, u32[]{:S(2)}, u32[]{:S(2)}) collective-permute-start(bf16[128,512]{1,0:T(8,128)(2,1)S(1)} %add.8.refs_1_), channel_id=1, source_target_pairs={{0,2},{1,3},{2,0},{3,1},{4,6},{5,7},{6,4},{7,5},{8,10},{9,11},{10,... | collective-permute-start | bytes 393224 | tf_op jit(solution)/shard_map/ppermute | solution.py:449
  18.1 5.5 %collective-permute-start.9 = (bf16[128,512]{1,0:T(8,128)(2,1)S(1)}, bf16[128,512]{1,0:T(8,128)(2,1)S(1)}, u32[]{:S(2)}, u32[]{:S(2)}) collective-permute-start(bf16[128,512]{1,0:T(8,128)(2,1)S(1)} %get-tuple-element.46.refs_3_), channel_id=1, source_target_pairs={{0,1},{1,0},{2,3},{3,2},{4,5},{5,4},{6,7},{7,6},{8,9},{9,8},{10,11... | collective-permute-start | bytes 393224 | tf_op jit(solution)/shard_map/ppermute | solution.py:449
  18.6 7.7 %collective-permute-start.7 = (bf16[64,1024]{1,0:T(8,128)(2,1)S(1)}, bf16[64,1024]{1,0:T(8,128)(2,1)S(1)}, u32[]{:S(2)}, u32[]{:S(2)}) collective-permute-start(bf16[64,1024]{1,0:T(8,128)(2,1)S(1)} %get-tuple-element.49), channel_id=1, source_target_pairs={{0,12},{4,8},{8,4},{12,0},{16,28},{20,24},{24,20},{28,16},{1,13},{... | collective-permute-start | bytes 393224 | tf_op jit(solution)/shard_map/ppermute | solution.py:449
  19.4 6.9 %collective-permute-start.8 = (bf16[64,1024]{1,0:T(8,128)(2,1)S(1)}, bf16[64,1024]{1,0:T(8,128)(2,1)S(1)}, u32[]{:S(2)}, u32[]{:S(2)}) collective-permute-start(bf16[64,1024]{1,0:T(8,128)(2,1)S(1)} %get-tuple-element.50), channel_id=1, source_target_pairs={{0,20},{4,16},{8,28},{12,24},{16,4},{20,0},{24,12},{28,8},{1,21},{... | collective-permute-start | bytes 393224 | tf_op jit(solution)/shard_map/ppermute | solution.py:449
  21.8 6.4 %collective-permute-start.6 = (bf16[128,512]{1,0:T(8,128)(2,1)S(1)}, bf16[128,512]{1,0:T(8,128)(2,1)S(1)}, u32[]{:S(2)}, u32[]{:S(2)}) collective-permute-start(bf16[128,512]{1,0:T(8,128)(2,1)S(1)} %get-tuple-element.47.refs_3_), channel_id=1, source_target_pairs={{0,1},{1,0},{2,3},{3,2},{4,5},{5,4},{6,7},{7,6},{8,9},{9,8},{10,11... | collective-permute-start | bytes 393224 | tf_op jit(solution)/shard_map/ppermute | solution.py:449
  23.6 8.2 %collective-permute-start.12 = (bf16[128,512]{1,0:T(8,128)(2,1)S(1)}, bf16[128,512]{1,0:T(8,128)(2,1)S(1)}, u32[]{:S(2)}, u32[]{:S(2)}) collective-permute-start(bf16[128,512]{1,0:T(8,128)(2,1)S(1)} %add.10.refs_3_), channel_id=1, source_target_pairs={{0,2},{1,3},{2,0},{3,1},{4,6},{5,7},{6,4},{7,5},{8,10},{9,11},{10,... | collective-permute-start | bytes 393224 | tf_op jit(solution)/shard_map/ppermute | solution.py:449
  26.7 8.3 %collective-permute-start.11 = (bf16[128,512]{1,0:T(8,128)(2,1)S(1)}, bf16[128,512]{1,0:T(8,128)(2,1)S(1)}, u32[]{:S(2)}, u32[]{:S(2)}) collective-permute-start(bf16[128,512]{1,0:T(8,128)(2,1)S(1)} %get-tuple-element.52.refs_2_), channel_id=1, source_target_pairs={{0,1},{1,0},{2,3},{3,2},{4,5},{5,4},{6,7},{7,6},{8,9},{9,8},{10,11... | collective-permute-start | bytes 393224 | tf_op jit(solution)/shard_map/ppermute | solution.py:449
  28.2 12.4 %collective-permute-start.10 = (bf16[128,512]{1,0:T(8,128)(2,1)S(1)}, bf16[128,512]{1,0:T(8,128)(2,1)S(1)}, u32[]{:S(2)}, u32[]{:S(2)}) collective-permute-start(bf16[128,512]{1,0:T(8,128)(2,1)S(1)} %add.11.refs_3_), channel_id=1, source_target_pairs={{0,2},{1,3},{2,0},{3,1},{4,6},{5,7},{6,4},{7,5},{8,10},{9,11},{10,... | collective-permute-start | bytes 393224 | tf_op jit(solution)/shard_map/ppermute | solution.py:449
  35.1 7.9 %collective-permute-start.14 = (bf16[128,512]{1,0:T(8,128)(2,1)S(1)}, bf16[128,512]{1,0:T(8,128)(2,1)S(1)}, u32[]{:S(2)}, u32[]{:S(2)}) collective-permute-start(bf16[128,512]{1,0:T(8,128)(2,1)S(1)} %add.13.refs_8_), channel_id=1, source_target_pairs={{0,2},{1,3},{2,0},{3,1},{4,6},{5,7},{6,4},{7,5},{8,10},{9,11},{10,... | collective-permute-start | bytes 393224 | tf_op jit(solution)/shard_map/ppermute | solution.py:449
  35.7 7.5 %collective-permute-start.17 = (bf16[128,512]{1,0:T(8,128)(2,1)S(1)}, bf16[128,512]{1,0:T(8,128)(2,1)S(1)}, u32[]{:S(2)}, u32[]{:S(2)}) collective-permute-start(bf16[128,512]{1,0:T(8,128)(2,1)S(1)} %add.12.refs_2_.refs_0_), channel_id=1, source_target_pairs={{0,1},{1,0},{2,3},{3,2},{4,5},{5,4},{6,7},{7,6},{8,9},{9,8},{10,11... | collective-permute-start | bytes 393224 | tf_op jit(solution)/shard_map/ppermute | solution.py:449
  40.7 6.5 %collective-permute-start.16 = (bf16[128,512]{1,0:T(8,128)(2,1)S(1)}, bf16[128,512]{1,0:T(8,128)(2,1)S(1)}, u32[]{:S(2)}, u32[]{:S(2)}) collective-permute-start(bf16[128,512]{1,0:T(8,128)(2,1)S(1)} %add.14.refs_1_.refs_0_), channel_id=1, source_target_pairs={{0,1},{1,0},{2,3},{3,2},{4,5},{5,4},{6,7},{7,6},{8,9},{9,8},{10,11... | collective-permute-start | bytes 393224 | tf_op jit(solution)/shard_map/ppermute | solution.py:449
  40.8 11.5 %collective-permute-start.13 = (bf16[128,512]{1,0:T(8,128)(2,1)S(1)}, bf16[128,512]{1,0:T(8,128)(2,1)S(1)}, u32[]{:S(2)}, u32[]{:S(2)}) collective-permute-start(bf16[128,512]{1,0:T(8,128)(2,1)S(1)} %release.1.refs_3_.refs_0_), channel_id=1, source_target_pairs={{0,1},{1,0},{2,3},{3,2},{4,5},{5,4},{6,7},{7,6},{8,9},{9,8},{10,11... | collective-permute-start | bytes 393224 | tf_op jit(solution)/shard_map/ppermute | solution.py:449
  43.0 8.5 %collective-permute-start.15 = (bf16[128,512]{1,0:T(8,128)(2,1)S(1)}, bf16[128,512]{1,0:T(8,128)(2,1)S(1)}, u32[]{:S(2)}, u32[]{:S(2)}) collective-permute-start(bf16[128,512]{1,0:T(8,128)(2,1)S(1)} %add.15.refs_6_.refs_0_), channel_id=1, source_target_pairs={{0,1},{1,0},{2,3},{3,2},{4,5},{5,4},{6,7},{7,6},{8,9},{9,8},{10,11... | collective-permute-start | bytes 393224 | tf_op jit(solution)/shard_map/ppermute | solution.py:449
  43.9 12.2 %collective-permute-start.18 = (bf16[128,1024]{1,0:T(8,128)(2,1)S(1)}, bf16[128,1024]{1,0:T(8,128)(2,1)S(1)}, u32[]{:S(2)}, u32[]{:S(2)}) collective-permute-start(bf16[128,1024]{1,0:T(8,128)(2,1)S(1)} %second.4.refs_6_), channel_id=1, source_target_pairs={{0,24},{4,28},{8,16},{12,20},{16,8},{20,12},{24,0},{28,4},{1,25},{... | collective-permute-start | bytes 786440 | tf_op jit(solution)/shard_map/ppermute | solution.py:449
  48.0 8.2 %collective-permute-start.20 = (bf16[64,1024]{1,0:T(8,128)(2,1)S(1)}, bf16[64,1024]{1,0:T(8,128)(2,1)S(1)}, u32[]{:S(2)}, u32[]{:S(2)}) collective-permute-start(bf16[64,1024]{1,0:T(8,128)(2,1)S(1)} %get-tuple-element.58.refs_6_), channel_id=1, source_target_pairs={{0,8},{4,12},{8,0},{12,4},{16,24},{20,28},{24,16},{28,20},{1,9},{5... | collective-permute-start | bytes 393224 | tf_op jit(solution)/shard_map/ppermute | solution.py:449
  50.3 5.9 %collective-permute-start.21 = (bf16[64,1024]{1,0:T(8,128)(2,1)S(1)}, bf16[64,1024]{1,0:T(8,128)(2,1)S(1)}, u32[]{:S(2)}, u32[]{:S(2)}) collective-permute-start(bf16[64,1024]{1,0:T(8,128)(2,1)S(1)} %get-tuple-element.63), channel_id=1, source_target_pairs={{0,16},{4,20},{8,24},{12,28},{16,0},{20,4},{24,8},{28,12},{1,17},{... | collective-permute-start | bytes 393224 | tf_op jit(solution)/shard_map/ppermute | solution.py:449
  52.2 5.8 %collective-permute-start.22 = (bf16[64,1024]{1,0:T(8,128)(2,1)S(1)}, bf16[64,1024]{1,0:T(8,128)(2,1)S(1)}, u32[]{:S(2)}, u32[]{:S(2)}) collective-permute-start(bf16[64,1024]{1,0:T(8,128)(2,1)S(1)} %get-tuple-element.59.refs_6_), channel_id=1, source_target_pairs={{0,12},{4,8},{8,4},{12,0},{16,28},{20,24},{24,20},{28,16},{1,13},{... | collective-permute-start | bytes 393224 | tf_op jit(solution)/shard_map/ppermute | solution.py:449
  52.3 6.3 %collective-permute-start.23 = (bf16[64,1024]{1,0:T(8,128)(2,1)S(1)}, bf16[64,1024]{1,0:T(8,128)(2,1)S(1)}, u32[]{:S(2)}, u32[]{:S(2)}) collective-permute-start(bf16[64,1024]{1,0:T(8,128)(2,1)S(1)} %get-tuple-element.64), channel_id=1, source_target_pairs={{0,20},{4,16},{8,28},{12,24},{16,4},{20,0},{24,12},{28,8},{1,21},{... | collective-permute-start | bytes 393224 | tf_op jit(solution)/shard_map/ppermute | solution.py:449
  56.1 1.6 %collective-permute-start.19 = (bf16[128,1024]{1,0:T(8,128)(2,1)S(1)}, bf16[128,1024]{1,0:T(8,128)(2,1)S(1)}, u32[]{:S(2)}, u32[]{:S(2)}) collective-permute-start(bf16[128,1024]{1,0:T(8,128)(2,1)S(1)} %pair.3.refs_3_), channel_id=1, source_target_pairs={{0,4},{4,0},{8,12},{12,8},{16,20},{20,16},{24,28},{28,24},{1,5},{5... | collective-permute-start | bytes 786440 | tf_op jit(solution)/shard_map/ppermute | solution.py:449

commit v5 on v4

--- a/solution.py
+++ b/solution.py
@@ -13,7 +13,7 @@
 ORDER = (
     ("first", 0), ("diagonal", 0), ("add", 0), ("prep", 0), ("turn", 0), ("first", 1),
     ("first", 2), ("add", 0), ("add", 1), ("first", 3), ("add", 2), ("add", 1), ("add", 3),
-    ("down", 0), ("add", 2), ("release", 0), ("add", 3), ("second", 1), ("second", 2),
+    ("down", 0), ("add", 2), ("second", 1), ("add", 3), ("release", 0), ("second", 2),
     ("second", 3), ("second", 0), ("cross", 0), ("gather", 0), ("gather", 1),
 )
 HELD = (0,)

time: 60 us -> 58.6 us (0.977)
  starting transfers between devices: 34 us -> 30.1 us
  waiting for transfers between devices: 11.2 us -> 13.8 us
    ppermute x24, starting transfers between devices: 34 us -> 30.1 us  [swap(): return lax.ppermute(block, axis, [(i, i ^ k) for i in range(size)])]
    ppermute x24, waiting for transfers between devices: 11.2 us -> 13.8 us  [swap(): return lax.ppermute(block, axis, [(i, i ^ k) for i in range(size)])]
  transfers between devices with their start and end apart: 24 -> 24, of which waited for: 12 -> 13; matrix products, arithmetic and copies ran while one was open for 0% -> 0% of each run, Pallas kernels for 18% -> 18%
where the time goes in v5:
time: 58.6 us; the launch traced here: 58.4 us
  starting transfers between devices  30.1 us (51%)
  waiting for transfers between devices  13.8 us (24%)
  Pallas kernels  13.5 us (23%)
  between operations  0.9 us (2%)
    ppermute x24, starting transfers between devices, swap(): return lax.ppermute(block, axis, [(i, i ^ k) for i in range(size)])  30.1 us
    ppermute x24, waiting for transfers between devices, swap(): return lax.ppermute(block, axis, [(i, i ^ k) for i in range(size)])  13.8 us
    pallas_call x28, Pallas kernels, call(): pl.pallas_call(run, name=name, out_shape=outs, in_specs=list(specs) + [AN...  13.5 us
  transfers between devices with their start and end apart: 24, of which 13 were waited for; matrix products, arithmetic and copies ran while one was open for 0% of the time, Pallas kernels for 18%

profile of v5, /device:TPU:0, one launch (start us, length us, event | category | flops | bytes accessed | tf_op | source)
XLA Modules:
  0.0 58.4 jit_solution(10380877932927191948)
XLA Ops:
  0.6 1.0 %place.1.refs_0_ = bf16[512,256]{1,0:T(8,128)(2,1)S(1)} custom-call(s32[1,256]{1,0:T(1,128)} %bitcast.14), custom_call_target="tpu_custom_call" | custom-call | flops 10000000000 | tf_op jit(solution)/shard_map/place/pallas_call | solution.py:41
  1.7 0.5 pack.1
  2.2 0.5 collective-permute-start
  2.7 0.3 rest.1
  3.1 0.8 %collective-permute-done.refs_2_.refs_1_ = bf16[128,1024]{1,0:T(8,128)(2,1)S(1)} collective-permute-done((bf16[128,1024]{1,0:T(8,128)(2,1)S(1)}, bf16[128,1024]{1,0:T(8,128)(2,1)S(1)}, u32[]{:S(2)}, u32[]{:S(2)}) %collective-permute-start) | collective-permute-done | bytes 262176 | tf_op jit(solution)/shard_map/ppermute | solution.py:449
  3.9 0.5 first.4
  4.4 3.0 %collective-permute-start.1 = (bf16[128,512]{1,0:T(8,128)(2,1)S(1)}, bf16[128,512]{1,0:T(8,128)(2,1)S(1)}, u32[]{:S(2)}, u32[]{:S(2)}) collective-permute-start(bf16[128,512]{1,0:T(8,128)(2,1)S(1)} %get-tuple-element.38.refs_2_), channel_id=1, source_target_pairs={{0,1},{1,0},{2,3},{3,2},{4,5},{5,4},{6,7},{7,6},{8,9},{9,8},{10,11... | collective-permute-start | bytes 393224 | tf_op jit(solution)/shard_map/ppermute | solution.py:449
  7.4 2.5 %collective-permute-start.5 = (bf16[128,1024]{1,0:T(8,128)(2,1)S(1)}, bf16[128,1024]{1,0:T(8,128)(2,1)S(1)}, u32[]{:S(2)}, u32[]{:S(2)}) collective-permute-start(bf16[128,1024]{1,0:T(8,128)(2,1)S(1)} %pair.2.refs_2_), channel_id=1, source_target_pairs={{0,24},{4,28},{8,16},{12,20},{16,8},{20,12},{24,0},{28,4},{1,25},{... | collective-permute-start | bytes 786440 | tf_op jit(solution)/shard_map/ppermute | solution.py:449
  9.9 0.5 collective-permute-start.3
  10.5 0.5 collective-permute-start.4
  11.2 2.8 %collective-permute-start.2 = (bf16[128,512]{1,0:T(8,128)(2,1)S(1)}, bf16[128,512]{1,0:T(8,128)(2,1)S(1)}, u32[]{:S(2)}, u32[]{:S(2)}) collective-permute-start(bf16[128,512]{1,0:T(8,128)(2,1)S(1)} %add.8.refs_1_), channel_id=1, source_target_pairs={{0,2},{1,3},{2,0},{3,1},{4,6},{5,7},{6,4},{7,5},{8,10},{9,11},{10,... | collective-permute-start | bytes 393224 | tf_op jit(solution)/shard_map/ppermute | solution.py:449
  14.0 1.0 %prep.1 = (f32[512,1024]{1,0:T(8,128)S(1)}, f32[512,1024]{1,0:T(8,128)S(1)}, bf16[512,1024]{1,0:T(8,128)(2,1)S(1)}) custom-call(bf16[512,2048]{1,0:T(8,128)(2,1)S(1)} %copy-done.1, bf16[128,512]{1,0:T(8,128)(2,1)S(1)} %add.8.refs_1_), custom_call_target="tpu_custom_call" | custom-call | flops 1 | tf_op jit(solution)/shard_map/prep/pallas_call | solution.py:41
  15.1 1.3 %turn.1 = (bf16[1024,1024]{1,0:T(8,128)(2,1)S(1)}, bf16[1024,1024]{1,0:T(8,128)(2,1)S(1)}, bf16[256,128]{1,0:T(8,128)(2,1)S(1)}, bf16[256,256]{1,0:T(8,128)(2,1)S(1)}, bf16[256,128]{1,0:T(8,128)(2,1)S(1)}) custom-call(bf16[512,256]{1,0:T(8,128)(2,1)S(1)} %place.1.refs_0_, bf16[1024,1024]{1,0:T(8,128)(2,1)S(1)} %bitcast.10, bf16[1024,1024]{1,0:T(8,128)(2,1)S(1)} %bitcast.11, ...), custom_call_target="tpu_custom_call" | custom-call | flops 1 | tf_op jit(solution)/shard_map/turn/pallas_call | solution.py:41
  16.4 1.2 %collective-permute-done.5.refs_1_.refs_7_ = bf16[128,1024]{1,0:T(8,128)(2,1)S(1)} collective-permute-done((bf16[128,1024]{1,0:T(8,128)(2,1)S(1)}, bf16[128,1024]{1,0:T(8,128)(2,1)S(1)}, u32[]{:S(2)}, u32[]{:S(2)}) %collective-permute-start.5) | collective-permute-done | bytes 262176 | tf_op jit(solution)/shard_map/ppermute | solution.py:449
  17.6 0.5 first.5
  18.1 0.5 collective-permute-start.8
  18.6 0.8 %collective-permute-done.3.refs_1_.refs_3_ = bf16[64,1024]{1,0:T(8,128)(2,1)S(1)} collective-permute-done((bf16[64,1024]{1,0:T(8,128)(2,1)S(1)}, bf16[64,1024]{1,0:T(8,128)(2,1)S(1)}, u32[]{:S(2)}, u32[]{:S(2)}) %collective-permute-start.3) | collective-permute-done | bytes 131104 | tf_op jit(solution)/shard_map/ppermute | solution.py:449
  19.4 2.0 %collective-permute-start.7 = (bf16[64,1024]{1,0:T(8,128)(2,1)S(1)}, bf16[64,1024]{1,0:T(8,128)(2,1)S(1)}, u32[]{:S(2)}, u32[]{:S(2)}) collective-permute-start(bf16[64,1024]{1,0:T(8,128)(2,1)S(1)} %get-tuple-element.49), channel_id=1, source_target_pairs={{0,20},{4,16},{8,28},{12,24},{16,4},{20,0},{24,12},{28,8},{1,21},{... | collective-permute-start | bytes 393224 | tf_op jit(solution)/shard_map/ppermute | solution.py:449
  21.4 0.5 first.6
  21.8 1.6 %collective-permute-start.11 = (bf16[128,512]{1,0:T(8,128)(2,1)S(1)}, bf16[128,512]{1,0:T(8,128)(2,1)S(1)}, u32[]{:S(2)}, u32[]{:S(2)}) collective-permute-start(bf16[128,512]{1,0:T(8,128)(2,1)S(1)} %get-tuple-element.47.refs_3_), channel_id=1, source_target_pairs={{0,1},{1,0},{2,3},{3,2},{4,5},{5,4},{6,7},{7,6},{8,9},{9,8},{10,11... | collective-permute-start | bytes 393224 | tf_op jit(solution)/shard_map/ppermute | solution.py:449
  23.6 2.7 %collective-permute-start.10 = (bf16[128,512]{1,0:T(8,128)(2,1)S(1)}, bf16[128,512]{1,0:T(8,128)(2,1)S(1)}, u32[]{:S(2)}, u32[]{:S(2)}) collective-permute-start(bf16[128,512]{1,0:T(8,128)(2,1)S(1)} %add.10.refs_3_), channel_id=1, source_target_pairs={{0,2},{1,3},{2,0},{3,1},{4,6},{5,7},{6,4},{7,5},{8,10},{9,11},{10,... | collective-permute-start | bytes 393224 | tf_op jit(solution)/shard_map/ppermute | solution.py:449
  26.3 0.5 first.7
  26.7 0.6 %collective-permute-start.9 = (bf16[128,512]{1,0:T(8,128)(2,1)S(1)}, bf16[128,512]{1,0:T(8,128)(2,1)S(1)}, u32[]{:S(2)}, u32[]{:S(2)}) collective-permute-start(bf16[128,512]{1,0:T(8,128)(2,1)S(1)} %get-tuple-element.52.refs_2_), channel_id=1, source_target_pairs={{0,1},{1,0},{2,3},{3,2},{4,5},{5,4},{6,7},{7,6},{8,9},{9,8},{10,11... | collective-permute-start | bytes 393224 | tf_op jit(solution)/shard_map/ppermute | solution.py:449
  27.4 0.8 %collective-permute-done.11.refs_1_ = bf16[128,512]{1,0:T(8,128)(2,1)S(1)} collective-permute-done((bf16[128,512]{1,0:T(8,128)(2,1)S(1)}, bf16[128,512]{1,0:T(8,128)(2,1)S(1)}, u32[]{:S(2)}, u32[]{:S(2)}) %collective-permute-start.11) | collective-permute-done | bytes 131104 | tf_op jit(solution)/shard_map/ppermute | solution.py:449
  28.2 2.1 %collective-permute-start.14 = (bf16[128,512]{1,0:T(8,128)(2,1)S(1)}, bf16[128,512]{1,0:T(8,128)(2,1)S(1)}, u32[]{:S(2)}, u32[]{:S(2)}) collective-permute-start(bf16[128,512]{1,0:T(8,128)(2,1)S(1)} %add.11.refs_3_), channel_id=1, source_target_pairs={{0,2},{1,3},{2,0},{3,1},{4,6},{5,7},{6,4},{7,5},{8,10},{9,11},{10,... | collective-permute-start | bytes 393224 | tf_op jit(solution)/shard_map/ppermute | solution.py:449
  30.3 1.5 %collective-permute-done.10.refs_2_ = bf16[128,512]{1,0:T(8,128)(2,1)S(1)} collective-permute-done((bf16[128,512]{1,0:T(8,128)(2,1)S(1)}, bf16[128,512]{1,0:T(8,128)(2,1)S(1)}, u32[]{:S(2)}, u32[]{:S(2)}) %collective-permute-start.10) | collective-permute-done | bytes 131104 | tf_op jit(solution)/shard_map/ppermute | solution.py:449
  31.8 1.1 %collective-permute-start.13 = (bf16[128,512]{1,0:T(8,128)(2,1)S(1)}, bf16[128,512]{1,0:T(8,128)(2,1)S(1)}, u32[]{:S(2)}, u32[]{:S(2)}) collective-permute-start(bf16[128,512]{1,0:T(8,128)(2,1)S(1)} %add.12.refs_2_.refs_0_), channel_id=1, source_target_pairs={{0,1},{1,0},{2,3},{3,2},{4,5},{5,4},{6,7},{7,6},{8,9},{9,8},{10,11... | collective-permute-start | bytes 393224 | tf_op jit(solution)/shard_map/ppermute | solution.py:449
  32.9 3.1 %collective-permute-done.9.refs_1_ = bf16[128,512]{1,0:T(8,128)(2,1)S(1)} collective-permute-done((bf16[128,512]{1,0:T(8,128)(2,1)S(1)}, bf16[128,512]{1,0:T(8,128)(2,1)S(1)}, u32[]{:S(2)}, u32[]{:S(2)}) %collective-permute-start.9) | collective-permute-done | bytes 131104 | tf_op jit(solution)/shard_map/ppermute | solution.py:449
  36.0 0.9 %collective-permute-start.12 = (bf16[128,512]{1,0:T(8,128)(2,1)S(1)}, bf16[128,512]{1,0:T(8,128)(2,1)S(1)}, u32[]{:S(2)}, u32[]{:S(2)}) collective-permute-start(bf16[128,512]{1,0:T(8,128)(2,1)S(1)} %add.13.refs_8_), channel_id=1, source_target_pairs={{0,2},{1,3},{2,0},{3,1},{4,6},{5,7},{6,4},{7,5},{8,10},{9,11},{10,... | collective-permute-start | bytes 393224 | tf_op jit(solution)/shard_map/ppermute | solution.py:449
  36.9 2.5 %down.1 = (f32[1024,1024]{1,0:T(8,128)}, f32[8,128]{1,0:T(8,128)S(1)}) custom-call(bf16[512,1024]{1,0:T(8,128)(2,1)S(1)} %get-tuple-element.40.refs_3_.refs_0_, bf16[64,1024]{1,0:T(8,128)(2,1)S(1)} %get-tuple-element.36.refs_1_.refs_3_, bf16[128,1024]{1,0:T(8,128)(2,1)S(1)} %collective-permute-done.refs_2_.refs_1_, ...), custom_call_target="tpu_custom_call" | custom-call | flops 1 | tf_op jit(solution)/shard_map/down/pallas_call | solution.py:41
  39.5 1.8 %collective-permute-start.17 = (bf16[128,512]{1,0:T(8,128)(2,1)S(1)}, bf16[128,512]{1,0:T(8,128)(2,1)S(1)}, u32[]{:S(2)}, u32[]{:S(2)}) collective-permute-start(bf16[128,512]{1,0:T(8,128)(2,1)S(1)} %add.14.refs_6_.refs_0_), channel_id=1, source_target_pairs={{0,1},{1,0},{2,3},{3,2},{4,5},{5,4},{6,7},{7,6},{8,9},{9,8},{10,11... | collective-permute-start | bytes 393224 | tf_op jit(solution)/shard_map/ppermute | solution.py:449
  41.3 0.7 %second.4.refs_3_ = bf16[128,1024]{1,0:T(8,128)(2,1)S(1)} custom-call(bf16[128,512]{1,0:T(8,128)(2,1)S(1)} %add.12.refs_2_.refs_0_, bf16[128,512]{1,0:T(8,128)(2,1)S(1)} %collective-permute-done.13.refs_1_, f32[512,1024]{1,0:T(8,128)S(1)} %get-tuple-element.54.refs_2_, f32[512,1024]{1,0:T(8,128)S(1)} %get-tuple-element.55.refs_3_, ...), custom_call_target="tpu_custom_call" | custom-call | flops 10000000000 | tf_op jit(solution)/shard_map/second/pallas_call | solution.py:41
  42.0 1.7 %collective-permute-done.12.refs_2_ = bf16[128,512]{1,0:T(8,128)(2,1)S(1)} collective-permute-done((bf16[128,512]{1,0:T(8,128)(2,1)S(1)}, bf16[128,512]{1,0:T(8,128)(2,1)S(1)}, u32[]{:S(2)}, u32[]{:S(2)}) %collective-permute-start.12) | collective-permute-done | bytes 131104 | tf_op jit(solution)/shard_map/ppermute | solution.py:449
  43.9 0.3 collective-permute-start.16
  44.2 2.5 %collective-permute-start.18 = (bf16[128,1024]{1,0:T(8,128)(2,1)S(1)}, bf16[128,1024]{1,0:T(8,128)(2,1)S(1)}, u32[]{:S(2)}, u32[]{:S(2)}) collective-permute-start(bf16[128,1024]{1,0:T(8,128)(2,1)S(1)} %second.4.refs_3_), channel_id=1, source_target_pairs={{0,24},{4,28},{8,16},{12,20},{16,8},{20,12},{24,0},{28,4},{1,25},{... | collective-permute-start | bytes 786440 | tf_op jit(solution)/shard_map/ppermute | solution.py:449
  46.7 0.7 %collective-permute-start.15 = (bf16[128,512]{1,0:T(8,128)(2,1)S(1)}, bf16[128,512]{1,0:T(8,128)(2,1)S(1)}, u32[]{:S(2)}, u32[]{:S(2)}) collective-permute-start(bf16[128,512]{1,0:T(8,128)(2,1)S(1)} %release.1.refs_6_.refs_0_), channel_id=1, source_target_pairs={{0,1},{1,0},{2,3},{3,2},{4,5},{5,4},{6,7},{7,6},{8,9},{9,8},{10,11... | collective-permute-start | bytes 393224 | tf_op jit(solution)/shard_map/ppermute | solution.py:449
  47.4 0.8 %second.5 = (bf16[64,1024]{1,0:T(8,128)(2,1)S(1)}, bf16[64,1024]{1,0:T(8,128)(2,1)S(1)}) custom-call(bf16[128,512]{1,0:T(8,128)(2,1)S(1)} %add.14.refs_6_.refs_0_, bf16[128,512]{1,0:T(8,128)(2,1)S(1)} %collective-permute-done.17.refs_1_, f32[512,1024]{1,0:T(8,128)S(1)} %get-tuple-element.54.refs_2_, f32[512,1024]{1,0:T(8,128)S(1)} %get-tuple-element.55.refs_3_, ...), custom_call_target="tpu_custom_call" | custom-call | flops 10000000000 | tf_op jit(solution)/shard_map/second/pallas_call | solution.py:41
  48.3 2.0 %collective-permute-start.21 = (bf16[64,1024]{1,0:T(8,128)(2,1)S(1)}, bf16[64,1024]{1,0:T(8,128)(2,1)S(1)}, u32[]{:S(2)}, u32[]{:S(2)}) collective-permute-start(bf16[64,1024]{1,0:T(8,128)(2,1)S(1)} %get-tuple-element.63), channel_id=1, source_target_pairs={{0,16},{4,20},{8,24},{12,28},{16,0},{20,4},{24,8},{28,12},{1,17},{... | collective-permute-start | bytes 393224 | tf_op jit(solution)/shard_map/ppermute | solution.py:449
  50.3 0.7 %second.6 = (bf16[64,1024]{1,0:T(8,128)(2,1)S(1)}, bf16[64,1024]{1,0:T(8,128)(2,1)S(1)}) custom-call(bf16[128,512]{1,0:T(8,128)(2,1)S(1)} %add.15.refs_1_.refs_0_, bf16[128,512]{1,0:T(8,128)(2,1)S(1)} %collective-permute-done.16.refs_1_, f32[512,1024]{1,0:T(8,128)S(1)} %get-tuple-element.54.refs_2_, f32[512,1024]{1,0:T(8,128)S(1)} %get-tuple-element.55.refs_3_, ...), custom_call_target="tpu_custom_call" | custom-call | flops 10000000000 | tf_op jit(solution)/shard_map/second/pallas_call | solution.py:41
  51.1 0.6 collective-permute-done.15.refs_1_
  51.6 1.1 %collective-permute-start.23 = (bf16[64,1024]{1,0:T(8,128)(2,1)S(1)}, bf16[64,1024]{1,0:T(8,128)(2,1)S(1)}, u32[]{:S(2)}, u32[]{:S(2)}) collective-permute-start(bf16[64,1024]{1,0:T(8,128)(2,1)S(1)} %get-tuple-element.64), channel_id=1, source_target_pairs={{0,20},{4,16},{8,28},{12,24},{16,4},{20,0},{24,12},{28,8},{1,21},{... | collective-permute-start | bytes 393224 | tf_op jit(solution)/shard_map/ppermute | solution.py:449
  52.8 0.7 %second.7 = (bf16[64,1024]{1,0:T(8,128)(2,1)S(1)}, bf16[64,1024]{1,0:T(8,128)(2,1)S(1)}) custom-call(bf16[128,512]{1,0:T(8,128)(2,1)S(1)} %release.1.refs_6_.refs_0_, bf16[128,512]{1,0:T(8,128)(2,1)S(1)} %collective-permute-done.15.refs_1_, f32[512,1024]{1,0:T(8,128)S(1)} %get-tuple-element.54.refs_2_, f32[512,1024]{1,0:T(8,128)S(1)} %get-tuple-element.55.refs_3_, ...), custom_call_target="tpu_custom_call" | custom-call | flops 10000000000 | tf_op jit(solution)/shard_map/second/pallas_call | solution.py:41
  53.6 0.8 %collective-permute-done.20.refs_1_ = bf16[64,1024]{1,0:T(8,128)(2,1)S(1)} collective-permute-done((bf16[64,1024]{1,0:T(8,128)(2,1)S(1)}, bf16[64,1024]{1,0:T(8,128)(2,1)S(1)}, u32[]{:S(2)}, u32[]{:S(2)}) %collective-permute-start.20) | collective-permute-done | bytes 131104 | tf_op jit(solution)/shard_map/ppermute | solution.py:449
  54.7 0.4 collective-permute-done.19.refs_2_
  55.2 0.3 gather.3.refs_1_.refs_4_
  55.5 1.5 %collective-permute-done.22.refs_2_ = bf16[64,1024]{1,0:T(8,128)(2,1)S(1)} collective-permute-done((bf16[64,1024]{1,0:T(8,128)(2,1)S(1)}, bf16[64,1024]{1,0:T(8,128)(2,1)S(1)}, u32[]{:S(2)}, u32[]{:S(2)}) %collective-permute-start.22) | collective-permute-done | bytes 131104 | tf_op jit(solution)/shard_map/ppermute | solution.py:449
  56.9 0.4 collective-permute-done.23.refs_3_
  57.4 1.0 %finish.1 = bf16[256,1024]{1,0:T(8,128)(2,1)} custom-call(bf16[256,128]{1,0:T(8,128)(2,1)S(1)} %get-tuple-element.41.refs_0_, bf16[256,1024]{1,0:T(8,128)(2,1)S(1)} %gather.3.refs_1_.refs_4_, bf16[64,1024]{1,0:T(8,128)(2,1)S(1)} %collective-permute-done.22.refs_2_, bf16[64,1024]{1,0:T(8,128)(2,1)S(1)} %collective-permute-done.23.refs_3_, ...), custom_call_target="tpu_custom_call" | custom-call | flops 1 | tf_op jit(solution)/shard_map/finish/pallas_call | solution.py:41
  (40 shorter events, 1.2 us)
Async XLA Ops:
  0.6 1.1 %copy-start.4 = (bf16[256,1024]{1,0:T(8,128)(2,1)S(1)}, bf16[256,1024]{1,0:T(8,128)(2,1)}, u32[]{:S(2)}) copy-start(bf16[256,1024]{1,0:T(8,128)(2,1)} %refs_2_.1) | copy-start | bytes 1572868
  0.6 1.1 %copy-start.5 = (bf16[256,8]{0,1:T(8,128)(2,1)S(1)}, bf16[256,8]{0,1:T(8,128)(2,1)}, u32[]{:S(2)}) copy-start(bf16[256,8]{0,1:T(8,128)(2,1)} %param.8) | copy-start | bytes 12292
  1.7 2.2 %copy-start = (bf16[1,1024,1024]{2,1,0:T(8,128)(2,1)S(1)}, bf16[1,1024,1024]{2,1,0:T(8,128)(2,1)}, u32[]{:S(2)}) copy-start(bf16[1,1024,1024]{2,1,0:T(8,128)(2,1)} %param.13) | copy-start | bytes 6291460
  2.2 1.7 %collective-permute-start = (bf16[128,1024]{1,0:T(8,128)(2,1)S(1)}, bf16[128,1024]{1,0:T(8,128)(2,1)S(1)}, u32[]{:S(2)}, u32[]{:S(2)}) collective-permute-start(bf16[128,1024]{1,0:T(8,128)(2,1)S(1)} %get-tuple-element.35.refs_2_), channel_id=1, source_target_pairs={{0,4},{4,0},{8,12},{12,8},{16,20},{20,16},{24,28},{28,24},{1,5},{5... | collective-permute-start | bytes 786440 | tf_op jit(solution)/shard_map/ppermute | solution.py:449
  4.4 6.8 %collective-permute-start.1 = (bf16[128,512]{1,0:T(8,128)(2,1)S(1)}, bf16[128,512]{1,0:T(8,128)(2,1)S(1)}, u32[]{:S(2)}, u32[]{:S(2)}) collective-permute-start(bf16[128,512]{1,0:T(8,128)(2,1)S(1)} %get-tuple-element.38.refs_2_), channel_id=1, source_target_pairs={{0,1},{1,0},{2,3},{3,2},{4,5},{5,4},{6,7},{7,6},{8,9},{9,8},{10,11... | collective-permute-start | bytes 393224 | tf_op jit(solution)/shard_map/ppermute | solution.py:449
  7.4 6.7 %copy-start.1 = (bf16[512,2048]{1,0:T(8,128)(2,1)S(1)}, bf16[512,2048]{1,0:T(8,128)(2,1)}, u32[]{:S(2)}) copy-start(bf16[512,2048]{1,0:T(8,128)(2,1)} %refs_0_.1) | copy-start | bytes 6291460
  7.4 10.2 %collective-permute-start.5 = (bf16[128,1024]{1,0:T(8,128)(2,1)S(1)}, bf16[128,1024]{1,0:T(8,128)(2,1)S(1)}, u32[]{:S(2)}, u32[]{:S(2)}) collective-permute-start(bf16[128,1024]{1,0:T(8,128)(2,1)S(1)} %pair.2.refs_2_), channel_id=1, source_target_pairs={{0,24},{4,28},{8,16},{12,20},{16,8},{20,12},{24,0},{28,4},{1,25},{... | collective-permute-start | bytes 786440 | tf_op jit(solution)/shard_map/ppermute | solution.py:449
  9.9 9.4 %collective-permute-start.3 = (bf16[64,1024]{1,0:T(8,128)(2,1)S(1)}, bf16[64,1024]{1,0:T(8,128)(2,1)S(1)}, u32[]{:S(2)}, u32[]{:S(2)}) collective-permute-start(bf16[64,1024]{1,0:T(8,128)(2,1)S(1)} %get-tuple-element.43), channel_id=1, source_target_pairs={{0,8},{4,12},{8,0},{12,4},{16,24},{20,28},{24,16},{28,20},{1,9},{5... | collective-permute-start | bytes 393224 | tf_op jit(solution)/shard_map/ppermute | solution.py:449
  10.5 10.9 %collective-permute-start.4 = (bf16[64,1024]{1,0:T(8,128)(2,1)S(1)}, bf16[64,1024]{1,0:T(8,128)(2,1)S(1)}, u32[]{:S(2)}, u32[]{:S(2)}) collective-permute-start(bf16[64,1024]{1,0:T(8,128)(2,1)S(1)} %get-tuple-element.44), channel_id=1, source_target_pairs={{0,16},{4,20},{8,24},{12,28},{16,0},{20,4},{24,8},{28,12},{1,17},{... | collective-permute-start | bytes 393224 | tf_op jit(solution)/shard_map/ppermute | solution.py:449
  11.2 3.9 %copy-start.2 = (bf16[1,1024,1024]{2,1,0:T(8,128)(2,1)S(1)}, bf16[1,1024,1024]{2,1,0:T(8,128)(2,1)}, u32[]{:S(2)}) copy-start(bf16[1,1024,1024]{2,1,0:T(8,128)(2,1)} %param.11) | copy-start | bytes 6291460
  11.2 3.9 %copy-start.3 = (bf16[1,1024,1024]{2,1,0:T(8,128)(2,1)S(1)}, bf16[1,1024,1024]{2,1,0:T(8,128)(2,1)}, u32[]{:S(2)}) copy-start(bf16[1,1024,1024]{2,1,0:T(8,128)(2,1)} %param.12) | copy-start | bytes 6291460
  11.2 12.3 %collective-permute-start.2 = (bf16[128,512]{1,0:T(8,128)(2,1)S(1)}, bf16[128,512]{1,0:T(8,128)(2,1)S(1)}, u32[]{:S(2)}, u32[]{:S(2)}) collective-permute-start(bf16[128,512]{1,0:T(8,128)(2,1)S(1)} %add.8.refs_1_), channel_id=1, source_target_pairs={{0,2},{1,3},{2,0},{3,1},{4,6},{5,7},{6,4},{7,5},{8,10},{9,11},{10,... | collective-permute-start | bytes 393224 | tf_op jit(solution)/shard_map/ppermute | solution.py:449
  18.1 5.5 %collective-permute-start.8 = (bf16[128,512]{1,0:T(8,128)(2,1)S(1)}, bf16[128,512]{1,0:T(8,128)(2,1)S(1)}, u32[]{:S(2)}, u32[]{:S(2)}) collective-permute-start(bf16[128,512]{1,0:T(8,128)(2,1)S(1)} %get-tuple-element.46.refs_3_), channel_id=1, source_target_pairs={{0,1},{1,0},{2,3},{3,2},{4,5},{5,4},{6,7},{7,6},{8,9},{9,8},{10,11... | collective-permute-start | bytes 393224 | tf_op jit(solution)/shard_map/ppermute | solution.py:449
  18.6 7.7 %collective-permute-start.6 = (bf16[64,1024]{1,0:T(8,128)(2,1)S(1)}, bf16[64,1024]{1,0:T(8,128)(2,1)S(1)}, u32[]{:S(2)}, u32[]{:S(2)}) collective-permute-start(bf16[64,1024]{1,0:T(8,128)(2,1)S(1)} %get-tuple-element.48), channel_id=1, source_target_pairs={{0,12},{4,8},{8,4},{12,0},{16,28},{20,24},{24,20},{28,16},{1,13},{... | collective-permute-start | bytes 393224 | tf_op jit(solution)/shard_map/ppermute | solution.py:449
  19.4 6.9 %collective-permute-start.7 = (bf16[64,1024]{1,0:T(8,128)(2,1)S(1)}, bf16[64,1024]{1,0:T(8,128)(2,1)S(1)}, u32[]{:S(2)}, u32[]{:S(2)}) collective-permute-start(bf16[64,1024]{1,0:T(8,128)(2,1)S(1)} %get-tuple-element.49), channel_id=1, source_target_pairs={{0,20},{4,16},{8,28},{12,24},{16,4},{20,0},{24,12},{28,8},{1,21},{... | collective-permute-start | bytes 393224 | tf_op jit(solution)/shard_map/ppermute | solution.py:449
  21.8 6.4 %collective-permute-start.11 = (bf16[128,512]{1,0:T(8,128)(2,1)S(1)}, bf16[128,512]{1,0:T(8,128)(2,1)S(1)}, u32[]{:S(2)}, u32[]{:S(2)}) collective-permute-start(bf16[128,512]{1,0:T(8,128)(2,1)S(1)} %get-tuple-element.47.refs_3_), channel_id=1, source_target_pairs={{0,1},{1,0},{2,3},{3,2},{4,5},{5,4},{6,7},{7,6},{8,9},{9,8},{10,11... | collective-permute-start | bytes 393224 | tf_op jit(solution)/shard_map/ppermute | solution.py:449
  23.6 8.2 %collective-permute-start.10 = (bf16[128,512]{1,0:T(8,128)(2,1)S(1)}, bf16[128,512]{1,0:T(8,128)(2,1)S(1)}, u32[]{:S(2)}, u32[]{:S(2)}) collective-permute-start(bf16[128,512]{1,0:T(8,128)(2,1)S(1)} %add.10.refs_3_), channel_id=1, source_target_pairs={{0,2},{1,3},{2,0},{3,1},{4,6},{5,7},{6,4},{7,5},{8,10},{9,11},{10,... | collective-permute-start | bytes 393224 | tf_op jit(solution)/shard_map/ppermute | solution.py:449
  26.7 9.3 %collective-permute-start.9 = (bf16[128,512]{1,0:T(8,128)(2,1)S(1)}, bf16[128,512]{1,0:T(8,128)(2,1)S(1)}, u32[]{:S(2)}, u32[]{:S(2)}) collective-permute-start(bf16[128,512]{1,0:T(8,128)(2,1)S(1)} %get-tuple-element.52.refs_2_), channel_id=1, source_target_pairs={{0,1},{1,0},{2,3},{3,2},{4,5},{5,4},{6,7},{7,6},{8,9},{9,8},{10,11... | collective-permute-start | bytes 393224 | tf_op jit(solution)/shard_map/ppermute | solution.py:449
  28.2 11.2 %collective-permute-start.14 = (bf16[128,512]{1,0:T(8,128)(2,1)S(1)}, bf16[128,512]{1,0:T(8,128)(2,1)S(1)}, u32[]{:S(2)}, u32[]{:S(2)}) collective-permute-start(bf16[128,512]{1,0:T(8,128)(2,1)S(1)} %add.11.refs_3_), channel_id=1, source_target_pairs={{0,2},{1,3},{2,0},{3,1},{4,6},{5,7},{6,4},{7,5},{8,10},{9,11},{10,... | collective-permute-start | bytes 393224 | tf_op jit(solution)/shard_map/ppermute | solution.py:449
  31.8 9.5 %collective-permute-start.13 = (bf16[128,512]{1,0:T(8,128)(2,1)S(1)}, bf16[128,512]{1,0:T(8,128)(2,1)S(1)}, u32[]{:S(2)}, u32[]{:S(2)}) collective-permute-start(bf16[128,512]{1,0:T(8,128)(2,1)S(1)} %add.12.refs_2_.refs_0_), channel_id=1, source_target_pairs={{0,1},{1,0},{2,3},{3,2},{4,5},{5,4},{6,7},{7,6},{8,9},{9,8},{10,11... | collective-permute-start | bytes 393224 | tf_op jit(solution)/shard_map/ppermute | solution.py:449
  36.0 7.7 %collective-permute-start.12 = (bf16[128,512]{1,0:T(8,128)(2,1)S(1)}, bf16[128,512]{1,0:T(8,128)(2,1)S(1)}, u32[]{:S(2)}, u32[]{:S(2)}) collective-permute-start(bf16[128,512]{1,0:T(8,128)(2,1)S(1)} %add.13.refs_8_), channel_id=1, source_target_pairs={{0,2},{1,3},{2,0},{3,1},{4,6},{5,7},{6,4},{7,5},{8,10},{9,11},{10,... | collective-permute-start | bytes 393224 | tf_op jit(solution)/shard_map/ppermute | solution.py:449
  39.5 7.9 %collective-permute-start.17 = (bf16[128,512]{1,0:T(8,128)(2,1)S(1)}, bf16[128,512]{1,0:T(8,128)(2,1)S(1)}, u32[]{:S(2)}, u32[]{:S(2)}) collective-permute-start(bf16[128,512]{1,0:T(8,128)(2,1)S(1)} %add.14.refs_6_.refs_0_), channel_id=1, source_target_pairs={{0,1},{1,0},{2,3},{3,2},{4,5},{5,4},{6,7},{7,6},{8,9},{9,8},{10,11... | collective-permute-start | bytes 393224 | tf_op jit(solution)/shard_map/ppermute | solution.py:449
  43.9 6.4 %collective-permute-start.16 = (bf16[128,512]{1,0:T(8,128)(2,1)S(1)}, bf16[128,512]{1,0:T(8,128)(2,1)S(1)}, u32[]{:S(2)}, u32[]{:S(2)}) collective-permute-start(bf16[128,512]{1,0:T(8,128)(2,1)S(1)} %add.15.refs_1_.refs_0_), channel_id=1, source_target_pairs={{0,1},{1,0},{2,3},{3,2},{4,5},{5,4},{6,7},{7,6},{8,9},{9,8},{10,11... | collective-permute-start | bytes 393224 | tf_op jit(solution)/shard_map/ppermute | solution.py:449
  44.2 9.3 %collective-permute-start.18 = (bf16[128,1024]{1,0:T(8,128)(2,1)S(1)}, bf16[128,1024]{1,0:T(8,128)(2,1)S(1)}, u32[]{:S(2)}, u32[]{:S(2)}) collective-permute-start(bf16[128,1024]{1,0:T(8,128)(2,1)S(1)} %second.4.refs_3_), channel_id=1, source_target_pairs={{0,24},{4,28},{8,16},{12,20},{16,8},{20,12},{24,0},{28,4},{1,25},{... | collective-permute-start | bytes 786440 | tf_op jit(solution)/shard_map/ppermute | solution.py:449
  46.7 5.0 %collective-permute-start.15 = (bf16[128,512]{1,0:T(8,128)(2,1)S(1)}, bf16[128,512]{1,0:T(8,128)(2,1)S(1)}, u32[]{:S(2)}, u32[]{:S(2)}) collective-permute-start(bf16[128,512]{1,0:T(8,128)(2,1)S(1)} %release.1.refs_6_.refs_0_), channel_id=1, source_target_pairs={{0,1},{1,0},{2,3},{3,2},{4,5},{5,4},{6,7},{7,6},{8,9},{9,8},{10,11... | collective-permute-start | bytes 393224 | tf_op jit(solution)/shard_map/ppermute | solution.py:449
  48.1 6.3 %collective-permute-start.20 = (bf16[64,1024]{1,0:T(8,128)(2,1)S(1)}, bf16[64,1024]{1,0:T(8,128)(2,1)S(1)}, u32[]{:S(2)}, u32[]{:S(2)}) collective-permute-start(bf16[64,1024]{1,0:T(8,128)(2,1)S(1)} %get-tuple-element.58.refs_6_), channel_id=1, source_target_pairs={{0,8},{4,12},{8,0},{12,4},{16,24},{20,28},{24,16},{28,20},{1,9},{5... | collective-permute-start | bytes 393224 | tf_op jit(solution)/shard_map/ppermute | solution.py:449
  48.3 6.2 %collective-permute-start.21 = (bf16[64,1024]{1,0:T(8,128)(2,1)S(1)}, bf16[64,1024]{1,0:T(8,128)(2,1)S(1)}, u32[]{:S(2)}, u32[]{:S(2)}) collective-permute-start(bf16[64,1024]{1,0:T(8,128)(2,1)S(1)} %get-tuple-element.63), channel_id=1, source_target_pairs={{0,16},{4,20},{8,24},{12,28},{16,0},{20,4},{24,8},{28,12},{1,17},{... | collective-permute-start | bytes 393224 | tf_op jit(solution)/shard_map/ppermute | solution.py:449
  51.0 5.9 %collective-permute-start.22 = (bf16[64,1024]{1,0:T(8,128)(2,1)S(1)}, bf16[64,1024]{1,0:T(8,128)(2,1)S(1)}, u32[]{:S(2)}, u32[]{:S(2)}) collective-permute-start(bf16[64,1024]{1,0:T(8,128)(2,1)S(1)} %get-tuple-element.59.refs_6_), channel_id=1, source_target_pairs={{0,12},{4,8},{8,4},{12,0},{16,28},{20,24},{24,20},{28,16},{1,13},{... | collective-permute-start | bytes 393224 | tf_op jit(solution)/shard_map/ppermute | solution.py:449
  51.6 5.7 %collective-permute-start.23 = (bf16[64,1024]{1,0:T(8,128)(2,1)S(1)}, bf16[64,1024]{1,0:T(8,128)(2,1)S(1)}, u32[]{:S(2)}, u32[]{:S(2)}) collective-permute-start(bf16[64,1024]{1,0:T(8,128)(2,1)S(1)} %get-tuple-element.64), channel_id=1, source_target_pairs={{0,20},{4,16},{8,28},{12,24},{16,4},{20,0},{24,12},{28,8},{1,21},{... | collective-permute-start | bytes 393224 | tf_op jit(solution)/shard_map/ppermute | solution.py:449
  53.6 1.6 %collective-permute-start.19 = (bf16[128,1024]{1,0:T(8,128)(2,1)S(1)}, bf16[128,1024]{1,0:T(8,128)(2,1)S(1)}, u32[]{:S(2)}, u32[]{:S(2)}) collective-permute-start(bf16[128,1024]{1,0:T(8,128)(2,1)S(1)} %pair.3.refs_3_), channel_id=1, source_target_pairs={{0,4},{4,0},{8,12},{12,8},{16,20},{20,16},{24,28},{28,24},{1,5},{5... | collective-permute-start | bytes 786440 | tf_op jit(solution)/shard_map/ppermute | solution.py:449

commit v6 on v5

--- a/solution.py
+++ b/solution.py
@@ -13,8 +13,8 @@
 ORDER = (
     ("first", 0), ("diagonal", 0), ("add", 0), ("prep", 0), ("turn", 0), ("first", 1),
     ("first", 2), ("add", 0), ("add", 1), ("first", 3), ("add", 2), ("add", 1), ("add", 3),
-    ("down", 0), ("add", 2), ("second", 1), ("add", 3), ("release", 0), ("second", 2),
-    ("second", 3), ("second", 0), ("cross", 0), ("gather", 0), ("gather", 1),
+    ("release", 0), ("down", 0), ("add", 2), ("second", 1), ("second", 0), ("add", 3),
+    ("second", 2), ("second", 3), ("cross", 0), ("gather", 0), ("gather", 1),
 )
 HELD = (0,)
 COST = {

time: 58.6 us -> 60 us (1.024)
  starting transfers between devices: 30.1 us -> 33.5 us
  waiting for transfers between devices: 13.8 us -> 11.8 us
    ppermute x24, starting transfers between devices: 30.1 us -> 33.5 us  [swap(): return lax.ppermute(block, axis, [(i, i ^ k) for i in range(size)])]
    ppermute x24, waiting for transfers between devices: 13.8 us -> 11.8 us  [swap(): return lax.ppermute(block, axis, [(i, i ^ k) for i in range(size)])]
  transfers between devices with their start and end apart: 24 -> 24, of which waited for: 13 -> 11; matrix products, arithmetic and copies ran while one was open for 0% -> 0% of each run, Pallas kernels for 18% -> 18%
where the time goes in v6:
time: 60 us; the launch traced here: 59.8 us
  starting transfers between devices  33.5 us (56%)
  Pallas kernels  13.5 us (22%)
  waiting for transfers between devices  11.8 us (20%)
  between operations  0.92 us (2%)
    ppermute x24, starting transfers between devices, swap(): return lax.ppermute(block, axis, [(i, i ^ k) for i in range(size)])  33.5 us
    pallas_call x28, Pallas kernels, call(): pl.pallas_call(run, name=name, out_shape=outs, in_specs=list(specs) + [AN...  13.5 us
    ppermute x24, waiting for transfers between devices, swap(): return lax.ppermute(block, axis, [(i, i ^ k) for i in range(size)])  11.8 us
  transfers between devices with their start and end apart: 24, of which 11 were waited for; matrix products, arithmetic and copies ran while one was open for 0% of the time, Pallas kernels for 18%

profile of v6, /device:TPU:0, one launch (start us, length us, event | category | flops | bytes accessed | tf_op | source)
XLA Modules:
  0.0 59.8 jit_solution(502943573145862026)
XLA Ops:
  0.6 1.0 %place.1.refs_0_ = bf16[512,256]{1,0:T(8,128)(2,1)S(1)} custom-call(s32[1,256]{1,0:T(1,128)} %bitcast.14), custom_call_target="tpu_custom_call" | custom-call | flops 10000000000 | tf_op jit(solution)/shard_map/place/pallas_call | solution.py:41
  1.7 0.5 pack.1
  2.2 0.5 collective-permute-start
  2.7 0.3 rest.1
  3.1 0.8 %collective-permute-done.refs_2_.refs_1_ = bf16[128,1024]{1,0:T(8,128)(2,1)S(1)} collective-permute-done((bf16[128,1024]{1,0:T(8,128)(2,1)S(1)}, bf16[128,1024]{1,0:T(8,128)(2,1)S(1)}, u32[]{:S(2)}, u32[]{:S(2)}) %collective-permute-start) | collective-permute-done | bytes 262176 | tf_op jit(solution)/shard_map/ppermute | solution.py:449
  3.9 0.5 first.4
  4.4 3.0 %collective-permute-start.1 = (bf16[128,512]{1,0:T(8,128)(2,1)S(1)}, bf16[128,512]{1,0:T(8,128)(2,1)S(1)}, u32[]{:S(2)}, u32[]{:S(2)}) collective-permute-start(bf16[128,512]{1,0:T(8,128)(2,1)S(1)} %get-tuple-element.38.refs_2_), channel_id=1, source_target_pairs={{0,1},{1,0},{2,3},{3,2},{4,5},{5,4},{6,7},{7,6},{8,9},{9,8},{10,11... | collective-permute-start | bytes 393224 | tf_op jit(solution)/shard_map/ppermute | solution.py:449
  7.4 2.5 %collective-permute-start.5 = (bf16[128,1024]{1,0:T(8,128)(2,1)S(1)}, bf16[128,1024]{1,0:T(8,128)(2,1)S(1)}, u32[]{:S(2)}, u32[]{:S(2)}) collective-permute-start(bf16[128,1024]{1,0:T(8,128)(2,1)S(1)} %pair.2.refs_2_), channel_id=1, source_target_pairs={{0,24},{4,28},{8,16},{12,20},{16,8},{20,12},{24,0},{28,4},{1,25},{... | collective-permute-start | bytes 786440 | tf_op jit(solution)/shard_map/ppermute | solution.py:449
  9.9 0.5 collective-permute-start.3
  10.5 0.5 collective-permute-start.4
  11.0 0.2 collective-permute-done.1.refs_1_
  11.2 2.8 %collective-permute-start.2 = (bf16[128,512]{1,0:T(8,128)(2,1)S(1)}, bf16[128,512]{1,0:T(8,128)(2,1)S(1)}, u32[]{:S(2)}, u32[]{:S(2)}) collective-permute-start(bf16[128,512]{1,0:T(8,128)(2,1)S(1)} %add.8.refs_1_), channel_id=1, source_target_pairs={{0,2},{1,3},{2,0},{3,1},{4,6},{5,7},{6,4},{7,5},{8,10},{9,11},{10,... | collective-permute-start | bytes 393224 | tf_op jit(solution)/shard_map/ppermute | solution.py:449
  14.0 1.0 %prep.1 = (f32[512,1024]{1,0:T(8,128)S(1)}, f32[512,1024]{1,0:T(8,128)S(1)}, bf16[512,1024]{1,0:T(8,128)(2,1)S(1)}) custom-call(bf16[512,2048]{1,0:T(8,128)(2,1)S(1)} %copy-done.1, bf16[128,512]{1,0:T(8,128)(2,1)S(1)} %add.8.refs_1_), custom_call_target="tpu_custom_call" | custom-call | flops 1 | tf_op jit(solution)/shard_map/prep/pallas_call | solution.py:41
  15.1 1.3 %turn.1 = (bf16[1024,1024]{1,0:T(8,128)(2,1)S(1)}, bf16[1024,1024]{1,0:T(8,128)(2,1)S(1)}, bf16[256,128]{1,0:T(8,128)(2,1)S(1)}, bf16[256,256]{1,0:T(8,128)(2,1)S(1)}, bf16[256,128]{1,0:T(8,128)(2,1)S(1)}) custom-call(bf16[512,256]{1,0:T(8,128)(2,1)S(1)} %place.1.refs_0_, bf16[1024,1024]{1,0:T(8,128)(2,1)S(1)} %bitcast.10, bf16[1024,1024]{1,0:T(8,128)(2,1)S(1)} %bitcast.11, ...), custom_call_target="tpu_custom_call" | custom-call | flops 1 | tf_op jit(solution)/shard_map/turn/pallas_call | solution.py:41
  16.4 1.2 %collective-permute-done.5.refs_1_.refs_7_ = bf16[128,1024]{1,0:T(8,128)(2,1)S(1)} collective-permute-done((bf16[128,1024]{1,0:T(8,128)(2,1)S(1)}, bf16[128,1024]{1,0:T(8,128)(2,1)S(1)}, u32[]{:S(2)}, u32[]{:S(2)}) %collective-permute-start.5) | collective-permute-done | bytes 262176 | tf_op jit(solution)/shard_map/ppermute | solution.py:449
  17.6 0.5 first.5
  18.1 0.5 collective-permute-start.8
  18.6 0.8 %collective-permute-done.3.refs_1_.refs_3_ = bf16[64,1024]{1,0:T(8,128)(2,1)S(1)} collective-permute-done((bf16[64,1024]{1,0:T(8,128)(2,1)S(1)}, bf16[64,1024]{1,0:T(8,128)(2,1)S(1)}, u32[]{:S(2)}, u32[]{:S(2)}) %collective-permute-start.3) | collective-permute-done | bytes 131104 | tf_op jit(solution)/shard_map/ppermute | solution.py:449
  19.4 2.0 %collective-permute-start.7 = (bf16[64,1024]{1,0:T(8,128)(2,1)S(1)}, bf16[64,1024]{1,0:T(8,128)(2,1)S(1)}, u32[]{:S(2)}, u32[]{:S(2)}) collective-permute-start(bf16[64,1024]{1,0:T(8,128)(2,1)S(1)} %get-tuple-element.49), channel_id=1, source_target_pairs={{0,20},{4,16},{8,28},{12,24},{16,4},{20,0},{24,12},{28,8},{1,21},{... | collective-permute-start | bytes 393224 | tf_op jit(solution)/shard_map/ppermute | solution.py:449
  21.4 0.5 first.6
  21.8 1.6 %collective-permute-start.11 = (bf16[128,512]{1,0:T(8,128)(2,1)S(1)}, bf16[128,512]{1,0:T(8,128)(2,1)S(1)}, u32[]{:S(2)}, u32[]{:S(2)}) collective-permute-start(bf16[128,512]{1,0:T(8,128)(2,1)S(1)} %get-tuple-element.47.refs_3_), channel_id=1, source_target_pairs={{0,1},{1,0},{2,3},{3,2},{4,5},{5,4},{6,7},{7,6},{8,9},{9,8},{10,11... | collective-permute-start | bytes 393224 | tf_op jit(solution)/shard_map/ppermute | solution.py:449
  23.6 2.7 %collective-permute-start.10 = (bf16[128,512]{1,0:T(8,128)(2,1)S(1)}, bf16[128,512]{1,0:T(8,128)(2,1)S(1)}, u32[]{:S(2)}, u32[]{:S(2)}) collective-permute-start(bf16[128,512]{1,0:T(8,128)(2,1)S(1)} %add.10.refs_3_), channel_id=1, source_target_pairs={{0,2},{1,3},{2,0},{3,1},{4,6},{5,7},{6,4},{7,5},{8,10},{9,11},{10,... | collective-permute-start | bytes 393224 | tf_op jit(solution)/shard_map/ppermute | solution.py:449
  26.3 0.5 first.7
  26.7 0.7 %collective-permute-start.9 = (bf16[128,512]{1,0:T(8,128)(2,1)S(1)}, bf16[128,512]{1,0:T(8,128)(2,1)S(1)}, u32[]{:S(2)}, u32[]{:S(2)}) collective-permute-start(bf16[128,512]{1,0:T(8,128)(2,1)S(1)} %get-tuple-element.52.refs_2_), channel_id=1, source_target_pairs={{0,1},{1,0},{2,3},{3,2},{4,5},{5,4},{6,7},{7,6},{8,9},{9,8},{10,11... | collective-permute-start | bytes 393224 | tf_op jit(solution)/shard_map/ppermute | solution.py:449
  27.4 0.8 %collective-permute-done.11.refs_1_ = bf16[128,512]{1,0:T(8,128)(2,1)S(1)} collective-permute-done((bf16[128,512]{1,0:T(8,128)(2,1)S(1)}, bf16[128,512]{1,0:T(8,128)(2,1)S(1)}, u32[]{:S(2)}, u32[]{:S(2)}) %collective-permute-start.11) | collective-permute-done | bytes 131104 | tf_op jit(solution)/shard_map/ppermute | solution.py:449
  28.2 2.1 %collective-permute-start.14 = (bf16[128,512]{1,0:T(8,128)(2,1)S(1)}, bf16[128,512]{1,0:T(8,128)(2,1)S(1)}, u32[]{:S(2)}, u32[]{:S(2)}) collective-permute-start(bf16[128,512]{1,0:T(8,128)(2,1)S(1)} %add.11.refs_3_), channel_id=1, source_target_pairs={{0,2},{1,3},{2,0},{3,1},{4,6},{5,7},{6,4},{7,5},{8,10},{9,11},{10,... | collective-permute-start | bytes 393224 | tf_op jit(solution)/shard_map/ppermute | solution.py:449
  30.3 1.5 %collective-permute-done.10.refs_2_ = bf16[128,512]{1,0:T(8,128)(2,1)S(1)} collective-permute-done((bf16[128,512]{1,0:T(8,128)(2,1)S(1)}, bf16[128,512]{1,0:T(8,128)(2,1)S(1)}, u32[]{:S(2)}, u32[]{:S(2)}) %collective-permute-start.10) | collective-permute-done | bytes 131104 | tf_op jit(solution)/shard_map/ppermute | solution.py:449
  31.8 1.2 %collective-permute-start.13 = (bf16[128,512]{1,0:T(8,128)(2,1)S(1)}, bf16[128,512]{1,0:T(8,128)(2,1)S(1)}, u32[]{:S(2)}, u32[]{:S(2)}) collective-permute-start(bf16[128,512]{1,0:T(8,128)(2,1)S(1)} %add.12.refs_2_.refs_0_), channel_id=1, source_target_pairs={{0,1},{1,0},{2,3},{3,2},{4,5},{5,4},{6,7},{7,6},{8,9},{9,8},{10,11... | collective-permute-start | bytes 393224 | tf_op jit(solution)/shard_map/ppermute | solution.py:449
  33.0 3.0 %collective-permute-done.9.refs_1_ = bf16[128,512]{1,0:T(8,128)(2,1)S(1)} collective-permute-done((bf16[128,512]{1,0:T(8,128)(2,1)S(1)}, bf16[128,512]{1,0:T(8,128)(2,1)S(1)}, u32[]{:S(2)}, u32[]{:S(2)}) %collective-permute-start.9) | collective-permute-done | bytes 131104 | tf_op jit(solution)/shard_map/ppermute | solution.py:449
  36.1 0.9 %collective-permute-start.16 = (bf16[128,512]{1,0:T(8,128)(2,1)S(1)}, bf16[128,512]{1,0:T(8,128)(2,1)S(1)}, u32[]{:S(2)}, u32[]{:S(2)}) collective-permute-start(bf16[128,512]{1,0:T(8,128)(2,1)S(1)} %add.13.refs_1_), channel_id=1, source_target_pairs={{0,2},{1,3},{2,0},{3,1},{4,6},{5,7},{6,4},{7,5},{8,10},{9,11},{10,... | collective-permute-start | bytes 393224 | tf_op jit(solution)/shard_map/ppermute | solution.py:449
  37.0 1.7 %collective-permute-start.12 = (bf16[128,512]{1,0:T(8,128)(2,1)S(1)}, bf16[128,512]{1,0:T(8,128)(2,1)S(1)}, u32[]{:S(2)}, u32[]{:S(2)}) collective-permute-start(bf16[128,512]{1,0:T(8,128)(2,1)S(1)} %release.1.refs_8_.refs_0_), channel_id=1, source_target_pairs={{0,1},{1,0},{2,3},{3,2},{4,5},{5,4},{6,7},{7,6},{8,9},{9,8},{10,11... | collective-permute-start | bytes 393224 | tf_op jit(solution)/shard_map/ppermute | solution.py:449
  38.7 2.5 %down.1 = (f32[1024,1024]{1,0:T(8,128)}, f32[8,128]{1,0:T(8,128)S(1)}) custom-call(bf16[512,1024]{1,0:T(8,128)(2,1)S(1)} %get-tuple-element.40.refs_3_.refs_0_, bf16[64,1024]{1,0:T(8,128)(2,1)S(1)} %get-tuple-element.36.refs_1_.refs_3_, bf16[128,1024]{1,0:T(8,128)(2,1)S(1)} %collective-permute-done.refs_2_.refs_1_, ...), custom_call_target="tpu_custom_call" | custom-call | flops 1 | tf_op jit(solution)/shard_map/down/pallas_call | solution.py:41
  41.2 0.4 collective-permute-start.18
  41.6 0.7 %second.4.refs_6_ = bf16[128,1024]{1,0:T(8,128)(2,1)S(1)} custom-call(bf16[128,512]{1,0:T(8,128)(2,1)S(1)} %add.12.refs_2_.refs_0_, bf16[128,512]{1,0:T(8,128)(2,1)S(1)} %collective-permute-done.13.refs_1_, f32[512,1024]{1,0:T(8,128)S(1)} %get-tuple-element.54.refs_2_, f32[512,1024]{1,0:T(8,128)S(1)} %get-tuple-element.55.refs_3_, ...), custom_call_target="tpu_custom_call" | custom-call | flops 10000000000 | tf_op jit(solution)/shard_map/second/pallas_call | solution.py:41
  42.4 3.8 %collective-permute-start.15 = (bf16[128,1024]{1,0:T(8,128)(2,1)S(1)}, bf16[128,1024]{1,0:T(8,128)(2,1)S(1)}, u32[]{:S(2)}, u32[]{:S(2)}) collective-permute-start(bf16[128,1024]{1,0:T(8,128)(2,1)S(1)} %second.4.refs_6_), channel_id=1, source_target_pairs={{0,24},{4,28},{8,16},{12,20},{16,8},{20,12},{24,0},{28,4},{1,25},{... | collective-permute-start | bytes 786440 | tf_op jit(solution)/shard_map/ppermute | solution.py:449
  46.2 0.7 %second.5 = (bf16[64,1024]{1,0:T(8,128)(2,1)S(1)}, bf16[64,1024]{1,0:T(8,128)(2,1)S(1)}) custom-call(bf16[128,512]{1,0:T(8,128)(2,1)S(1)} %release.1.refs_8_.refs_0_, bf16[128,512]{1,0:T(8,128)(2,1)S(1)} %collective-permute-done.12.refs_1_, f32[512,1024]{1,0:T(8,128)S(1)} %get-tuple-element.54.refs_2_, f32[512,1024]{1,0:T(8,128)S(1)} %get-tuple-element.55.refs_3_, ...), custom_call_target="tpu_custom_call" | custom-call | flops 10000000000 | tf_op jit(solution)/shard_map/second/pallas_call | solution.py:41
  47.0 0.5 collective-permute-start.17
  47.5 0.7 %second.6 = (bf16[64,1024]{1,0:T(8,128)(2,1)S(1)}, bf16[64,1024]{1,0:T(8,128)(2,1)S(1)}) custom-call(bf16[128,512]{1,0:T(8,128)(2,1)S(1)} %add.14.refs_6_.refs_0_, bf16[128,512]{1,0:T(8,128)(2,1)S(1)} %collective-permute-done.18.refs_1_, f32[512,1024]{1,0:T(8,128)S(1)} %get-tuple-element.54.refs_2_, f32[512,1024]{1,0:T(8,128)S(1)} %get-tuple-element.55.refs_3_, ...), custom_call_target="tpu_custom_call" | custom-call | flops 10000000000 | tf_op jit(solution)/shard_map/second/pallas_call | solution.py:41
  48.3 1.0 %collective-permute-start.20 = (bf16[64,1024]{1,0:T(8,128)(2,1)S(1)}, bf16[64,1024]{1,0:T(8,128)(2,1)S(1)}, u32[]{:S(2)}, u32[]{:S(2)}) collective-permute-start(bf16[64,1024]{1,0:T(8,128)(2,1)S(1)} %get-tuple-element.60.refs_6_), channel_id=1, source_target_pairs={{0,8},{4,12},{8,0},{12,4},{16,24},{20,28},{24,16},{28,20},{1,9},{5... | collective-permute-start | bytes 393224 | tf_op jit(solution)/shard_map/ppermute | solution.py:449
  49.3 2.2 %collective-permute-start.21 = (bf16[64,1024]{1,0:T(8,128)(2,1)S(1)}, bf16[64,1024]{1,0:T(8,128)(2,1)S(1)}, u32[]{:S(2)}, u32[]{:S(2)}) collective-permute-start(bf16[64,1024]{1,0:T(8,128)(2,1)S(1)} %get-tuple-element.63), channel_id=1, source_target_pairs={{0,16},{4,20},{8,24},{12,28},{16,0},{20,4},{24,8},{28,12},{1,17},{... | collective-permute-start | bytes 393224 | tf_op jit(solution)/shard_map/ppermute | solution.py:449
  51.5 0.5 collective-permute-done.17.refs_1_
  52.0 0.7 %second.7 = (bf16[64,1024]{1,0:T(8,128)(2,1)S(1)}, bf16[64,1024]{1,0:T(8,128)(2,1)S(1)}) custom-call(bf16[128,512]{1,0:T(8,128)(2,1)S(1)} %add.15.refs_6_.refs_0_, bf16[128,512]{1,0:T(8,128)(2,1)S(1)} %collective-permute-done.17.refs_1_, f32[512,1024]{1,0:T(8,128)S(1)} %get-tuple-element.54.refs_2_, f32[512,1024]{1,0:T(8,128)S(1)} %get-tuple-element.55.refs_3_, ...), custom_call_target="tpu_custom_call" | custom-call | flops 10000000000 | tf_op jit(solution)/shard_map/second/pallas_call | solution.py:41
  52.8 2.3 %collective-permute-start.23 = (bf16[64,1024]{1,0:T(8,128)(2,1)S(1)}, bf16[64,1024]{1,0:T(8,128)(2,1)S(1)}, u32[]{:S(2)}, u32[]{:S(2)}) collective-permute-start(bf16[64,1024]{1,0:T(8,128)(2,1)S(1)} %get-tuple-element.64), channel_id=1, source_target_pairs={{0,20},{4,16},{8,28},{12,24},{16,4},{20,0},{24,12},{28,8},{1,21},{... | collective-permute-start | bytes 393224 | tf_op jit(solution)/shard_map/ppermute | solution.py:449
  55.2 0.3 gather.2.refs_4_.refs_5_
  55.5 1.2 %collective-permute-done.19.refs_2_ = bf16[128,1024]{1,0:T(8,128)(2,1)S(1)} collective-permute-done((bf16[128,1024]{1,0:T(8,128)(2,1)S(1)}, bf16[128,1024]{1,0:T(8,128)(2,1)S(1)}, u32[]{:S(2)}, u32[]{:S(2)}) %collective-permute-start.19) | collective-permute-done | bytes 262176 | tf_op jit(solution)/shard_map/ppermute | solution.py:449
  56.7 0.3 gather.3.refs_1_.refs_4_
  57.2 1.5 %collective-permute-done.23.refs_3_ = bf16[64,1024]{1,0:T(8,128)(2,1)S(1)} collective-permute-done((bf16[64,1024]{1,0:T(8,128)(2,1)S(1)}, bf16[64,1024]{1,0:T(8,128)(2,1)S(1)}, u32[]{:S(2)}, u32[]{:S(2)}) %collective-permute-start.23) | collective-permute-done | bytes 131104 | tf_op jit(solution)/shard_map/ppermute | solution.py:449
  58.8 1.0 %finish.1 = bf16[256,1024]{1,0:T(8,128)(2,1)} custom-call(bf16[256,128]{1,0:T(8,128)(2,1)S(1)} %get-tuple-element.41.refs_0_, bf16[256,1024]{1,0:T(8,128)(2,1)S(1)} %gather.3.refs_1_.refs_4_, bf16[64,1024]{1,0:T(8,128)(2,1)S(1)} %collective-permute-done.22.refs_2_, bf16[64,1024]{1,0:T(8,128)(2,1)S(1)} %collective-permute-done.23.refs_3_, ...), custom_call_target="tpu_custom_call" | custom-call | flops 1 | tf_op jit(solution)/shard_map/finish/pallas_call | solution.py:41
  (40 shorter events, 0.7 us)
Async XLA Ops:
  0.6 1.1 %copy-start.4 = (bf16[256,1024]{1,0:T(8,128)(2,1)S(1)}, bf16[256,1024]{1,0:T(8,128)(2,1)}, u32[]{:S(2)}) copy-start(bf16[256,1024]{1,0:T(8,128)(2,1)} %refs_2_.1) | copy-start | bytes 1572868
  0.6 1.1 %copy-start.5 = (bf16[256,8]{0,1:T(8,128)(2,1)S(1)}, bf16[256,8]{0,1:T(8,128)(2,1)}, u32[]{:S(2)}) copy-start(bf16[256,8]{0,1:T(8,128)(2,1)} %param.8) | copy-start | bytes 12292
  1.7 2.2 %copy-start = (bf16[1,1024,1024]{2,1,0:T(8,128)(2,1)S(1)}, bf16[1,1024,1024]{2,1,0:T(8,128)(2,1)}, u32[]{:S(2)}) copy-start(bf16[1,1024,1024]{2,1,0:T(8,128)(2,1)} %param.13) | copy-start | bytes 6291460
  2.2 1.7 %collective-permute-start = (bf16[128,1024]{1,0:T(8,128)(2,1)S(1)}, bf16[128,1024]{1,0:T(8,128)(2,1)S(1)}, u32[]{:S(2)}, u32[]{:S(2)}) collective-permute-start(bf16[128,1024]{1,0:T(8,128)(2,1)S(1)} %get-tuple-element.35.refs_2_), channel_id=1, source_target_pairs={{0,4},{4,0},{8,12},{12,8},{16,20},{20,16},{24,28},{28,24},{1,5},{5... | collective-permute-start | bytes 786440 | tf_op jit(solution)/shard_map/ppermute | solution.py:449
  4.4 6.8 %collective-permute-start.1 = (bf16[128,512]{1,0:T(8,128)(2,1)S(1)}, bf16[128,512]{1,0:T(8,128)(2,1)S(1)}, u32[]{:S(2)}, u32[]{:S(2)}) collective-permute-start(bf16[128,512]{1,0:T(8,128)(2,1)S(1)} %get-tuple-element.38.refs_2_), channel_id=1, source_target_pairs={{0,1},{1,0},{2,3},{3,2},{4,5},{5,4},{6,7},{7,6},{8,9},{9,8},{10,11... | collective-permute-start | bytes 393224 | tf_op jit(solution)/shard_map/ppermute | solution.py:449
  7.4 6.7 %copy-start.1 = (bf16[512,2048]{1,0:T(8,128)(2,1)S(1)}, bf16[512,2048]{1,0:T(8,128)(2,1)}, u32[]{:S(2)}) copy-start(bf16[512,2048]{1,0:T(8,128)(2,1)} %refs_0_.1) | copy-start | bytes 6291460
  7.4 10.2 %collective-permute-start.5 = (bf16[128,1024]{1,0:T(8,128)(2,1)S(1)}, bf16[128,1024]{1,0:T(8,128)(2,1)S(1)}, u32[]{:S(2)}, u32[]{:S(2)}) collective-permute-start(bf16[128,1024]{1,0:T(8,128)(2,1)S(1)} %pair.2.refs_2_), channel_id=1, source_target_pairs={{0,24},{4,28},{8,16},{12,20},{16,8},{20,12},{24,0},{28,4},{1,25},{... | collective-permute-start | bytes 786440 | tf_op jit(solution)/shard_map/ppermute | solution.py:449
  9.9 9.4 %collective-permute-start.3 = (bf16[64,1024]{1,0:T(8,128)(2,1)S(1)}, bf16[64,1024]{1,0:T(8,128)(2,1)S(1)}, u32[]{:S(2)}, u32[]{:S(2)}) collective-permute-start(bf16[64,1024]{1,0:T(8,128)(2,1)S(1)} %get-tuple-element.43), channel_id=1, source_target_pairs={{0,8},{4,12},{8,0},{12,4},{16,24},{20,28},{24,16},{28,20},{1,9},{5... | collective-permute-start | bytes 393224 | tf_op jit(solution)/shard_map/ppermute | solution.py:449
  10.5 10.9 %collective-permute-start.4 = (bf16[64,1024]{1,0:T(8,128)(2,1)S(1)}, bf16[64,1024]{1,0:T(8,128)(2,1)S(1)}, u32[]{:S(2)}, u32[]{:S(2)}) collective-permute-start(bf16[64,1024]{1,0:T(8,128)(2,1)S(1)} %get-tuple-element.44), channel_id=1, source_target_pairs={{0,16},{4,20},{8,24},{12,28},{16,0},{20,4},{24,8},{28,12},{1,17},{... | collective-permute-start | bytes 393224 | tf_op jit(solution)/shard_map/ppermute | solution.py:449
  11.2 3.9 %copy-start.2 = (bf16[1,1024,1024]{2,1,0:T(8,128)(2,1)S(1)}, bf16[1,1024,1024]{2,1,0:T(8,128)(2,1)}, u32[]{:S(2)}) copy-start(bf16[1,1024,1024]{2,1,0:T(8,128)(2,1)} %param.11) | copy-start | bytes 6291460
  11.2 3.9 %copy-start.3 = (bf16[1,1024,1024]{2,1,0:T(8,128)(2,1)S(1)}, bf16[1,1024,1024]{2,1,0:T(8,128)(2,1)}, u32[]{:S(2)}) copy-start(bf16[1,1024,1024]{2,1,0:T(8,128)(2,1)} %param.12) | copy-start | bytes 6291460
  11.2 12.3 %collective-permute-start.2 = (bf16[128,512]{1,0:T(8,128)(2,1)S(1)}, bf16[128,512]{1,0:T(8,128)(2,1)S(1)}, u32[]{:S(2)}, u32[]{:S(2)}) collective-permute-start(bf16[128,512]{1,0:T(8,128)(2,1)S(1)} %add.8.refs_1_), channel_id=1, source_target_pairs={{0,2},{1,3},{2,0},{3,1},{4,6},{5,7},{6,4},{7,5},{8,10},{9,11},{10,... | collective-permute-start | bytes 393224 | tf_op jit(solution)/shard_map/ppermute | solution.py:449
  18.1 5.5 %collective-permute-start.8 = (bf16[128,512]{1,0:T(8,128)(2,1)S(1)}, bf16[128,512]{1,0:T(8,128)(2,1)S(1)}, u32[]{:S(2)}, u32[]{:S(2)}) collective-permute-start(bf16[128,512]{1,0:T(8,128)(2,1)S(1)} %get-tuple-element.46.refs_3_), channel_id=1, source_target_pairs={{0,1},{1,0},{2,3},{3,2},{4,5},{5,4},{6,7},{7,6},{8,9},{9,8},{10,11... | collective-permute-start | bytes 393224 | tf_op jit(solution)/shard_map/ppermute | solution.py:449
  18.6 7.7 %collective-permute-start.6 = (bf16[64,1024]{1,0:T(8,128)(2,1)S(1)}, bf16[64,1024]{1,0:T(8,128)(2,1)S(1)}, u32[]{:S(2)}, u32[]{:S(2)}) collective-permute-start(bf16[64,1024]{1,0:T(8,128)(2,1)S(1)} %get-tuple-element.48), channel_id=1, source_target_pairs={{0,12},{4,8},{8,4},{12,0},{16,28},{20,24},{24,20},{28,16},{1,13},{... | collective-permute-start | bytes 393224 | tf_op jit(solution)/shard_map/ppermute | solution.py:449
  19.4 6.9 %collective-permute-start.7 = (bf16[64,1024]{1,0:T(8,128)(2,1)S(1)}, bf16[64,1024]{1,0:T(8,128)(2,1)S(1)}, u32[]{:S(2)}, u32[]{:S(2)}) collective-permute-start(bf16[64,1024]{1,0:T(8,128)(2,1)S(1)} %get-tuple-element.49), channel_id=1, source_target_pairs={{0,20},{4,16},{8,28},{12,24},{16,4},{20,0},{24,12},{28,8},{1,21},{... | collective-permute-start | bytes 393224 | tf_op jit(solution)/shard_map/ppermute | solution.py:449
  21.8 6.4 %collective-permute-start.11 = (bf16[128,512]{1,0:T(8,128)(2,1)S(1)}, bf16[128,512]{1,0:T(8,128)(2,1)S(1)}, u32[]{:S(2)}, u32[]{:S(2)}) collective-permute-start(bf16[128,512]{1,0:T(8,128)(2,1)S(1)} %get-tuple-element.47.refs_3_), channel_id=1, source_target_pairs={{0,1},{1,0},{2,3},{3,2},{4,5},{5,4},{6,7},{7,6},{8,9},{9,8},{10,11... | collective-permute-start | bytes 393224 | tf_op jit(solution)/shard_map/ppermute | solution.py:449
  23.6 8.2 %collective-permute-start.10 = (bf16[128,512]{1,0:T(8,128)(2,1)S(1)}, bf16[128,512]{1,0:T(8,128)(2,1)S(1)}, u32[]{:S(2)}, u32[]{:S(2)}) collective-permute-start(bf16[128,512]{1,0:T(8,128)(2,1)S(1)} %add.10.refs_3_), channel_id=1, source_target_pairs={{0,2},{1,3},{2,0},{3,1},{4,6},{5,7},{6,4},{7,5},{8,10},{9,11},{10,... | collective-permute-start | bytes 393224 | tf_op jit(solution)/shard_map/ppermute | solution.py:449
  26.7 9.3 %collective-permute-start.9 = (bf16[128,512]{1,0:T(8,128)(2,1)S(1)}, bf16[128,512]{1,0:T(8,128)(2,1)S(1)}, u32[]{:S(2)}, u32[]{:S(2)}) collective-permute-start(bf16[128,512]{1,0:T(8,128)(2,1)S(1)} %get-tuple-element.52.refs_2_), channel_id=1, source_target_pairs={{0,1},{1,0},{2,3},{3,2},{4,5},{5,4},{6,7},{7,6},{8,9},{9,8},{10,11... | collective-permute-start | bytes 393224 | tf_op jit(solution)/shard_map/ppermute | solution.py:449
  28.2 13.0 %collective-permute-start.14 = (bf16[128,512]{1,0:T(8,128)(2,1)S(1)}, bf16[128,512]{1,0:T(8,128)(2,1)S(1)}, u32[]{:S(2)}, u32[]{:S(2)}) collective-permute-start(bf16[128,512]{1,0:T(8,128)(2,1)S(1)} %add.11.refs_3_), channel_id=1, source_target_pairs={{0,2},{1,3},{2,0},{3,1},{4,6},{5,7},{6,4},{7,5},{8,10},{9,11},{10,... | collective-permute-start | bytes 393224 | tf_op jit(solution)/shard_map/ppermute | solution.py:449
  31.8 9.8 %collective-permute-start.13 = (bf16[128,512]{1,0:T(8,128)(2,1)S(1)}, bf16[128,512]{1,0:T(8,128)(2,1)S(1)}, u32[]{:S(2)}, u32[]{:S(2)}) collective-permute-start(bf16[128,512]{1,0:T(8,128)(2,1)S(1)} %add.12.refs_2_.refs_0_), channel_id=1, source_target_pairs={{0,1},{1,0},{2,3},{3,2},{4,5},{5,4},{6,7},{7,6},{8,9},{9,8},{10,11... | collective-permute-start | bytes 393224 | tf_op jit(solution)/shard_map/ppermute | solution.py:449
  36.1 10.9 %collective-permute-start.16 = (bf16[128,512]{1,0:T(8,128)(2,1)S(1)}, bf16[128,512]{1,0:T(8,128)(2,1)S(1)}, u32[]{:S(2)}, u32[]{:S(2)}) collective-permute-start(bf16[128,512]{1,0:T(8,128)(2,1)S(1)} %add.13.refs_1_), channel_id=1, source_target_pairs={{0,2},{1,3},{2,0},{3,1},{4,6},{5,7},{6,4},{7,5},{8,10},{9,11},{10,... | collective-permute-start | bytes 393224 | tf_op jit(solution)/shard_map/ppermute | solution.py:449
  37.0 9.2 %collective-permute-start.12 = (bf16[128,512]{1,0:T(8,128)(2,1)S(1)}, bf16[128,512]{1,0:T(8,128)(2,1)S(1)}, u32[]{:S(2)}, u32[]{:S(2)}) collective-permute-start(bf16[128,512]{1,0:T(8,128)(2,1)S(1)} %release.1.refs_8_.refs_0_), channel_id=1, source_target_pairs={{0,1},{1,0},{2,3},{3,2},{4,5},{5,4},{6,7},{7,6},{8,9},{9,8},{10,11... | collective-permute-start | bytes 393224 | tf_op jit(solution)/shard_map/ppermute | solution.py:449
  41.2 6.3 %collective-permute-start.18 = (bf16[128,512]{1,0:T(8,128)(2,1)S(1)}, bf16[128,512]{1,0:T(8,128)(2,1)S(1)}, u32[]{:S(2)}, u32[]{:S(2)}) collective-permute-start(bf16[128,512]{1,0:T(8,128)(2,1)S(1)} %add.14.refs_6_.refs_0_), channel_id=1, source_target_pairs={{0,1},{1,0},{2,3},{3,2},{4,5},{5,4},{6,7},{7,6},{8,9},{9,8},{10,11... | collective-permute-start | bytes 393224 | tf_op jit(solution)/shard_map/ppermute | solution.py:449
  42.4 12.7 %collective-permute-start.15 = (bf16[128,1024]{1,0:T(8,128)(2,1)S(1)}, bf16[128,1024]{1,0:T(8,128)(2,1)S(1)}, u32[]{:S(2)}, u32[]{:S(2)}) collective-permute-start(bf16[128,1024]{1,0:T(8,128)(2,1)S(1)} %second.4.refs_6_), channel_id=1, source_target_pairs={{0,24},{4,28},{8,16},{12,20},{16,8},{20,12},{24,0},{28,4},{1,25},{... | collective-permute-start | bytes 786440 | tf_op jit(solution)/shard_map/ppermute | solution.py:449
  47.0 5.0 %collective-permute-start.17 = (bf16[128,512]{1,0:T(8,128)(2,1)S(1)}, bf16[128,512]{1,0:T(8,128)(2,1)S(1)}, u32[]{:S(2)}, u32[]{:S(2)}) collective-permute-start(bf16[128,512]{1,0:T(8,128)(2,1)S(1)} %add.15.refs_6_.refs_0_), channel_id=1, source_target_pairs={{0,1},{1,0},{2,3},{3,2},{4,5},{5,4},{6,7},{7,6},{8,9},{9,8},{10,11... | collective-permute-start | bytes 393224 | tf_op jit(solution)/shard_map/ppermute | solution.py:449
  48.3 7.0 %collective-permute-start.20 = (bf16[64,1024]{1,0:T(8,128)(2,1)S(1)}, bf16[64,1024]{1,0:T(8,128)(2,1)S(1)}, u32[]{:S(2)}, u32[]{:S(2)}) collective-permute-start(bf16[64,1024]{1,0:T(8,128)(2,1)S(1)} %get-tuple-element.60.refs_6_), channel_id=1, source_target_pairs={{0,8},{4,12},{8,0},{12,4},{16,24},{20,28},{24,16},{28,20},{1,9},{5... | collective-permute-start | bytes 393224 | tf_op jit(solution)/shard_map/ppermute | solution.py:449
  49.3 5.9 %collective-permute-start.21 = (bf16[64,1024]{1,0:T(8,128)(2,1)S(1)}, bf16[64,1024]{1,0:T(8,128)(2,1)S(1)}, u32[]{:S(2)}, u32[]{:S(2)}) collective-permute-start(bf16[64,1024]{1,0:T(8,128)(2,1)S(1)} %get-tuple-element.63), channel_id=1, source_target_pairs={{0,16},{4,20},{8,24},{12,28},{16,0},{20,4},{24,8},{28,12},{1,17},{... | collective-permute-start | bytes 393224 | tf_op jit(solution)/shard_map/ppermute | solution.py:449
  52.8 4.5 %collective-permute-start.22 = (bf16[64,1024]{1,0:T(8,128)(2,1)S(1)}, bf16[64,1024]{1,0:T(8,128)(2,1)S(1)}, u32[]{:S(2)}, u32[]{:S(2)}) collective-permute-start(bf16[64,1024]{1,0:T(8,128)(2,1)S(1)} %get-tuple-element.61.refs_2_), channel_id=1, source_target_pairs={{0,12},{4,8},{8,4},{12,0},{16,28},{20,24},{24,20},{28,16},{1,13},{... | collective-permute-start | bytes 393224 | tf_op jit(solution)/shard_map/ppermute | solution.py:449
  52.8 5.9 %collective-permute-start.23 = (bf16[64,1024]{1,0:T(8,128)(2,1)S(1)}, bf16[64,1024]{1,0:T(8,128)(2,1)S(1)}, u32[]{:S(2)}, u32[]{:S(2)}) collective-permute-start(bf16[64,1024]{1,0:T(8,128)(2,1)S(1)} %get-tuple-element.64), channel_id=1, source_target_pairs={{0,20},{4,16},{8,28},{12,24},{16,4},{20,0},{24,12},{28,8},{1,21},{... | collective-permute-start | bytes 393224 | tf_op jit(solution)/shard_map/ppermute | solution.py:449
  55.1 1.6 %collective-permute-start.19 = (bf16[128,1024]{1,0:T(8,128)(2,1)S(1)}, bf16[128,1024]{1,0:T(8,128)(2,1)S(1)}, u32[]{:S(2)}, u32[]{:S(2)}) collective-permute-start(bf16[128,1024]{1,0:T(8,128)(2,1)S(1)} %pair.3.refs_3_), channel_id=1, source_target_pairs={{0,4},{4,0},{8,12},{12,8},{16,20},{20,16},{24,28},{28,24},{1,5},{5... | collective-permute-start | bytes 786440 | tf_op jit(solution)/shard_map/ppermute | solution.py:449

commit v7 on v6

--- a/solution.py
+++ b/solution.py
@@ -12,9 +12,9 @@
 PARTS = (CHUNKS[2], CHUNKS[0] + CHUNKS[1], CHUNKS[3])
 ORDER = (
     ("first", 0), ("diagonal", 0), ("add", 0), ("prep", 0), ("turn", 0), ("first", 1),
-    ("first", 2), ("add", 0), ("add", 1), ("first", 3), ("add", 2), ("add", 1), ("add", 3),
-    ("release", 0), ("down", 0), ("add", 2), ("second", 1), ("second", 0), ("add", 3),
-    ("second", 2), ("second", 3), ("cross", 0), ("gather", 0), ("gather", 1),
+    ("first", 2), ("add", 0), ("add", 1), ("first", 3), ("add", 2), ("release", 0), ("add", 1),
+    ("add", 3), ("down", 0), ("add", 2), ("second", 1), ("add", 3), ("second", 2), ("second", 0),
+    ("second", 3), ("cross", 0), ("gather", 0), ("gather", 1),
 )
 HELD = (0,)
 COST = {

time: 60 us -> 59.8 us (level)
  starting transfers between devices: 33.5 us -> 30.2 us
  waiting for transfers between devices: 11.8 us -> 14.9 us
    ppermute x24, starting transfers between devices: 33.5 us -> 30.2 us  [swap(): return lax.ppermute(block, axis, [(i, i ^ k) for i in range(size)])]
    ppermute x24, waiting for transfers between devices: 11.8 us -> 14.9 us  [swap(): return lax.ppermute(block, axis, [(i, i ^ k) for i in range(size)])]
  transfers between devices with their start and end apart: 24 -> 24, of which waited for: 11 -> 10; matrix products, arithmetic and copies ran while one was open for 0% -> 0% of each run, Pallas kernels for 18% -> 18%
where the time goes in v7:
time: 59.8 us; the launch traced here: 59.6 us
  starting transfers between devices  30.2 us (51%)
  waiting for transfers between devices  14.9 us (25%)
  Pallas kernels  13.5 us (23%)
  between operations  0.92 us (2%)
    ppermute x24, starting transfers between devices, swap(): return lax.ppermute(block, axis, [(i, i ^ k) for i in range(size)])  30.2 us
    ppermute x24, waiting for transfers between devices, swap(): return lax.ppermute(block, axis, [(i, i ^ k) for i in range(size)])  14.9 us
    pallas_call x28, Pallas kernels, call(): pl.pallas_call(run, name=name, out_shape=outs, in_specs=list(specs) + [AN...  13.5 us
  transfers between devices with their start and end apart: 24, of which 10 were waited for; matrix products, arithmetic and copies ran while one was open for 0% of the time, Pallas kernels for 18%

profile of v7, /device:TPU:0, one launch (start us, length us, event | category | flops | bytes accessed | tf_op | source)
XLA Modules:
  0.0 59.6 jit_solution(834248256577950985)
XLA Ops:
  0.6 1.0 %place.1.refs_0_ = bf16[512,256]{1,0:T(8,128)(2,1)S(1)} custom-call(s32[1,256]{1,0:T(1,128)} %bitcast.14), custom_call_target="tpu_custom_call" | custom-call | flops 10000000000 | tf_op jit(solution)/shard_map/place/pallas_call | solution.py:41
  1.7 0.5 pack.1
  2.2 0.5 collective-permute-start
  2.7 0.3 rest.1
  3.1 0.8 %collective-permute-done.refs_2_.refs_1_ = bf16[128,1024]{1,0:T(8,128)(2,1)S(1)} collective-permute-done((bf16[128,1024]{1,0:T(8,128)(2,1)S(1)}, bf16[128,1024]{1,0:T(8,128)(2,1)S(1)}, u32[]{:S(2)}, u32[]{:S(2)}) %collective-permute-start) | collective-permute-done | bytes 262176 | tf_op jit(solution)/shard_map/ppermute | solution.py:449
  3.9 0.5 first.4
  4.4 3.0 %collective-permute-start.1 = (bf16[128,512]{1,0:T(8,128)(2,1)S(1)}, bf16[128,512]{1,0:T(8,128)(2,1)S(1)}, u32[]{:S(2)}, u32[]{:S(2)}) collective-permute-start(bf16[128,512]{1,0:T(8,128)(2,1)S(1)} %get-tuple-element.38.refs_2_), channel_id=1, source_target_pairs={{0,1},{1,0},{2,3},{3,2},{4,5},{5,4},{6,7},{7,6},{8,9},{9,8},{10,11... | collective-permute-start | bytes 393224 | tf_op jit(solution)/shard_map/ppermute | solution.py:449
  7.4 2.5 %collective-permute-start.5 = (bf16[128,1024]{1,0:T(8,128)(2,1)S(1)}, bf16[128,1024]{1,0:T(8,128)(2,1)S(1)}, u32[]{:S(2)}, u32[]{:S(2)}) collective-permute-start(bf16[128,1024]{1,0:T(8,128)(2,1)S(1)} %pair.2.refs_2_), channel_id=1, source_target_pairs={{0,24},{4,28},{8,16},{12,20},{16,8},{20,12},{24,0},{28,4},{1,25},{... | collective-permute-start | bytes 786440 | tf_op jit(solution)/shard_map/ppermute | solution.py:449
  9.9 0.5 collective-permute-start.3
  10.5 0.5 collective-permute-start.4
  11.0 0.2 collective-permute-done.1.refs_1_
  11.2 2.8 %collective-permute-start.2 = (bf16[128,512]{1,0:T(8,128)(2,1)S(1)}, bf16[128,512]{1,0:T(8,128)(2,1)S(1)}, u32[]{:S(2)}, u32[]{:S(2)}) collective-permute-start(bf16[128,512]{1,0:T(8,128)(2,1)S(1)} %add.8.refs_1_), channel_id=1, source_target_pairs={{0,2},{1,3},{2,0},{3,1},{4,6},{5,7},{6,4},{7,5},{8,10},{9,11},{10,... | collective-permute-start | bytes 393224 | tf_op jit(solution)/shard_map/ppermute | solution.py:449
  14.0 1.0 %prep.1 = (f32[512,1024]{1,0:T(8,128)S(1)}, f32[512,1024]{1,0:T(8,128)S(1)}, bf16[512,1024]{1,0:T(8,128)(2,1)S(1)}) custom-call(bf16[512,2048]{1,0:T(8,128)(2,1)S(1)} %copy-done.1, bf16[128,512]{1,0:T(8,128)(2,1)S(1)} %add.8.refs_1_), custom_call_target="tpu_custom_call" | custom-call | flops 1 | tf_op jit(solution)/shard_map/prep/pallas_call | solution.py:41
  15.1 1.3 %turn.1 = (bf16[1024,1024]{1,0:T(8,128)(2,1)S(1)}, bf16[1024,1024]{1,0:T(8,128)(2,1)S(1)}, bf16[256,128]{1,0:T(8,128)(2,1)S(1)}, bf16[256,256]{1,0:T(8,128)(2,1)S(1)}, bf16[256,128]{1,0:T(8,128)(2,1)S(1)}) custom-call(bf16[512,256]{1,0:T(8,128)(2,1)S(1)} %place.1.refs_0_, bf16[1024,1024]{1,0:T(8,128)(2,1)S(1)} %bitcast.10, bf16[1024,1024]{1,0:T(8,128)(2,1)S(1)} %bitcast.11, ...), custom_call_target="tpu_custom_call" | custom-call | flops 1 | tf_op jit(solution)/shard_map/turn/pallas_call | solution.py:41
  16.4 1.2 %collective-permute-done.5.refs_1_.refs_7_ = bf16[128,1024]{1,0:T(8,128)(2,1)S(1)} collective-permute-done((bf16[128,1024]{1,0:T(8,128)(2,1)S(1)}, bf16[128,1024]{1,0:T(8,128)(2,1)S(1)}, u32[]{:S(2)}, u32[]{:S(2)}) %collective-permute-start.5) | collective-permute-done | bytes 262176 | tf_op jit(solution)/shard_map/ppermute | solution.py:449
  17.6 0.5 first.5
  18.1 0.5 collective-permute-start.9
  18.6 0.8 %collective-permute-done.3.refs_1_.refs_3_ = bf16[64,1024]{1,0:T(8,128)(2,1)S(1)} collective-permute-done((bf16[64,1024]{1,0:T(8,128)(2,1)S(1)}, bf16[64,1024]{1,0:T(8,128)(2,1)S(1)}, u32[]{:S(2)}, u32[]{:S(2)}) %collective-permute-start.3) | collective-permute-done | bytes 131104 | tf_op jit(solution)/shard_map/ppermute | solution.py:449
  19.4 2.0 %collective-permute-start.8 = (bf16[64,1024]{1,0:T(8,128)(2,1)S(1)}, bf16[64,1024]{1,0:T(8,128)(2,1)S(1)}, u32[]{:S(2)}, u32[]{:S(2)}) collective-permute-start(bf16[64,1024]{1,0:T(8,128)(2,1)S(1)} %get-tuple-element.50), channel_id=1, source_target_pairs={{0,20},{4,16},{8,28},{12,24},{16,4},{20,0},{24,12},{28,8},{1,21},{... | collective-permute-start | bytes 393224 | tf_op jit(solution)/shard_map/ppermute | solution.py:449
  21.4 0.5 first.6
  21.8 1.6 %collective-permute-start.6 = (bf16[128,512]{1,0:T(8,128)(2,1)S(1)}, bf16[128,512]{1,0:T(8,128)(2,1)S(1)}, u32[]{:S(2)}, u32[]{:S(2)}) collective-permute-start(bf16[128,512]{1,0:T(8,128)(2,1)S(1)} %get-tuple-element.47.refs_3_), channel_id=1, source_target_pairs={{0,1},{1,0},{2,3},{3,2},{4,5},{5,4},{6,7},{7,6},{8,9},{9,8},{10,11... | collective-permute-start | bytes 393224 | tf_op jit(solution)/shard_map/ppermute | solution.py:449
  23.6 2.7 %collective-permute-start.13 = (bf16[128,512]{1,0:T(8,128)(2,1)S(1)}, bf16[128,512]{1,0:T(8,128)(2,1)S(1)}, u32[]{:S(2)}, u32[]{:S(2)}) collective-permute-start(bf16[128,512]{1,0:T(8,128)(2,1)S(1)} %add.10.refs_3_), channel_id=1, source_target_pairs={{0,2},{1,3},{2,0},{3,1},{4,6},{5,7},{6,4},{7,5},{8,10},{9,11},{10,... | collective-permute-start | bytes 393224 | tf_op jit(solution)/shard_map/ppermute | solution.py:449
  26.3 0.5 first.7
  26.7 0.6 %collective-permute-start.12 = (bf16[128,512]{1,0:T(8,128)(2,1)S(1)}, bf16[128,512]{1,0:T(8,128)(2,1)S(1)}, u32[]{:S(2)}, u32[]{:S(2)}) collective-permute-start(bf16[128,512]{1,0:T(8,128)(2,1)S(1)} %get-tuple-element.52.refs_2_), channel_id=1, source_target_pairs={{0,1},{1,0},{2,3},{3,2},{4,5},{5,4},{6,7},{7,6},{8,9},{9,8},{10,11... | collective-permute-start | bytes 393224 | tf_op jit(solution)/shard_map/ppermute | solution.py:449
  27.4 0.8 %collective-permute-done.6.refs_1_ = bf16[128,512]{1,0:T(8,128)(2,1)S(1)} collective-permute-done((bf16[128,512]{1,0:T(8,128)(2,1)S(1)}, bf16[128,512]{1,0:T(8,128)(2,1)S(1)}, u32[]{:S(2)}, u32[]{:S(2)}) %collective-permute-start.6) | collective-permute-done | bytes 131104 | tf_op jit(solution)/shard_map/ppermute | solution.py:449
  28.3 2.1 %collective-permute-start.11 = (bf16[128,512]{1,0:T(8,128)(2,1)S(1)}, bf16[128,512]{1,0:T(8,128)(2,1)S(1)}, u32[]{:S(2)}, u32[]{:S(2)}) collective-permute-start(bf16[128,512]{1,0:T(8,128)(2,1)S(1)} %add.11.refs_1_), channel_id=1, source_target_pairs={{0,2},{1,3},{2,0},{3,1},{4,6},{5,7},{6,4},{7,5},{8,10},{9,11},{10,... | collective-permute-start | bytes 393224 | tf_op jit(solution)/shard_map/ppermute | solution.py:449
  30.3 2.0 %collective-permute-start.10 = (bf16[128,512]{1,0:T(8,128)(2,1)S(1)}, bf16[128,512]{1,0:T(8,128)(2,1)S(1)}, u32[]{:S(2)}, u32[]{:S(2)}) collective-permute-start(bf16[128,512]{1,0:T(8,128)(2,1)S(1)} %release.1.refs_3_.refs_0_), channel_id=1, source_target_pairs={{0,1},{1,0},{2,3},{3,2},{4,5},{5,4},{6,7},{7,6},{8,9},{9,8},{10,11... | collective-permute-start | bytes 393224 | tf_op jit(solution)/shard_map/ppermute | solution.py:449
  32.4 0.5 collective-permute-start.16
  32.9 3.1 %collective-permute-done.12.refs_1_ = bf16[128,512]{1,0:T(8,128)(2,1)S(1)} collective-permute-done((bf16[128,512]{1,0:T(8,128)(2,1)S(1)}, bf16[128,512]{1,0:T(8,128)(2,1)S(1)}, u32[]{:S(2)}, u32[]{:S(2)}) %collective-permute-start.12) | collective-permute-done | bytes 131104 | tf_op jit(solution)/shard_map/ppermute | solution.py:449
  36.0 0.9 %collective-permute-start.15 = (bf16[128,512]{1,0:T(8,128)(2,1)S(1)}, bf16[128,512]{1,0:T(8,128)(2,1)S(1)}, u32[]{:S(2)}, u32[]{:S(2)}) collective-permute-start(bf16[128,512]{1,0:T(8,128)(2,1)S(1)} %add.13.refs_8_), channel_id=1, source_target_pairs={{0,2},{1,3},{2,0},{3,1},{4,6},{5,7},{6,4},{7,5},{8,10},{9,11},{10,... | collective-permute-start | bytes 393224 | tf_op jit(solution)/shard_map/ppermute | solution.py:449
  36.9 2.5 %down.1 = (f32[1024,1024]{1,0:T(8,128)}, f32[8,128]{1,0:T(8,128)S(1)}) custom-call(bf16[512,1024]{1,0:T(8,128)(2,1)S(1)} %get-tuple-element.40.refs_3_.refs_0_, bf16[64,1024]{1,0:T(8,128)(2,1)S(1)} %get-tuple-element.36.refs_1_.refs_3_, bf16[128,1024]{1,0:T(8,128)(2,1)S(1)} %collective-permute-done.refs_2_.refs_1_, ...), custom_call_target="tpu_custom_call" | custom-call | flops 1 | tf_op jit(solution)/shard_map/down/pallas_call | solution.py:41
  39.5 1.8 %collective-permute-start.14 = (bf16[128,512]{1,0:T(8,128)(2,1)S(1)}, bf16[128,512]{1,0:T(8,128)(2,1)S(1)}, u32[]{:S(2)}, u32[]{:S(2)}) collective-permute-start(bf16[128,512]{1,0:T(8,128)(2,1)S(1)} %add.14.refs_6_.refs_0_), channel_id=1, source_target_pairs={{0,1},{1,0},{2,3},{3,2},{4,5},{5,4},{6,7},{7,6},{8,9},{9,8},{10,11... | collective-permute-start | bytes 393224 | tf_op jit(solution)/shard_map/ppermute | solution.py:449
  41.3 3.5 %collective-permute-done.16.refs_1_ = bf16[128,512]{1,0:T(8,128)(2,1)S(1)} collective-permute-done((bf16[128,512]{1,0:T(8,128)(2,1)S(1)}, bf16[128,512]{1,0:T(8,128)(2,1)S(1)}, u32[]{:S(2)}, u32[]{:S(2)}) %collective-permute-start.16) | collective-permute-done | bytes 131104 | tf_op jit(solution)/shard_map/ppermute | solution.py:449
  44.8 0.7 %second.4.refs_3_ = bf16[128,1024]{1,0:T(8,128)(2,1)S(1)} custom-call(bf16[128,512]{1,0:T(8,128)(2,1)S(1)} %add.12.refs_2_.refs_0_, bf16[128,512]{1,0:T(8,128)(2,1)S(1)} %collective-permute-done.16.refs_1_, f32[512,1024]{1,0:T(8,128)S(1)} %get-tuple-element.53.refs_2_, f32[512,1024]{1,0:T(8,128)S(1)} %get-tuple-element.54.refs_3_, ...), custom_call_target="tpu_custom_call" | custom-call | flops 10000000000 | tf_op jit(solution)/shard_map/second/pallas_call | solution.py:41
  45.5 1.7 %collective-permute-start.17 = (bf16[128,1024]{1,0:T(8,128)(2,1)S(1)}, bf16[128,1024]{1,0:T(8,128)(2,1)S(1)}, u32[]{:S(2)}, u32[]{:S(2)}) collective-permute-start(bf16[128,1024]{1,0:T(8,128)(2,1)S(1)} %second.4.refs_3_), channel_id=1, source_target_pairs={{0,24},{4,28},{8,16},{12,20},{16,8},{20,12},{24,0},{28,4},{1,25},{... | collective-permute-start | bytes 786440 | tf_op jit(solution)/shard_map/ppermute | solution.py:449
  47.2 0.1 collective-permute-start.18
  47.3 0.8 %second.5 = (bf16[64,1024]{1,0:T(8,128)(2,1)S(1)}, bf16[64,1024]{1,0:T(8,128)(2,1)S(1)}) custom-call(bf16[128,512]{1,0:T(8,128)(2,1)S(1)} %add.14.refs_6_.refs_0_, bf16[128,512]{1,0:T(8,128)(2,1)S(1)} %collective-permute-done.14.refs_1_, f32[512,1024]{1,0:T(8,128)S(1)} %get-tuple-element.53.refs_2_, f32[512,1024]{1,0:T(8,128)S(1)} %get-tuple-element.54.refs_3_, ...), custom_call_target="tpu_custom_call" | custom-call | flops 10000000000 | tf_op jit(solution)/shard_map/second/pallas_call | solution.py:41
  48.1 0.7 %collective-permute-start.20 = (bf16[64,1024]{1,0:T(8,128)(2,1)S(1)}, bf16[64,1024]{1,0:T(8,128)(2,1)S(1)}, u32[]{:S(2)}, u32[]{:S(2)}) collective-permute-start(bf16[64,1024]{1,0:T(8,128)(2,1)S(1)} %get-tuple-element.58.refs_6_), channel_id=1, source_target_pairs={{0,8},{4,12},{8,0},{12,4},{16,24},{20,28},{24,16},{28,20},{1,9},{5... | collective-permute-start | bytes 393224 | tf_op jit(solution)/shard_map/ppermute | solution.py:449
  48.8 1.5 %collective-permute-start.21 = (bf16[64,1024]{1,0:T(8,128)(2,1)S(1)}, bf16[64,1024]{1,0:T(8,128)(2,1)S(1)}, u32[]{:S(2)}, u32[]{:S(2)}) collective-permute-start(bf16[64,1024]{1,0:T(8,128)(2,1)S(1)} %get-tuple-element.63), channel_id=1, source_target_pairs={{0,16},{4,20},{8,24},{12,28},{16,0},{20,4},{24,8},{28,12},{1,17},{... | collective-permute-start | bytes 393224 | tf_op jit(solution)/shard_map/ppermute | solution.py:449
  50.3 0.7 %second.6 = (bf16[64,1024]{1,0:T(8,128)(2,1)S(1)}, bf16[64,1024]{1,0:T(8,128)(2,1)S(1)}) custom-call(bf16[128,512]{1,0:T(8,128)(2,1)S(1)} %release.1.refs_3_.refs_0_, bf16[128,512]{1,0:T(8,128)(2,1)S(1)} %collective-permute-done.10.refs_1_, f32[512,1024]{1,0:T(8,128)S(1)} %get-tuple-element.53.refs_2_, f32[512,1024]{1,0:T(8,128)S(1)} %get-tuple-element.54.refs_3_, ...), custom_call_target="tpu_custom_call" | custom-call | flops 10000000000 | tf_op jit(solution)/shard_map/second/pallas_call | solution.py:41
  51.0 1.3 %collective-permute-done.18.refs_1_ = bf16[128,512]{1,0:T(8,128)(2,1)S(1)} collective-permute-done((bf16[128,512]{1,0:T(8,128)(2,1)S(1)}, bf16[128,512]{1,0:T(8,128)(2,1)S(1)}, u32[]{:S(2)}, u32[]{:S(2)}) %collective-permute-start.18) | collective-permute-done | bytes 131104 | tf_op jit(solution)/shard_map/ppermute | solution.py:449
  52.3 0.7 %second.7 = (bf16[64,1024]{1,0:T(8,128)(2,1)S(1)}, bf16[64,1024]{1,0:T(8,128)(2,1)S(1)}) custom-call(bf16[128,512]{1,0:T(8,128)(2,1)S(1)} %add.15.refs_6_.refs_0_, bf16[128,512]{1,0:T(8,128)(2,1)S(1)} %collective-permute-done.18.refs_1_, f32[512,1024]{1,0:T(8,128)S(1)} %get-tuple-element.53.refs_2_, f32[512,1024]{1,0:T(8,128)S(1)} %get-tuple-element.54.refs_3_, ...), custom_call_target="tpu_custom_call" | custom-call | flops 10000000000 | tf_op jit(solution)/shard_map/second/pallas_call | solution.py:41
  53.1 1.6 %collective-permute-start.23 = (bf16[64,1024]{1,0:T(8,128)(2,1)S(1)}, bf16[64,1024]{1,0:T(8,128)(2,1)S(1)}, u32[]{:S(2)}, u32[]{:S(2)}) collective-permute-start(bf16[64,1024]{1,0:T(8,128)(2,1)S(1)} %get-tuple-element.64), channel_id=1, source_target_pairs={{0,20},{4,16},{8,28},{12,24},{16,4},{20,0},{24,12},{28,8},{1,21},{... | collective-permute-start | bytes 393224 | tf_op jit(solution)/shard_map/ppermute | solution.py:449
  54.8 1.7 %collective-permute-done.20.refs_1_ = bf16[64,1024]{1,0:T(8,128)(2,1)S(1)} collective-permute-done((bf16[64,1024]{1,0:T(8,128)(2,1)S(1)}, bf16[64,1024]{1,0:T(8,128)(2,1)S(1)}, u32[]{:S(2)}, u32[]{:S(2)}) %collective-permute-start.20) | collective-permute-done | bytes 131104 | tf_op jit(solution)/shard_map/ppermute | solution.py:449
  56.5 0.3 gather.2.refs_4_.refs_5_
  56.8 0.3 gather.3.refs_1_.refs_4_
  57.1 1.5 %collective-permute-done.22.refs_2_ = bf16[64,1024]{1,0:T(8,128)(2,1)S(1)} collective-permute-done((bf16[64,1024]{1,0:T(8,128)(2,1)S(1)}, bf16[64,1024]{1,0:T(8,128)(2,1)S(1)}, u32[]{:S(2)}, u32[]{:S(2)}) %collective-permute-start.22) | collective-permute-done | bytes 131104 | tf_op jit(solution)/shard_map/ppermute | solution.py:449
  58.6 1.0 %finish.1 = bf16[256,1024]{1,0:T(8,128)(2,1)} custom-call(bf16[256,128]{1,0:T(8,128)(2,1)S(1)} %get-tuple-element.41.refs_0_, bf16[256,1024]{1,0:T(8,128)(2,1)S(1)} %gather.3.refs_1_.refs_4_, bf16[64,1024]{1,0:T(8,128)(2,1)S(1)} %collective-permute-done.22.refs_2_, bf16[64,1024]{1,0:T(8,128)(2,1)S(1)} %collective-permute-done.23.refs_3_, ...), custom_call_target="tpu_custom_call" | custom-call | flops 1 | tf_op jit(solution)/shard_map/finish/pallas_call | solution.py:41
  (40 shorter events, 0.6 us)
Async XLA Ops:
  0.6 1.1 %copy-start.4 = (bf16[256,1024]{1,0:T(8,128)(2,1)S(1)}, bf16[256,1024]{1,0:T(8,128)(2,1)}, u32[]{:S(2)}) copy-start(bf16[256,1024]{1,0:T(8,128)(2,1)} %refs_2_.1) | copy-start | bytes 1572868
  0.6 1.1 %copy-start.5 = (bf16[256,8]{0,1:T(8,128)(2,1)S(1)}, bf16[256,8]{0,1:T(8,128)(2,1)}, u32[]{:S(2)}) copy-start(bf16[256,8]{0,1:T(8,128)(2,1)} %param.8) | copy-start | bytes 12292
  1.7 2.2 %copy-start = (bf16[1,1024,1024]{2,1,0:T(8,128)(2,1)S(1)}, bf16[1,1024,1024]{2,1,0:T(8,128)(2,1)}, u32[]{:S(2)}) copy-start(bf16[1,1024,1024]{2,1,0:T(8,128)(2,1)} %param.13) | copy-start | bytes 6291460
  2.2 1.7 %collective-permute-start = (bf16[128,1024]{1,0:T(8,128)(2,1)S(1)}, bf16[128,1024]{1,0:T(8,128)(2,1)S(1)}, u32[]{:S(2)}, u32[]{:S(2)}) collective-permute-start(bf16[128,1024]{1,0:T(8,128)(2,1)S(1)} %get-tuple-element.35.refs_2_), channel_id=1, source_target_pairs={{0,4},{4,0},{8,12},{12,8},{16,20},{20,16},{24,28},{28,24},{1,5},{5... | collective-permute-start | bytes 786440 | tf_op jit(solution)/shard_map/ppermute | solution.py:449
  4.4 6.8 %collective-permute-start.1 = (bf16[128,512]{1,0:T(8,128)(2,1)S(1)}, bf16[128,512]{1,0:T(8,128)(2,1)S(1)}, u32[]{:S(2)}, u32[]{:S(2)}) collective-permute-start(bf16[128,512]{1,0:T(8,128)(2,1)S(1)} %get-tuple-element.38.refs_2_), channel_id=1, source_target_pairs={{0,1},{1,0},{2,3},{3,2},{4,5},{5,4},{6,7},{7,6},{8,9},{9,8},{10,11... | collective-permute-start | bytes 393224 | tf_op jit(solution)/shard_map/ppermute | solution.py:449
  7.4 6.7 %copy-start.1 = (bf16[512,2048]{1,0:T(8,128)(2,1)S(1)}, bf16[512,2048]{1,0:T(8,128)(2,1)}, u32[]{:S(2)}) copy-start(bf16[512,2048]{1,0:T(8,128)(2,1)} %refs_0_.1) | copy-start | bytes 6291460
  7.4 10.2 %collective-permute-start.5 = (bf16[128,1024]{1,0:T(8,128)(2,1)S(1)}, bf16[128,1024]{1,0:T(8,128)(2,1)S(1)}, u32[]{:S(2)}, u32[]{:S(2)}) collective-permute-start(bf16[128,1024]{1,0:T(8,128)(2,1)S(1)} %pair.2.refs_2_), channel_id=1, source_target_pairs={{0,24},{4,28},{8,16},{12,20},{16,8},{20,12},{24,0},{28,4},{1,25},{... | collective-permute-start | bytes 786440 | tf_op jit(solution)/shard_map/ppermute | solution.py:449
  9.9 9.4 %collective-permute-start.3 = (bf16[64,1024]{1,0:T(8,128)(2,1)S(1)}, bf16[64,1024]{1,0:T(8,128)(2,1)S(1)}, u32[]{:S(2)}, u32[]{:S(2)}) collective-permute-start(bf16[64,1024]{1,0:T(8,128)(2,1)S(1)} %get-tuple-element.43), channel_id=1, source_target_pairs={{0,8},{4,12},{8,0},{12,4},{16,24},{20,28},{24,16},{28,20},{1,9},{5... | collective-permute-start | bytes 393224 | tf_op jit(solution)/shard_map/ppermute | solution.py:449
  10.5 10.9 %collective-permute-start.4 = (bf16[64,1024]{1,0:T(8,128)(2,1)S(1)}, bf16[64,1024]{1,0:T(8,128)(2,1)S(1)}, u32[]{:S(2)}, u32[]{:S(2)}) collective-permute-start(bf16[64,1024]{1,0:T(8,128)(2,1)S(1)} %get-tuple-element.44), channel_id=1, source_target_pairs={{0,16},{4,20},{8,24},{12,28},{16,0},{20,4},{24,8},{28,12},{1,17},{... | collective-permute-start | bytes 393224 | tf_op jit(solution)/shard_map/ppermute | solution.py:449
  11.2 3.9 %copy-start.2 = (bf16[1,1024,1024]{2,1,0:T(8,128)(2,1)S(1)}, bf16[1,1024,1024]{2,1,0:T(8,128)(2,1)}, u32[]{:S(2)}) copy-start(bf16[1,1024,1024]{2,1,0:T(8,128)(2,1)} %param.11) | copy-start | bytes 6291460
  11.2 3.9 %copy-start.3 = (bf16[1,1024,1024]{2,1,0:T(8,128)(2,1)S(1)}, bf16[1,1024,1024]{2,1,0:T(8,128)(2,1)}, u32[]{:S(2)}) copy-start(bf16[1,1024,1024]{2,1,0:T(8,128)(2,1)} %param.12) | copy-start | bytes 6291460
  11.2 12.3 %collective-permute-start.2 = (bf16[128,512]{1,0:T(8,128)(2,1)S(1)}, bf16[128,512]{1,0:T(8,128)(2,1)S(1)}, u32[]{:S(2)}, u32[]{:S(2)}) collective-permute-start(bf16[128,512]{1,0:T(8,128)(2,1)S(1)} %add.8.refs_1_), channel_id=1, source_target_pairs={{0,2},{1,3},{2,0},{3,1},{4,6},{5,7},{6,4},{7,5},{8,10},{9,11},{10,... | collective-permute-start | bytes 393224 | tf_op jit(solution)/shard_map/ppermute | solution.py:449
  18.1 5.5 %collective-permute-start.9 = (bf16[128,512]{1,0:T(8,128)(2,1)S(1)}, bf16[128,512]{1,0:T(8,128)(2,1)S(1)}, u32[]{:S(2)}, u32[]{:S(2)}) collective-permute-start(bf16[128,512]{1,0:T(8,128)(2,1)S(1)} %get-tuple-element.46.refs_3_), channel_id=1, source_target_pairs={{0,1},{1,0},{2,3},{3,2},{4,5},{5,4},{6,7},{7,6},{8,9},{9,8},{10,11... | collective-permute-start | bytes 393224 | tf_op jit(solution)/shard_map/ppermute | solution.py:449
  18.6 7.7 %collective-permute-start.7 = (bf16[64,1024]{1,0:T(8,128)(2,1)S(1)}, bf16[64,1024]{1,0:T(8,128)(2,1)S(1)}, u32[]{:S(2)}, u32[]{:S(2)}) collective-permute-start(bf16[64,1024]{1,0:T(8,128)(2,1)S(1)} %get-tuple-element.49), channel_id=1, source_target_pairs={{0,12},{4,8},{8,4},{12,0},{16,28},{20,24},{24,20},{28,16},{1,13},{... | collective-permute-start | bytes 393224 | tf_op jit(solution)/shard_map/ppermute | solution.py:449
  19.4 6.9 %collective-permute-start.8 = (bf16[64,1024]{1,0:T(8,128)(2,1)S(1)}, bf16[64,1024]{1,0:T(8,128)(2,1)S(1)}, u32[]{:S(2)}, u32[]{:S(2)}) collective-permute-start(bf16[64,1024]{1,0:T(8,128)(2,1)S(1)} %get-tuple-element.50), channel_id=1, source_target_pairs={{0,20},{4,16},{8,28},{12,24},{16,4},{20,0},{24,12},{28,8},{1,21},{... | collective-permute-start | bytes 393224 | tf_op jit(solution)/shard_map/ppermute | solution.py:449
  21.8 6.4 %collective-permute-start.6 = (bf16[128,512]{1,0:T(8,128)(2,1)S(1)}, bf16[128,512]{1,0:T(8,128)(2,1)S(1)}, u32[]{:S(2)}, u32[]{:S(2)}) collective-permute-start(bf16[128,512]{1,0:T(8,128)(2,1)S(1)} %get-tuple-element.47.refs_3_), channel_id=1, source_target_pairs={{0,1},{1,0},{2,3},{3,2},{4,5},{5,4},{6,7},{7,6},{8,9},{9,8},{10,11... | collective-permute-start | bytes 393224 | tf_op jit(solution)/shard_map/ppermute | solution.py:449
  23.6 8.8 %collective-permute-start.13 = (bf16[128,512]{1,0:T(8,128)(2,1)S(1)}, bf16[128,512]{1,0:T(8,128)(2,1)S(1)}, u32[]{:S(2)}, u32[]{:S(2)}) collective-permute-start(bf16[128,512]{1,0:T(8,128)(2,1)S(1)} %add.10.refs_3_), channel_id=1, source_target_pairs={{0,2},{1,3},{2,0},{3,1},{4,6},{5,7},{6,4},{7,5},{8,10},{9,11},{10,... | collective-permute-start | bytes 393224 | tf_op jit(solution)/shard_map/ppermute | solution.py:449
  26.7 9.3 %collective-permute-start.12 = (bf16[128,512]{1,0:T(8,128)(2,1)S(1)}, bf16[128,512]{1,0:T(8,128)(2,1)S(1)}, u32[]{:S(2)}, u32[]{:S(2)}) collective-permute-start(bf16[128,512]{1,0:T(8,128)(2,1)S(1)} %get-tuple-element.52.refs_2_), channel_id=1, source_target_pairs={{0,1},{1,0},{2,3},{3,2},{4,5},{5,4},{6,7},{7,6},{8,9},{9,8},{10,11... | collective-permute-start | bytes 393224 | tf_op jit(solution)/shard_map/ppermute | solution.py:449
  28.3 11.2 %collective-permute-start.11 = (bf16[128,512]{1,0:T(8,128)(2,1)S(1)}, bf16[128,512]{1,0:T(8,128)(2,1)S(1)}, u32[]{:S(2)}, u32[]{:S(2)}) collective-permute-start(bf16[128,512]{1,0:T(8,128)(2,1)S(1)} %add.11.refs_1_), channel_id=1, source_target_pairs={{0,2},{1,3},{2,0},{3,1},{4,6},{5,7},{6,4},{7,5},{8,10},{9,11},{10,... | collective-permute-start | bytes 393224 | tf_op jit(solution)/shard_map/ppermute | solution.py:449
  30.3 19.9 %collective-permute-start.10 = (bf16[128,512]{1,0:T(8,128)(2,1)S(1)}, bf16[128,512]{1,0:T(8,128)(2,1)S(1)}, u32[]{:S(2)}, u32[]{:S(2)}) collective-permute-start(bf16[128,512]{1,0:T(8,128)(2,1)S(1)} %release.1.refs_3_.refs_0_), channel_id=1, source_target_pairs={{0,1},{1,0},{2,3},{3,2},{4,5},{5,4},{6,7},{7,6},{8,9},{9,8},{10,11... | collective-permute-start | bytes 393224 | tf_op jit(solution)/shard_map/ppermute | solution.py:449
  32.4 12.4 %collective-permute-start.16 = (bf16[128,512]{1,0:T(8,128)(2,1)S(1)}, bf16[128,512]{1,0:T(8,128)(2,1)S(1)}, u32[]{:S(2)}, u32[]{:S(2)}) collective-permute-start(bf16[128,512]{1,0:T(8,128)(2,1)S(1)} %add.12.refs_2_.refs_0_), channel_id=1, source_target_pairs={{0,1},{1,0},{2,3},{3,2},{4,5},{5,4},{6,7},{7,6},{8,9},{9,8},{10,11... | collective-permute-start | bytes 393224 | tf_op jit(solution)/shard_map/ppermute | solution.py:449
  36.0 11.1 %collective-permute-start.15 = (bf16[128,512]{1,0:T(8,128)(2,1)S(1)}, bf16[128,512]{1,0:T(8,128)(2,1)S(1)}, u32[]{:S(2)}, u32[]{:S(2)}) collective-permute-start(bf16[128,512]{1,0:T(8,128)(2,1)S(1)} %add.13.refs_8_), channel_id=1, source_target_pairs={{0,2},{1,3},{2,0},{3,1},{4,6},{5,7},{6,4},{7,5},{8,10},{9,11},{10,... | collective-permute-start | bytes 393224 | tf_op jit(solution)/shard_map/ppermute | solution.py:449
  39.5 7.8 %collective-permute-start.14 = (bf16[128,512]{1,0:T(8,128)(2,1)S(1)}, bf16[128,512]{1,0:T(8,128)(2,1)S(1)}, u32[]{:S(2)}, u32[]{:S(2)}) collective-permute-start(bf16[128,512]{1,0:T(8,128)(2,1)S(1)} %add.14.refs_6_.refs_0_), channel_id=1, source_target_pairs={{0,1},{1,0},{2,3},{3,2},{4,5},{5,4},{6,7},{7,6},{8,9},{9,8},{10,11... | collective-permute-start | bytes 393224 | tf_op jit(solution)/shard_map/ppermute | solution.py:449
  45.5 9.2 %collective-permute-start.17 = (bf16[128,1024]{1,0:T(8,128)(2,1)S(1)}, bf16[128,1024]{1,0:T(8,128)(2,1)S(1)}, u32[]{:S(2)}, u32[]{:S(2)}) collective-permute-start(bf16[128,1024]{1,0:T(8,128)(2,1)S(1)} %second.4.refs_3_), channel_id=1, source_target_pairs={{0,24},{4,28},{8,16},{12,20},{16,8},{20,12},{24,0},{28,4},{1,25},{... | collective-permute-start | bytes 786440 | tf_op jit(solution)/shard_map/ppermute | solution.py:449
  47.2 5.0 %collective-permute-start.18 = (bf16[128,512]{1,0:T(8,128)(2,1)S(1)}, bf16[128,512]{1,0:T(8,128)(2,1)S(1)}, u32[]{:S(2)}, u32[]{:S(2)}) collective-permute-start(bf16[128,512]{1,0:T(8,128)(2,1)S(1)} %add.15.refs_6_.refs_0_), channel_id=1, source_target_pairs={{0,1},{1,0},{2,3},{3,2},{4,5},{5,4},{6,7},{7,6},{8,9},{9,8},{10,11... | collective-permute-start | bytes 393224 | tf_op jit(solution)/shard_map/ppermute | solution.py:449
  48.1 8.4 %collective-permute-start.20 = (bf16[64,1024]{1,0:T(8,128)(2,1)S(1)}, bf16[64,1024]{1,0:T(8,128)(2,1)S(1)}, u32[]{:S(2)}, u32[]{:S(2)}) collective-permute-start(bf16[64,1024]{1,0:T(8,128)(2,1)S(1)} %get-tuple-element.58.refs_6_), channel_id=1, source_target_pairs={{0,8},{4,12},{8,0},{12,4},{16,24},{20,28},{24,16},{28,20},{1,9},{5... | collective-permute-start | bytes 393224 | tf_op jit(solution)/shard_map/ppermute | solution.py:449
  48.8 7.7 %collective-permute-start.21 = (bf16[64,1024]{1,0:T(8,128)(2,1)S(1)}, bf16[64,1024]{1,0:T(8,128)(2,1)S(1)}, u32[]{:S(2)}, u32[]{:S(2)}) collective-permute-start(bf16[64,1024]{1,0:T(8,128)(2,1)S(1)} %get-tuple-element.63), channel_id=1, source_target_pairs={{0,16},{4,20},{8,24},{12,28},{16,0},{20,4},{24,8},{28,12},{1,17},{... | collective-permute-start | bytes 393224 | tf_op jit(solution)/shard_map/ppermute | solution.py:449
  53.0 5.6 %collective-permute-start.22 = (bf16[64,1024]{1,0:T(8,128)(2,1)S(1)}, bf16[64,1024]{1,0:T(8,128)(2,1)S(1)}, u32[]{:S(2)}, u32[]{:S(2)}) collective-permute-start(bf16[64,1024]{1,0:T(8,128)(2,1)S(1)} %get-tuple-element.61.refs_2_), channel_id=1, source_target_pairs={{0,12},{4,8},{8,4},{12,0},{16,28},{20,24},{24,20},{28,16},{1,13},{... | collective-permute-start | bytes 393224 | tf_op jit(solution)/shard_map/ppermute | solution.py:449
  53.1 5.5 %collective-permute-start.23 = (bf16[64,1024]{1,0:T(8,128)(2,1)S(1)}, bf16[64,1024]{1,0:T(8,128)(2,1)S(1)}, u32[]{:S(2)}, u32[]{:S(2)}) collective-permute-start(bf16[64,1024]{1,0:T(8,128)(2,1)S(1)} %get-tuple-element.64), channel_id=1, source_target_pairs={{0,20},{4,16},{8,28},{12,24},{16,4},{20,0},{24,12},{28,8},{1,21},{... | collective-permute-start | bytes 393224 | tf_op jit(solution)/shard_map/ppermute | solution.py:449
  54.7 2.1 %collective-permute-start.19 = (bf16[128,1024]{1,0:T(8,128)(2,1)S(1)}, bf16[128,1024]{1,0:T(8,128)(2,1)S(1)}, u32[]{:S(2)}, u32[]{:S(2)}) collective-permute-start(bf16[128,1024]{1,0:T(8,128)(2,1)S(1)} %pair.3.refs_3_), channel_id=1, source_target_pairs={{0,4},{4,0},{8,12},{12,8},{16,20},{20,16},{24,28},{28,24},{1,5},{5... | collective-permute-start | bytes 786440 | tf_op jit(solution)/shard_map/ppermute | solution.py:449
